TPU v7x, 512 devices: a whole 4x8x8 slice. The times are simulated.
512 devices in a mesh: section: 2 (over core), dp: 32 (over x, y), mp: 8 (over z).
Axes of the slice: x: 4, y: 8, z: 8, core: 2. Of those that a mesh axis runs over, the one named last changes fastest.
Arguments:
- rollout_rows: bfloat16 [2, 32, 8, 8192], P('section', 'dp', None, 'mp'), may hold values from -6 to 6
- response_lengths: int32 [2, 32], P('section', 'dp'), may hold values from 1 to 4, 80 in all within a row
- tile_counts: int32 [2, 32], P('section', 'dp'), may hold values from 1 to 2, 48 in all within a row
- prompt_owner: int32 [2, 32], P('section'), may hold values from 0 to 31, each once within a row
- proj_gain: bfloat16 [8192], P('mp'), may hold values from 0.099609375 to 1.8984375
- proj_in: bfloat16 [8192, 8192], P('mp', 'dp'), may hold values from -0.0625 to 0.0625
- proj_out: bfloat16 [8192, 8192], P('dp', 'mp'), may hold values from -0.0625 to 0.0625
- norm_gain: bfloat16 [2, 8192], P('section', 'mp'), may hold values from 0.099609375 to 1.8984375
- gate_w: bfloat16 [2, 8192, 16384], P('section', 'mp', 'dp'), may hold values from -0.0625 to 0.0625
- up_w: bfloat16 [2, 8192, 16384], P('section', 'mp', 'dp'), may hold values from -0.0625 to 0.0625
- down_w: bfloat16 [2, 16384, 8192], P('section', 'dp', 'mp'), may hold values from -0.046875 to 0.046875
Outputs:
- section_hidden: bfloat16 [2, 2, 256, 8192], P('section', None, 'dp', 'mp')
Inputs may be any that keep to these rules, and one draw needn't show every extreme that they name: In each micro-batch every owner slot gets exactly one prompt; prompt k of micro-batch m goes to owner slot prompt_owner[m, k], which is held by dp device prompt_owner[m, k]; each dp device owns exactly one slot.
All inputs are finite; a program needn't handle non-finite values. No bound on the sum of `response_lengths` or of `tile_counts` on one device may be relied on, other than what follows from the above.
Results may differ from a plain program's by a relative error of at most 0.03.
Values may be sent and summed in bfloat16 or wider, within the bound.
No kernel may reach another device: no remote copies, remote signals or barrier semaphores. Data moves between devices by JAX's collectives and lax.ppermute only.
A program may use at most 64 MiB of HBM per device.

v0:
```python
import jax
import jax.numpy as jnp
from jax import lax
from jax.sharding import PartitionSpec as P

D = 8192
VIS = 8192
MAXT = 2
TROWS = 2
LMAX = 4


EPS_LN = 1e-05
EPS_RMS = 1e-06


def from_behind(array, axis, by):
    devices = lax.axis_size(axis)
    return lax.ppermute(array, axis, [(i, (i + by) % devices) for i in range(devices)])


def keep_live(slot_rows, lengths, tile_count):
    image_rows = MAXT * TROWS
    position = jnp.arange(slot_rows.shape[1], dtype=jnp.int32)[None, :]
    keeping = jnp.where(
        position < image_rows,
        position < tile_count[:, None] * TROWS,
        position - image_rows < lengths[:, None],
    )
    return slot_rows * keeping[:, :, None].astype(slot_rows.dtype)


def slab(local_rows, prepare, finish, arrange, out_rows):
    gathered = lax.all_gather(local_rows, "dp", axis=0, tiled=True)
    products, row_stats = prepare(gathered)
    products, row_stats = lax.psum((products, row_stats), "mp")
    hidden = finish(products, row_stats)
    return lax.psum_scatter(
        arrange(hidden, gathered, jnp.int32(0), lax.axis_size("dp") * out_rows).astype(
            jnp.bfloat16
        ),
        "dp",
        scatter_dimension=0,
        tiled=True,
    ).astype(jnp.float32)


def projector_parts(gain, w_in, select):

    def prepare(gathered):
        image = select(gathered)
        values = image.astype(jnp.float32)
        row_stats = jnp.stack([jnp.sum(values, axis=1), jnp.sum(values * values, axis=1)], axis=1)
        scaled = (values * gain.astype(jnp.float32)).astype(jnp.bfloat16)
        mixture = jnp.dot(scaled, w_in, preferred_element_type=jnp.float32)
        column = jnp.dot(gain[None, :], w_in, preferred_element_type=jnp.float32)
        return (jnp.concatenate([mixture, column], axis=0), row_stats)

    def finish(products, row_stats):
        center = row_stats[:, 0] / VIS
        spread = row_stats[:, 1] / VIS - center * center
        before = (products[:-1] - center[:, None] * products[-1:]) * lax.rsqrt(spread + EPS_LN)[
            :, None
        ]
        return jax.nn.gelu(before, approximate=False).astype(jnp.bfloat16)

    return (prepare, finish)


def layer_parts(gain, w_gate, w_up):

    def prepare(gathered):
        values = gathered.astype(jnp.float32)
        row_stats = jnp.sum(values * values, axis=1, keepdims=True)
        normed = (values * gain.astype(jnp.float32)).astype(jnp.bfloat16)
        gate_part = jnp.dot(normed, w_gate, preferred_element_type=jnp.float32)
        up_part = jnp.dot(normed, w_up, preferred_element_type=jnp.float32)
        return (jnp.concatenate([gate_part, up_part], axis=1), row_stats)

    def finish(products, row_stats):
        factor = lax.rsqrt(row_stats / D + EPS_RMS)
        hidden_width = w_gate.shape[1]
        gate_pre = products[:, :hidden_width] * factor
        up_pre = products[:, hidden_width:] * factor
        return (jax.nn.silu(gate_pre) * up_pre).astype(jnp.bfloat16)

    return (prepare, finish)


def plain_arrange(weight):

    def arrange(hidden, gathered, first_row, row_count):
        return jnp.dot(hidden, weight, preferred_element_type=jnp.float32)

    return arrange


def run_layer(sequence, gain, w_gate, w_up, w_down):
    prepare, finish = layer_parts(gain, w_gate, w_up)
    total = slab(sequence, prepare, finish, plain_arrange(w_down), sequence.shape[0])
    return (sequence.astype(jnp.float32) + total).astype(jnp.bfloat16)


def pass_on(block):
    return from_behind(block, "section", 1)


def per_device(
    rollout_rows,
    response_lengths,
    tile_counts,
    prompt_owner,
    proj_gain,
    proj_in,
    proj_out,
    norm_gain,
    gate_w,
    up_w,
    down_w,
):
    image_rows = MAXT * TROWS
    slot_rows = image_rows + LMAX
    prompts = rollout_rows.shape[1]
    width_local = rollout_rows.shape[3]
    owners = prompt_owner[0]
    slots_total = owners.shape[0]
    index_all = jnp.arange(slots_total, dtype=jnp.int32)
    live = keep_live(rollout_rows[0], response_lengths[0], tile_counts[0])
    mine = lax.dynamic_slice_in_dim(owners, lax.axis_index("dp") * prompts, prompts, 0)
    placing = (index_all[:, None] == mine[None, :]).astype(jnp.bfloat16)
    outgoing = jnp.dot(
        placing, live.reshape(prompts, -1), preferred_element_type=jnp.float32
    ).astype(jnp.bfloat16)
    incoming = lax.all_to_all(outgoing, "dp", split_axis=0, concat_axis=0, tiled=True)
    owned = jnp.sum(incoming.reshape(-1, prompts, slot_rows * width_local), axis=0).reshape(
        prompts, slot_rows, width_local
    )
    image = owned[:, :image_rows].reshape(prompts * image_rows, width_local)

    def select_plain(gathered):
        return gathered

    prepare, finish = projector_parts(proj_gain, proj_in, select_plain)
    projected = slab(image, prepare, finish, plain_arrange(proj_out), prompts * image_rows)
    projected = projected.astype(jnp.bfloat16).reshape(prompts, image_rows, width_local)
    sequence = jnp.concatenate([projected, owned[:, image_rows:]], axis=1).reshape(
        prompts * slot_rows, width_local
    )
    first_section = lax.axis_index("section") == 0
    other = pass_on(sequence)
    tick_one = run_layer(
        jnp.where(first_section, sequence, other), norm_gain[0], gate_w[0], up_w[0], down_w[0]
    )
    came_one = pass_on(tick_one)
    tick_two = run_layer(
        jnp.where(first_section, other, came_one), norm_gain[0], gate_w[0], up_w[0], down_w[0]
    )
    came_two = pass_on(tick_two)
    tick_three = run_layer(came_two, norm_gain[0], gate_w[0], up_w[0], down_w[0])
    early = jnp.stack([tick_one, tick_two])
    late = jnp.stack([tick_two, tick_three])
    return jnp.where(first_section, early, late)[None]


def solution(mesh):
    placed = (
        P("section", "dp", None, "mp"),
        P("section", "dp"),
        P("section", "dp"),
        P("section", None),
        P("mp"),
        P("mp", "dp"),
        P("dp", "mp"),
        P("section", "mp"),
        P("section", "mp", "dp"),
        P("section", "mp", "dp"),
        P("section", "dp", "mp"),
    )
    return jax.shard_map(
        per_device,
        mesh=mesh,
        in_specs=placed,
        out_specs=P("section", None, "dp", "mp"),
        check_vma=False,
    )
```

profile of v0, /device:TPU:16, one launch (start us, length us, event | category | flops | bytes accessed | tf_op | source)
XLA Modules:
  0.0 1421.5 jit_solution(8030215168522272815)
XLA Ops:
  12.9 10.2 all-to-all-start
  23.4 16.3 %all-to-all-done = bf16[32,2,4096]{2,1,0:T(2,128)(2,1)S(1)} async-done(((bf16[32,2,4096]{2,1,0:T(2,128)(2,1)}), bf16[32,2,4096]{2,1,0:T(2,128)(2,1)S(1)}, u32[]{:S(2)}, u32[]{:S(2)}) %all-to-all-start) | async-done | bytes 524320 | tf_op jit(solution)/shard_map/all_to_all | solution.py:134
  41.3 47.4 %all-gather = bf16[1,128,1024]{2,0,1:T(2,128)(2,1)S(1)} all-gather(bf16[1,4,1024]{2,0,1:T(2,128)(2,1)S(1)} %copy.14), channel_id=2, replica_groups=mesh['section'=2,'dp'=32,'mp'=8] {'dp'}, dimensions={1}, use_global_device_ids=true | all-gather | bytes 270336 | tf_op jit(solution)/shard_map/all_gather | solution.py:34
  90.7 23.2 %psum.57 = f32[128,2]{0,1:T(2,128)S(1)} all-reduce(f32[128,2]{0,1:T(2,128)S(1)} %pad_maximum_fusion.4), channel_id=1, replica_groups=mesh['section'=2,'dp'=32,'mp'=8] {'mp'}, use_global_device_ids=true, to_apply=%region_4.5 | all-reduce | flops 256 | bytes 2048 | tf_op jit(solution)/shard_map/psum | solution.py:36
  114.6 72.5 %all-reduce.7.cloned.1.call-done = f32[129,256]{1,0:T(8,128)} async-done(((f32[129,256]{1,0:T(8,128)}), f32[129,256]{1,0:T(8,128)}) %all-reduce.7.cloned.1.call-update) | async-done | bytes 132112 | tf_op jit(solution)/shard_map/psum | solution.py:36
  187.8 2.3 convolution_convert_fusion.3
  192.1 150.7 %all-reduce.15.cloned.1.call-done = bf16[128,1024]{1,0:T(8,128)(2,1)} async-done(((bf16[128,1024]{1,0:T(8,128)(2,1)}), bf16[128,1024]{1,0:T(8,128)(2,1)}) %all-reduce.15.cloned.1.call-update) | async-done | bytes 262160
  343.5 1.9 collective-permute-start
  346.6 47.4 %all_gather.13 = bf16[256,1024]{1,0:T(8,128)(2,1)S(1)} all-gather(bf16[8,1024]{1,0:T(8,128)(2,1)S(1)} %broadcast_select_fusion.1), channel_id=1, replica_groups=mesh['section'=2,'dp'=32,'mp'=8] {'dp'}, dimensions={0}, use_global_device_ids=true | all-gather | bytes 540672 | tf_op jit(solution)/shard_map/all_gather | solution.py:34
  398.3 18.1 %psum.59 = f32[256,1]{0,1:T(1,128)S(1)} all-reduce(f32[256,1]{0,1:T(1,128)S(1)} %bitcast.81), channel_id=1, replica_groups=mesh['section'=2,'dp'=32,'mp'=8] {'mp'}, use_global_device_ids=true, to_apply=%region_8.9 | all-reduce | flops 256 | bytes 2048 | tf_op jit(solution)/shard_map/psum | solution.py:36
  416.4 62.7 %all-reduce.9.cloned.1.call-done = f32[256,1024]{1,0:T(8,128)} async-done(((f32[256,1024]{1,0:T(8,128)}), f32[256,1024]{1,0:T(8,128)}) %all-reduce.9.cloned.1.call-update) | async-done | bytes 1048592 | tf_op jit(solution)/shard_map/psum | solution.py:36
  479.1 2.5 convolution_convert_fusion.2
  481.8 218.6 %reduce-scatter.4.cloned.1.call-done = bf16[8,1024]{1,0:T(8,128)(2,1)} async-done(((bf16[256,1024]{1,0:T(8,128)(2,1)}), bf16[8,1024]{1,0:T(8,128)(2,1)}) %reduce-scatter.4.cloned.1.call-update) | async-done | bytes 16400 | tf_op jit(solution)/shard_map/reduce_scatter | solution.py:38
  701.1 1.9 collective-permute-start.1
  704.1 47.1 %all_gather.14 = bf16[256,1024]{1,0:T(8,128)(2,1)S(1)} all-gather(bf16[8,1024]{1,0:T(8,128)(2,1)S(1)} %broadcast_select_fusion), channel_id=1, replica_groups=mesh['section'=2,'dp'=32,'mp'=8] {'dp'}, dimensions={0}, use_global_device_ids=true | all-gather | bytes 540672 | tf_op jit(solution)/shard_map/all_gather | solution.py:34
  754.9 18.1 %psum.61 = f32[256,1]{0,1:T(1,128)S(1)} all-reduce(f32[256,1]{0,1:T(1,128)S(1)} %bitcast.82), channel_id=1, replica_groups=mesh['section'=2,'dp'=32,'mp'=8] {'mp'}, use_global_device_ids=true, to_apply=%region_12.13 | all-reduce | flops 256 | bytes 2048 | tf_op jit(solution)/shard_map/psum | solution.py:36
  773.0 62.8 %all-reduce.11.cloned.1.call-done = f32[256,1024]{1,0:T(8,128)} async-done(((f32[256,1024]{1,0:T(8,128)}), f32[256,1024]{1,0:T(8,128)}) %all-reduce.11.cloned.1.call-update) | async-done | bytes 1048592 | tf_op jit(solution)/shard_map/psum | solution.py:36
  835.8 2.6 convolution_convert_fusion.1
  838.4 217.9 %reduce-scatter.6.cloned.1.call-done = bf16[8,1024]{1,0:T(8,128)(2,1)} async-done(((bf16[256,1024]{1,0:T(8,128)(2,1)}), bf16[8,1024]{1,0:T(8,128)(2,1)}) %reduce-scatter.6.cloned.1.call-update) | async-done | bytes 16400 | tf_op jit(solution)/shard_map/reduce_scatter | solution.py:38
  1060.1 47.1 %all_gather.15 = bf16[256,1024]{1,0:T(8,128)(2,1)S(1)} all-gather(bf16[8,1024]{1,0:T(8,128)(2,1)S(1)} %collective-permute-done.2), channel_id=1, replica_groups=mesh['section'=2,'dp'=32,'mp'=8] {'dp'}, dimensions={0}, use_global_device_ids=true | all-gather | bytes 540672 | tf_op jit(solution)/shard_map/all_gather | solution.py:34
  1110.8 18.2 %psum.63 = f32[256,1]{0,1:T(1,128)S(1)} all-reduce(f32[256,1]{0,1:T(1,128)S(1)} %bitcast.83), channel_id=1, replica_groups=mesh['section'=2,'dp'=32,'mp'=8] {'mp'}, use_global_device_ids=true, to_apply=%region_16.17 | all-reduce | flops 256 | bytes 2048 | tf_op jit(solution)/shard_map/psum | solution.py:36
  1129.1 62.9 %all-reduce.13.cloned.1.call-done = f32[256,1024]{1,0:T(8,128)} async-done(((f32[256,1024]{1,0:T(8,128)}), f32[256,1024]{1,0:T(8,128)}) %all-reduce.13.cloned.1.call-update) | async-done | bytes 1048592 | tf_op jit(solution)/shard_map/psum | solution.py:36
  1192.0 2.6 convolution_convert_fusion
  1194.5 218.8 %reduce-scatter.8.cloned.1.call-done = bf16[8,1024]{1,0:T(8,128)(2,1)} async-done(((bf16[256,1024]{1,0:T(8,128)(2,1)}), bf16[8,1024]{1,0:T(8,128)(2,1)}) %reduce-scatter.8.cloned.1.call-update) | async-done | bytes 16400 | tf_op jit(solution)/shard_map/reduce_scatter | solution.py:38
  (97 shorter events, 32.0 us)
Async XLA Ops:
  6.5 472.6 %copy-start = (bf16[1,512,1024]{2,1,0:T(8,128)(2,1)S(1)}, bf16[1,512,1024]{2,1,0:T(8,128)(2,1)}, u32[]{:S(2)}) copy-start(bf16[1,512,1024]{2,1,0:T(8,128)(2,1)} %param.21) | copy-start | bytes 3145732
  6.5 3.4 copy-start.8
  12.9 10.2 copy-start.9
  12.9 10.3 copy-start.7
  12.9 26.8 %all-to-all-start = ((bf16[32,2,4096]{2,1,0:T(2,128)(2,1)}), bf16[32,2,4096]{2,1,0:T(2,128)(2,1)S(1)}, u32[]{:S(2)}, u32[]{:S(2)}) async-start(bf16[32,2,4096]{2,1,0:T(2,128)(2,1)} %reshape.169), calls=%async_computation | async-start | bytes 1048576 | tf_op jit(solution)/shard_map/all_to_all | solution.py:134
  23.1 164.0 %all-reduce.7.cloned.1.call-start = ((), (), s32[]{:S(2)}) async-start(), calls=%async_computation.4 | async-start | bytes 278528 | tf_op jit(solution)/shard_map/psum | solution.py:36
  90.4 96.7 %copy-start.11 = (bf16[256,1024]{1,0:T(8,128)(2,1)S(1)}, bf16[256,1024]{1,0:T(8,128)(2,1)}, u32[]{:S(2)}) copy-start(bf16[256,1024]{1,0:T(8,128)(2,1)} %param.17) | copy-start | bytes 1572868
  114.6 228.2 %all-reduce.15.cloned.1.call-start = ((), (), s32[]{:S(2)}) async-start(), calls=%async_computation.11 | async-start | bytes 524288
  187.8 206.2 %copy-start.1 = (bf16[1,1024,512]{2,1,0:T(8,128)(2,1)S(1)}, bf16[1,1024,512]{2,1,0:T(8,128)(2,1)}, u32[]{:S(2)}) copy-start(bf16[1,1024,512]{2,1,0:T(8,128)(2,1)} %param.20) | copy-start | bytes 3145732
  190.1 289.1 %all-reduce.9.cloned.1.call-start = ((), (), s32[]{:S(2)}) async-start(), calls=%async_computation.5 | async-start | bytes 2097152 | tf_op jit(solution)/shard_map/psum | solution.py:36
  343.5 1.9 copy-start.10
  343.5 3.1 collective-permute-start
  394.0 0.8 copy-start.5
  394.0 1.4 copy-start.2
  397.1 303.3 %reduce-scatter.4.cloned.1.call-start = ((), (), s32[]{:S(2)}) async-start(), calls=%async_computation.6 | async-start | bytes 540672 | tf_op jit(solution)/shard_map/reduce_scatter | solution.py:38
  481.7 354.1 %all-reduce.11.cloned.1.call-start = ((), (), s32[]{:S(2)}) async-start(), calls=%async_computation.7 | async-start | bytes 2097152 | tf_op jit(solution)/shard_map/psum | solution.py:36
  701.1 3.1 collective-permute-start.1
  751.2 0.8 copy-start.6
  753.6 302.7 %reduce-scatter.6.cloned.1.call-start = ((), (), s32[]{:S(2)}) async-start(), calls=%async_computation.8 | async-start | bytes 540672 | tf_op jit(solution)/shard_map/reduce_scatter | solution.py:38
  838.4 353.6 %all-reduce.13.cloned.1.call-start = ((), (), s32[]{:S(2)}) async-start(), calls=%async_computation.9 | async-start | bytes 2097152 | tf_op jit(solution)/shard_map/psum | solution.py:36
  1057.1 3.1 collective-permute-start.2
  1107.2 0.8 copy-start.3
  1109.6 1.0 copy-start.4
  1109.6 303.7 %reduce-scatter.8.cloned.1.call-start = ((), (), s32[]{:S(2)}) async-start(), calls=%async_computation.10 | async-start | bytes 540672 | tf_op jit(solution)/shard_map/reduce_scatter | solution.py:38
  (2 other events, 1.3 us)
Sparse Core Ops, SparseCore 0:
  114.7 72.3 all-reduce.6
  191.0 151.7 all-reduce.14
  397.2 81.9 all-reduce.8
  484.0 216.2 reduce-scatter.3
  753.8 81.9 all-reduce.10
  840.0 216.2 reduce-scatter.5
  1109.7 82.1 all-reduce.12
  1197.0 216.2 reduce-scatter.7
where the time goes:
time: 1420 us
  waiting for transfers between devices  1090 us (77%)
  blocking collectives  267 us (19%)
  starting transfers between devices  16.3 us (1%)
  between operations  15.8 us (1%)
    reduce_scatter x3, waiting for transfers between devices, slab(): lax.psum_scatter(arrange(hidden, gathered, jnp.int32(0), lax.axis_size('d...  655 us
    psum x4, waiting for transfers between devices, slab(): products, row_stats = lax.psum((products, row_stats), 'mp')  261 us
    all_gather x4, blocking collectives, slab(): gathered = lax.all_gather(local_rows, 'dp', axis=0, tiled=True)  189 us
    unnamed x9, waiting for transfers between devices  151 us
    psum x4, blocking collectives, slab(): products, row_stats = lax.psum((products, row_stats), 'mp')  77.6 us
  transfers between devices with their start and end apart: 12, of which 12 were waited for; matrix products, arithmetic and copies ran while one was open for 0% of the time, Pallas kernels for 0%

commit v1 on v0

v1 whole, which is shorter than its diff:
```python
import jax
import jax.numpy as jnp
from jax import lax
from jax.sharding import PartitionSpec as P

D = 8192
VIS = 8192
MAXT = 2
TROWS = 2
LMAX = 4
IMG = MAXT * TROWS
SLOT = IMG + LMAX
EPS_LN = 1e-05
EPS_RMS = 1e-06
LANES = 128
BF = jnp.bfloat16
F32 = jnp.float32


def exchange(blocks, axis):
    return lax.all_to_all(blocks, axis, 0, 0, tiled=True)


def spread(block, axis):
    peers = lax.axis_size(axis)
    return exchange(jnp.broadcast_to(block[None], (peers,) + block.shape), axis)


def swap(block):
    return lax.ppermute(block, "section", [(0, 1), (1, 0)])


def terms(values, count):
    parts = []
    for _ in range(count):
        part = lax.reduce_precision(values, 8, 7)
        parts.append(part.astype(BF))
        values = values - part
    return parts


def dot(a, b):
    return jnp.dot(a, b, preferred_element_type=F32)


def keep_live(slot_rows, lengths, tile_count):
    position = jnp.arange(slot_rows.shape[1], dtype=jnp.int32)[None, :]
    keeping = jnp.where(
        position < IMG,
        position < tile_count[:, None] * TROWS,
        position - IMG < lengths[:, None],
    )
    return slot_rows * keeping[:, :, None].astype(slot_rows.dtype)


def projector_partial(image, gain, w_in):
    width = image.shape[1]
    values = image.astype(F32)
    sums = jnp.sum(values, axis=1)
    squares = jnp.sum(values * values, axis=1)
    scaled = (values * gain.astype(F32)).astype(BF)
    column = dot(gain[None, :], w_in)
    centered = dot(scaled, w_in) - (sums / width)[:, None] * column
    rows, hidden = centered.shape
    small = jnp.stack(terms(sums, 3) + terms(squares, 3))
    small = jnp.pad(small, ((0, 0), (0, hidden - rows)))
    extra = jnp.concatenate([small, jnp.concatenate(terms(column, 3))], axis=0)
    extra = jnp.pad(extra, ((0, 16 - extra.shape[0]), (0, 0)))
    return jnp.concatenate([centered.astype(BF), extra], axis=0)


def projector_active(parts, rows, width):
    values = parts.astype(F32)
    extra = values[:, rows:]
    sums = jnp.sum(extra[:, 0:3, :rows], axis=1)
    squares = jnp.sum(extra[:, 3:6, :rows], axis=(0, 1))
    columns = jnp.sum(extra[:, 6:9], axis=1)
    center = jnp.sum(sums, axis=0) / VIS
    variance = squares / VIS - center * center
    offsets = sums / width - center[None, :]
    before = jnp.sum(values[:, :rows], axis=0)
    before = before + jnp.sum(offsets[:, :, None] * columns[:, None, :], axis=0)
    before = before * lax.rsqrt(variance + EPS_LN)[:, None]
    return jax.nn.gelu(before, approximate=False).astype(BF)


def layer_partial(rows, gain, w_gate, w_up):
    values = rows.astype(F32)
    squares = jnp.sum(values * values, axis=1)
    normed = (values * gain.astype(F32)).astype(BF)
    stats = jnp.pad(jnp.stack(terms(squares, 2), axis=1), ((0, 0), (0, LANES - 2)))
    return jnp.concatenate(
        [dot(normed, w_gate).astype(BF), dot(normed, w_up).astype(BF), stats], axis=1
    )


def layer_inner(parts, hidden):
    total = jnp.sum(parts.astype(F32), axis=0)
    squares = jnp.sum(total[:, 2 * hidden :], axis=1)
    factor = lax.rsqrt(squares / D + EPS_RMS)[:, None]
    gate_pre = total[:, :hidden] * factor
    up_pre = total[:, hidden : 2 * hidden] * factor
    return (jax.nn.silu(gate_pre) * up_pre).astype(BF)


def layer_blocks(rows, gain, w_gate, w_up, w_down, ordering):
    mp = lax.axis_size("mp")
    dp = lax.axis_size("dp")
    hidden = w_gate.shape[1]
    sent = layer_partial(rows, gain, w_gate, w_up)
    parts = exchange(sent.reshape(mp, rows.shape[0] // mp, -1), "mp")
    inner = spread(layer_inner(parts, hidden), "mp").reshape(rows.shape[0], hidden)
    if ordering is not None:
        inner = dot(ordering, inner).astype(BF)
    blocks = dot(inner, w_down).astype(BF)
    blocks = exchange(blocks.reshape(dp, -1, blocks.shape[1]), "dp")
    return jnp.sum(blocks.astype(F32), axis=0)


def per_device(
    rollout_rows,
    response_lengths,
    tile_counts,
    prompt_owner,
    proj_gain,
    proj_in,
    proj_out,
    norm_gain,
    gate_w,
    up_w,
    down_w,
):
    dp = lax.axis_size("dp")
    width = rollout_rows.shape[3]
    first = lax.axis_index("section") == 0
    place = lax.axis_index("dp")
    owners = prompt_owner[0]
    own = (norm_gain, gate_w[0], up_w[0], down_w[0])
    other = tuple(swap(array) for array in own)
    layer0 = [jnp.where(first, a, b) for a, b in zip(own, other)]
    layer1 = [jnp.where(first, b, a) for a, b in zip(own, other)]
    layer0[0], layer1[0] = layer0[0][0], layer1[0][0]

    live = keep_live(rollout_rows[0], response_lengths[0], tile_counts[0])[0]
    gathered = spread(live, "dp")
    image = gathered[:, :IMG].reshape(dp * IMG, width)

    sent = projector_partial(image, proj_gain, proj_in)
    parts = spread(sent, "mp")
    active = projector_active(parts, dp * IMG, width)
    blocks = exchange(dot(active, proj_out).astype(BF).reshape(dp, IMG, width), "dp")
    projected = jnp.sum(blocks.astype(F32), axis=0).astype(BF)
    all_projected = spread(projected, "dp")

    own_rows = jnp.concatenate([projected, live[IMG:]], axis=0)
    rows = jnp.concatenate([all_projected, gathered[:, IMG:]], axis=1).reshape(dp * SLOT, width)
    total = layer_blocks(rows, *layer0, None)
    own_next = (own_rows.astype(F32) + total).astype(BF)
    rows_next = spread(own_next, "dp")

    source = jnp.sum(jnp.where(owners == place, jnp.arange(dp, dtype=jnp.int32), 0))
    slot_early = lax.dynamic_index_in_dim(rows_next, source, 0, keepdims=False)
    row_at = jnp.arange(dp * SLOT, dtype=jnp.int32)
    target = (owners[:, None] * SLOT + jnp.arange(SLOT, dtype=jnp.int32)[None, :]).reshape(-1)
    ordering = (row_at[:, None] == target[None, :]).astype(BF)
    total = layer_blocks(rows_next.reshape(dp * SLOT, width), *layer1, ordering)
    slot_late = (slot_early.astype(F32) + total).astype(BF)

    came = swap(jnp.where(first, slot_late, slot_early))
    kept = jnp.where(first, slot_early, slot_late)
    return jnp.where(first, jnp.stack([kept, came]), jnp.stack([came, kept]))[None]


def solution(mesh):
    placed = (
        P("section", "dp", None, "mp"),
        P("section", "dp"),
        P("section", "dp"),
        P("section", None),
        P("mp"),
        P("mp", "dp"),
        P("dp", "mp"),
        P("section", "mp"),
        P("section", "mp", "dp"),
        P("section", "mp", "dp"),
        P("section", "dp", "mp"),
    )
    return jax.shard_map(
        per_device,
        mesh=mesh,
        in_specs=placed,
        out_specs=P("section", None, "dp", "mp"),
        check_vma=False,
    )
```

time: 1420 us -> 249 us (0.18)
  the two profiles are of different devices: /device:TPU:16 before, /device:TPU:9 now
where the time goes in v1:
time: 249 us; the launch traced here: 248 us
  waiting for transfers between devices  82.2 us (33%)
  starting transfers between devices  80.3 us (32%)
  blocking collectives  60.7 us (24%)
  matrix products  9.74 us (4%)
  other arithmetic  5.61 us (2%)
  local copies, waits for them, and re-layouts  5.23 us (2%)
  between operations  3.85 us (2%)
    all_to_all x8, waiting for transfers between devices, exchange(): return lax.all_to_all(blocks, axis, 0, 0, tiled=True)  80.2 us
    all_to_all x3, blocking collectives, exchange(): return lax.all_to_all(blocks, axis, 0, 0, tiled=True)  60.7 us
    all_to_all x8, starting transfers between devices, exchange(): return lax.all_to_all(blocks, axis, 0, 0, tiled=True)  52.6 us
    ppermute x5, starting transfers between devices, swap(): return lax.ppermute(block, 'section', [(0, 1), (1, 0)])  27.6 us
    dot_general x9, matrix products, dot(): return jnp.dot(a, b, preferred_element_type=F32)  9.74 us
  transfers between devices with their start and end apart: 13, of which 10 were waited for; matrix products, arithmetic and copies ran while one was open for 2% of the time, Pallas kernels for 0%

profile of v1, /device:TPU:9, one launch (start us, length us, event | category | flops | bytes accessed | tf_op | source)
XLA Modules:
  0.0 247.5 jit_solution(13876215594699281505)
XLA Ops:
  3.1 9.6 %all-to-all-start = ((bf16[32,8,1024]{2,1,0:T(8,128)(2,1)}), bf16[32,8,1024]{2,1,0:T(8,128)(2,1)S(1)}, u32[]{:S(2)}, u32[]{:S(2)}) async-start(bf16[32,8,1024]{2,1,0:T(8,128)(2,1)} %broadcast_in_dim.15), calls=%async_computation | async-start | bytes 1048576 | tf_op jit(solution)/shard_map/all_to_all | solution.py:21
  12.9 15.7 %all-to-all-done = bf16[32,8,1024]{2,1,0:T(8,128)(2,1)S(1)} async-done(((bf16[32,8,1024]{2,1,0:T(8,128)(2,1)}), bf16[32,8,1024]{2,1,0:T(8,128)(2,1)S(1)}, u32[]{:S(2)}, u32[]{:S(2)}) %all-to-all-start) | async-done | bytes 524320 | tf_op jit(solution)/shard_map/all_to_all | solution.py:21
  30.0 24.5 %all_to_all.55 = bf16[8,144,256]{2,1,0:T(8,128)(2,1)S(1)} all-to-all(bf16[8,144,256]{2,1,0:T(8,128)(2,1)S(1)} %broadcast_in_dim.16), channel_id=1, replica_groups=mesh['section'=2,'dp'=32,'mp'=8] {'mp'}, dimensions={0} | all-to-all | bytes 1179648 | tf_op jit(solution)/shard_map/all_to_all | solution.py:21
  56.5 8.3 %all-to-all-start.2 = ((bf16[32,4,1024]{2,1,0:T(4,128)(2,1)}), bf16[32,4,1024]{2,1,0:T(4,128)(2,1)S(1)}, u32[]{:S(2)}, u32[]{:S(2)}) async-start(bf16[32,4,1024]{2,1,0:T(4,128)(2,1)} %reshape.435), calls=%async_computation.2 | async-start | bytes 524288 | tf_op jit(solution)/shard_map/all_to_all | solution.py:21
  64.8 5.1 %collective-permute-start.1 = (bf16[1024,512]{1,0:T(8,128)(2,1)S(1)}, bf16[1024,512]{1,0:T(8,128)(2,1)}, u32[]{:S(2)}, u32[]{:S(2)}) collective-permute-start(bf16[1024,512]{1,0:T(8,128)(2,1)S(1)} %bitcast.98), channel_id=1, source_target_pairs={{0,256},{256,0},{1,257},{257,1},{2,258},{258,2},{3,259},{259,3},{4... | collective-permute-start | bytes 3145736 | tf_op jit(solution)/shard_map/ppermute | solution.py:30
  69.9 5.0 %all-to-all-done.2 = bf16[32,4,1024]{2,1,0:T(4,128)(2,1)S(1)} async-done(((bf16[32,4,1024]{2,1,0:T(4,128)(2,1)}), bf16[32,4,1024]{2,1,0:T(4,128)(2,1)S(1)}, u32[]{:S(2)}, u32[]{:S(2)}) %all-to-all-start.2) | async-done | bytes 262176 | tf_op jit(solution)/shard_map/all_to_all | solution.py:21
  75.9 4.2 %all-to-all-start.3 = ((bf16[32,4,1024]{2,1,0:T(4,128)(2,1)}), bf16[32,4,1024]{2,1,0:T(4,128)(2,1)S(1)}, u32[]{:S(2)}, u32[]{:S(2)}) async-start(bf16[32,4,1024]{2,1,0:T(4,128)(2,1)} %broadcast_in_dim.17), calls=%async_computation.3 | async-start | bytes 524288 | tf_op jit(solution)/shard_map/all_to_all | solution.py:21
  80.1 6.2 %collective-permute-start.2 = (bf16[1024,512]{1,0:T(8,128)(2,1)S(1)}, bf16[1024,512]{1,0:T(8,128)(2,1)}, u32[]{:S(2)}, u32[]{:S(2)}) collective-permute-start(bf16[1024,512]{1,0:T(8,128)(2,1)S(1)} %bitcast.99), channel_id=1, source_target_pairs={{0,256},{256,0},{1,257},{257,1},{2,258},{258,2},{3,259},{259,3},{4... | collective-permute-start | bytes 3145736 | tf_op jit(solution)/shard_map/ppermute | solution.py:30
  86.3 1.9 collective-permute-start
  95.3 4.4 %all-to-all-start.4 = ((bf16[8,32,1152]{2,1,0:T(8,128)(2,1)}), bf16[8,32,1152]{2,1,0:T(8,128)(2,1)S(1)}, u32[]{:S(2)}, u32[]{:S(2)}) async-start(bf16[8,32,1152]{2,1,0:T(8,128)(2,1)} %bitcast.10), calls=%async_computation.4 | async-start | bytes 1179648 | tf_op jit(solution)/shard_map/all_to_all | solution.py:21
  99.7 3.8 %collective-permute-start.3 = (bf16[512,1024]{1,0:T(8,128)(2,1)}, bf16[512,1024]{1,0:T(8,128)(2,1)}, u32[]{:S(2)}, u32[]{:S(2)}) collective-permute-start(bf16[512,1024]{1,0:T(8,128)(2,1)} %bitcast.100), channel_id=1, source_target_pairs={{0,256},{256,0},{1,257},{257,1},{2,258},{258,2},{3,259},{259,3},{4... | collective-permute-start | bytes 3145736 | tf_op jit(solution)/shard_map/ppermute | solution.py:30
  103.6 13.5 %all-to-all-done.4 = bf16[8,32,1152]{2,1,0:T(8,128)(2,1)S(1)} async-done(((bf16[8,32,1152]{2,1,0:T(8,128)(2,1)}), bf16[8,32,1152]{2,1,0:T(8,128)(2,1)S(1)}, u32[]{:S(2)}, u32[]{:S(2)}) %all-to-all-start.4) | async-done | bytes 589856 | tf_op jit(solution)/shard_map/all_to_all | solution.py:21
  118.1 3.4 %all-to-all-start.5 = ((bf16[8,32,512]{2,1,0:T(8,128)(2,1)}), bf16[8,32,512]{2,1,0:T(8,128)(2,1)S(1)}, u32[]{:S(2)}, u32[]{:S(2)}) async-start(bf16[8,32,512]{2,1,0:T(8,128)(2,1)} %broadcast_in_dim.18), calls=%async_computation.5 | async-start | bytes 524288 | tf_op jit(solution)/shard_map/all_to_all | solution.py:21
  121.5 9.3 %all-to-all-done.5 = bf16[8,32,512]{2,1,0:T(8,128)(2,1)S(1)} async-done(((bf16[8,32,512]{2,1,0:T(8,128)(2,1)}), bf16[8,32,512]{2,1,0:T(8,128)(2,1)S(1)}, u32[]{:S(2)}, u32[]{:S(2)}) %all-to-all-start.5) | async-done | bytes 262176 | tf_op jit(solution)/shard_map/all_to_all | solution.py:21
  130.9 2.8 %fusion = bf16[32,8,1024]{2,1,0:T(8,128)(2,1)} fusion(bf16[256,512]{1,0:T(8,128)(2,1)S(1)} %bitcast.89, bf16[512,1024]{1,0:T(8,128)(2,1)} %collective-permute-done.3, pred[]{:T(512)S(6)} %eq.25, bf16[1,512,1024]{2,1,0:T(8,128)(2,1)} %param.21), kind=kOutput, calls=%fused_computation.6 | convolution fusion | flops 269221888 | bytes 2883585 | tf_op jit(solution)/shard_map/dot_general | solution.py:43
  133.7 11.0 %all-to-all-start.6 = ((bf16[32,8,1024]{2,1,0:T(8,128)(2,1)}), bf16[32,8,1024]{2,1,0:T(8,128)(2,1)S(1)}, u32[]{:S(2)}, u32[]{:S(2)}) async-start(bf16[32,8,1024]{2,1,0:T(8,128)(2,1)} %fusion), calls=%async_computation.6 | async-start | bytes 1048576 | tf_op jit(solution)/shard_map/all_to_all | solution.py:21
  144.8 16.7 %all-to-all-done.6 = bf16[32,8,1024]{2,1,0:T(8,128)(2,1)S(1)} async-done(((bf16[32,8,1024]{2,1,0:T(8,128)(2,1)}), bf16[32,8,1024]{2,1,0:T(8,128)(2,1)S(1)}, u32[]{:S(2)}, u32[]{:S(2)}) %all-to-all-start.6) | async-done | bytes 524320 | tf_op jit(solution)/shard_map/all_to_all | solution.py:21
  161.6 20.9 %all_to_all.56 = bf16[32,8,1024]{2,1,0:T(8,128)(2,1)S(1)} all-to-all(bf16[32,8,1024]{2,1,0:T(8,128)(2,1)S(1)} %broadcast_in_dim.19), channel_id=1, replica_groups=mesh['section'=2,'dp'=32,'mp'=8] {'dp'}, dimensions={0} | all-to-all | bytes 1048576 | tf_op jit(solution)/shard_map/all_to_all | solution.py:21
  184.0 15.3 %all_to_all.57 = bf16[8,32,1152]{2,1,0:T(8,128)(2,1)S(1)} all-to-all(bf16[8,32,1152]{2,1,0:T(8,128)(2,1)S(1)} %bitcast.87), channel_id=1, replica_groups=mesh['section'=2,'dp'=32,'mp'=8] {'mp'}, dimensions={0} | all-to-all | bytes 1179648 | tf_op jit(solution)/shard_map/all_to_all | solution.py:21
  200.3 3.4 %all-to-all-start.9 = ((bf16[8,32,512]{2,1,0:T(8,128)(2,1)}), bf16[8,32,512]{2,1,0:T(8,128)(2,1)S(1)}, u32[]{:S(2)}, u32[]{:S(2)}) async-start(bf16[8,32,512]{2,1,0:T(8,128)(2,1)} %broadcast_in_dim.21), calls=%async_computation.9 | async-start | bytes 524288 | tf_op jit(solution)/shard_map/all_to_all | solution.py:21
  203.9 9.1 %all-to-all-done.9 = bf16[8,32,512]{2,1,0:T(8,128)(2,1)S(1)} async-done(((bf16[8,32,512]{2,1,0:T(8,128)(2,1)}), bf16[8,32,512]{2,1,0:T(8,128)(2,1)S(1)}, u32[]{:S(2)}, u32[]{:S(2)}) %all-to-all-start.9) | async-done | bytes 262176 | tf_op jit(solution)/shard_map/all_to_all | solution.py:21
  214.4 8.3 %all-to-all-start.10 = ((bf16[32,8,1024]{2,1,0:T(8,128)(2,1)}), bf16[32,8,1024]{2,1,0:T(8,128)(2,1)S(1)}, u32[]{:S(2)}, u32[]{:S(2)}) async-start(bf16[32,8,1024]{2,1,0:T(8,128)(2,1)} %fusion.1), calls=%async_computation.10 | async-start | bytes 1048576 | tf_op jit(solution)/shard_map/all_to_all | solution.py:21
  225.3 10.1 %all-to-all-done.10 = bf16[32,8,1024]{2,1,0:T(8,128)(2,1)S(1)} async-done(((bf16[32,8,1024]{2,1,0:T(8,128)(2,1)}), bf16[32,8,1024]{2,1,0:T(8,128)(2,1)S(1)}, u32[]{:S(2)}, u32[]{:S(2)}) %all-to-all-start.10) | async-done | bytes 524320 | tf_op jit(solution)/shard_map/all_to_all | solution.py:21
  235.5 10.6 %collective-permute-start.4 = (bf16[8,1024]{1,0:T(8,128)(2,1)S(1)}, bf16[8,1024]{1,0:T(8,128)(2,1)S(1)}, u32[]{:S(2)}, u32[]{:S(2)}) collective-permute-start(bf16[8,1024]{1,0:T(8,128)(2,1)S(1)} %fusion.82), channel_id=1, source_target_pairs={{0,256},{256,0},{1,257},{257,1},{2,258},{258,2},{3,259},{259,3},{4... | collective-permute-start | bytes 49160 | tf_op jit(solution)/shard_map/ppermute | solution.py:30
  (99 shorter events, 20.5 us)
Async XLA Ops:
  0.0 55.0 %copy-start = (bf16[256,1024]{1,0:T(8,128)(2,1)S(1)}, bf16[256,1024]{1,0:T(8,128)(2,1)}, u32[]{:S(2)}) copy-start(bf16[256,1024]{1,0:T(8,128)(2,1)} %param.17) | copy-start | bytes 1572868
  0.0 12.7 %copy-start.3 = (bf16[1024]{0:T(1024)(128)(2,1)S(1)}, bf16[1024]{0:T(1024)(128)(2,1)}, u32[]{:S(2)}) copy-start(bf16[1024]{0:T(1024)(128)(2,1)} %param.15) | copy-start | bytes 6148
  0.0 12.7 %copy-start.1 = (bf16[1024,256]{1,0:T(8,128)(2,1)S(1)}, bf16[1024,256]{1,0:T(8,128)(2,1)}, u32[]{:S(2)}) copy-start(bf16[1024,256]{1,0:T(8,128)(2,1)} %param.16) | copy-start | bytes 1572868
  3.1 25.6 %all-to-all-start = ((bf16[32,8,1024]{2,1,0:T(8,128)(2,1)}), bf16[32,8,1024]{2,1,0:T(8,128)(2,1)S(1)}, u32[]{:S(2)}, u32[]{:S(2)}) async-start(bf16[32,8,1024]{2,1,0:T(8,128)(2,1)} %broadcast_in_dim.15), calls=%async_computation | async-start | bytes 1048576 | tf_op jit(solution)/shard_map/all_to_all | solution.py:21
  55.1 9.7 %copy-start.5 = (bf16[1,1024,512]{2,1,0:T(8,128)(2,1)S(1)}, bf16[1,1024,512]{2,1,0:T(8,128)(2,1)}, u32[]{:S(2)}) copy-start(bf16[1,1024,512]{2,1,0:T(8,128)(2,1)} %param.19) | copy-start | bytes 3145732
  55.6 24.5 %copy-start.6 = (bf16[1,1024,512]{2,1,0:T(8,128)(2,1)S(1)}, bf16[1,1024,512]{2,1,0:T(8,128)(2,1)}, u32[]{:S(2)}) copy-start(bf16[1,1024,512]{2,1,0:T(8,128)(2,1)} %param.20) | copy-start | bytes 3145732
  55.6 30.7 %copy-start.4 = (bf16[1,1024]{1,0:T(2,128)(2,1)S(1)}, bf16[1,1024]{1,0:T(2,128)(2,1)}, u32[]{:S(2)}) copy-start(bf16[1,1024]{1,0:T(2,128)(2,1)} %param.18) | copy-start | bytes 6148
  56.5 18.5 %all-to-all-start.2 = ((bf16[32,4,1024]{2,1,0:T(4,128)(2,1)}), bf16[32,4,1024]{2,1,0:T(4,128)(2,1)S(1)}, u32[]{:S(2)}, u32[]{:S(2)}) async-start(bf16[32,4,1024]{2,1,0:T(4,128)(2,1)} %reshape.435), calls=%async_computation.2 | async-start | bytes 524288 | tf_op jit(solution)/shard_map/all_to_all | solution.py:21
  64.8 26.1 %collective-permute-start.1 = (bf16[1024,512]{1,0:T(8,128)(2,1)S(1)}, bf16[1024,512]{1,0:T(8,128)(2,1)}, u32[]{:S(2)}, u32[]{:S(2)}) collective-permute-start(bf16[1024,512]{1,0:T(8,128)(2,1)S(1)} %bitcast.98), channel_id=1, source_target_pairs={{0,256},{256,0},{1,257},{257,1},{2,258},{258,2},{3,259},{259,3},{4... | collective-permute-start | bytes 3145736 | tf_op jit(solution)/shard_map/ppermute | solution.py:30
  75.9 14.3 %all-to-all-start.3 = ((bf16[32,4,1024]{2,1,0:T(4,128)(2,1)}), bf16[32,4,1024]{2,1,0:T(4,128)(2,1)S(1)}, u32[]{:S(2)}, u32[]{:S(2)}) async-start(bf16[32,4,1024]{2,1,0:T(4,128)(2,1)} %broadcast_in_dim.17), calls=%async_computation.3 | async-start | bytes 524288 | tf_op jit(solution)/shard_map/all_to_all | solution.py:21
  80.1 12.6 %collective-permute-start.2 = (bf16[1024,512]{1,0:T(8,128)(2,1)S(1)}, bf16[1024,512]{1,0:T(8,128)(2,1)}, u32[]{:S(2)}, u32[]{:S(2)}) collective-permute-start(bf16[1024,512]{1,0:T(8,128)(2,1)S(1)} %bitcast.99), channel_id=1, source_target_pairs={{0,256},{256,0},{1,257},{257,1},{2,258},{258,2},{3,259},{259,3},{4... | collective-permute-start | bytes 3145736 | tf_op jit(solution)/shard_map/ppermute | solution.py:30
  86.3 3.1 %collective-permute-start = (bf16[1,1024]{1,0:T(2,128)(2,1)S(1)}, bf16[1,1024]{1,0:T(2,128)(2,1)S(1)}, u32[]{:S(2)}, u32[]{:S(2)}) collective-permute-start(bf16[1,1024]{1,0:T(2,128)(2,1)S(1)} %copy-done.4), channel_id=1, source_target_pairs={{0,256},{256,0},{1,257},{257,1},{2,258},{258,2},{3,259},{259,3},{4... | collective-permute-start | bytes 6152 | tf_op jit(solution)/shard_map/ppermute | solution.py:30
  95.3 21.7 %all-to-all-start.4 = ((bf16[8,32,1152]{2,1,0:T(8,128)(2,1)}), bf16[8,32,1152]{2,1,0:T(8,128)(2,1)S(1)}, u32[]{:S(2)}, u32[]{:S(2)}) async-start(bf16[8,32,1152]{2,1,0:T(8,128)(2,1)} %bitcast.10), calls=%async_computation.4 | async-start | bytes 1179648 | tf_op jit(solution)/shard_map/all_to_all | solution.py:21
  99.7 21.8 %collective-permute-start.3 = (bf16[512,1024]{1,0:T(8,128)(2,1)}, bf16[512,1024]{1,0:T(8,128)(2,1)}, u32[]{:S(2)}, u32[]{:S(2)}) collective-permute-start(bf16[512,1024]{1,0:T(8,128)(2,1)} %bitcast.100), channel_id=1, source_target_pairs={{0,256},{256,0},{1,257},{257,1},{2,258},{258,2},{3,259},{259,3},{4... | collective-permute-start | bytes 3145736 | tf_op jit(solution)/shard_map/ppermute | solution.py:30
  118.1 12.7 %all-to-all-start.5 = ((bf16[8,32,512]{2,1,0:T(8,128)(2,1)}), bf16[8,32,512]{2,1,0:T(8,128)(2,1)S(1)}, u32[]{:S(2)}, u32[]{:S(2)}) async-start(bf16[8,32,512]{2,1,0:T(8,128)(2,1)} %broadcast_in_dim.18), calls=%async_computation.5 | async-start | bytes 524288 | tf_op jit(solution)/shard_map/all_to_all | solution.py:21
  130.9 13.9 %copy-start.2 = (bf16[1,1,8,1024]{3,2,1,0:T(8,128)(2,1)S(1)}, bf16[1,1,8,1024]{3,2,1,0:T(8,128)(2,1)}, u32[]{:S(2)}) copy-start(bf16[1,1,8,1024]{3,2,1,0:T(8,128)(2,1)} %param.11) | copy-start | bytes 49156
  133.7 27.8 %all-to-all-start.6 = ((bf16[32,8,1024]{2,1,0:T(8,128)(2,1)}), bf16[32,8,1024]{2,1,0:T(8,128)(2,1)S(1)}, u32[]{:S(2)}, u32[]{:S(2)}) async-start(bf16[32,8,1024]{2,1,0:T(8,128)(2,1)} %fusion), calls=%async_computation.6 | async-start | bytes 1048576 | tf_op jit(solution)/shard_map/all_to_all | solution.py:21
  184.0 19.8 %copy-start.8 = (s32[1,32]{1,0:T(1,128)S(1)}, s32[1,32]{1,0:T(1,128)}, u32[]{:S(2)}) copy-start(s32[1,32]{1,0:T(1,128)} %param.14) | copy-start | bytes 388
  199.3 13.7 %copy-start.7 = (bf16[1,512,1024]{2,1,0:T(8,128)(2,1)S(1)}, bf16[1,512,1024]{2,1,0:T(8,128)(2,1)}, u32[]{:S(2)}) copy-start(bf16[1,512,1024]{2,1,0:T(8,128)(2,1)} %param.21) | copy-start | bytes 3145732
  200.3 12.7 %all-to-all-start.9 = ((bf16[8,32,512]{2,1,0:T(8,128)(2,1)}), bf16[8,32,512]{2,1,0:T(8,128)(2,1)S(1)}, u32[]{:S(2)}, u32[]{:S(2)}) async-start(bf16[8,32,512]{2,1,0:T(8,128)(2,1)} %broadcast_in_dim.21), calls=%async_computation.9 | async-start | bytes 524288 | tf_op jit(solution)/shard_map/all_to_all | solution.py:21
  214.4 21.0 %all-to-all-start.10 = ((bf16[32,8,1024]{2,1,0:T(8,128)(2,1)}), bf16[32,8,1024]{2,1,0:T(8,128)(2,1)S(1)}, u32[]{:S(2)}, u32[]{:S(2)}) async-start(bf16[32,8,1024]{2,1,0:T(8,128)(2,1)} %fusion.1), calls=%async_computation.10 | async-start | bytes 1048576 | tf_op jit(solution)/shard_map/all_to_all | solution.py:21
  235.5 11.4 %collective-permute-start.4 = (bf16[8,1024]{1,0:T(8,128)(2,1)S(1)}, bf16[8,1024]{1,0:T(8,128)(2,1)S(1)}, u32[]{:S(2)}, u32[]{:S(2)}) collective-permute-start(bf16[8,1024]{1,0:T(8,128)(2,1)S(1)} %fusion.82), channel_id=1, source_target_pairs={{0,256},{256,0},{1,257},{257,1},{2,258},{258,2},{3,259},{259,3},{4... | collective-permute-start | bytes 49160 | tf_op jit(solution)/shard_map/ppermute | solution.py:30

commit v2 on v1

--- a/solution.py
+++ b/solution.py
@@ -13,6 +13,7 @@
 EPS_LN = 1e-05
 EPS_RMS = 1e-06
 LANES = 128
+DEAD = 64.0
 BF = jnp.bfloat16
 F32 = jnp.float32
 
@@ -43,14 +44,46 @@
     return jnp.dot(a, b, preferred_element_type=F32)
 
 
-def keep_live(slot_rows, lengths, tile_count):
-    position = jnp.arange(slot_rows.shape[1], dtype=jnp.int32)[None, :]
-    keeping = jnp.where(
-        position < IMG,
-        position < tile_count[:, None] * TROWS,
-        position - IMG < lengths[:, None],
-    )
-    return slot_rows * keeping[:, :, None].astype(slot_rows.dtype)
+def doubling_gather(block, axis):
+    peers = lax.axis_size(axis)
+    blocks = block[None]
+    while blocks.shape[0] < peers:
+        step = blocks.shape[0]
+        came = lax.ppermute(blocks, axis, [(i, i ^ step) for i in range(peers)])
+        blocks = jnp.concatenate([blocks, came], axis=0)
+    return blocks
+
+
+def marked(rows, count):
+    alive = jnp.arange(rows.shape[0], dtype=jnp.int32) < count
+    return jnp.where(alive[:, None], rows, jnp.asarray(DEAD, rows.dtype))
+
+
+def placement(rows, key, kept):
+    count = rows.shape[0]
+    alive = jnp.broadcast_to((rows[:, :1] < DEAD / 2), (count, LANES)).astype(BF)
+    before = (key[None, :] < key[:, None]).astype(BF)
+    position = dot(before, alive)[:, :kept]
+    at = lax.broadcasted_iota(jnp.int32, (count, kept), 1).astype(F32)
+    return jnp.where(position == at, alive[:, :kept], jnp.asarray(0, BF))
+
+
+def pick(matrix, rows):
+    return lax.dot_general(
+        matrix, rows, (((0,), (0,)), ((), ())), preferred_element_type=F32
+    ).astype(BF)
+
+
+def to_tiles(rows):
+    count, width = rows.shape
+    tiles = rows.reshape(count // 8, 8, width // LANES, LANES).transpose(0, 2, 1, 3)
+    return tiles.reshape(-1, LANES)
+
+
+def from_tiles(tiles, width):
+    columns = width // LANES
+    rows = tiles.reshape(-1, columns, 8, LANES).transpose(0, 2, 1, 3)
+    return rows.reshape(-1, width)
 
 
 def projector_partial(image, gain, w_in):
@@ -103,18 +136,16 @@
     return (jax.nn.silu(gate_pre) * up_pre).astype(BF)
 
 
-def layer_blocks(rows, gain, w_gate, w_up, w_down, ordering):
+def layer_hidden(rows, gain, w_gate, w_up):
     mp = lax.axis_size("mp")
-    dp = lax.axis_size("dp")
     hidden = w_gate.shape[1]
     sent = layer_partial(rows, gain, w_gate, w_up)
     parts = exchange(sent.reshape(mp, rows.shape[0] // mp, -1), "mp")
-    inner = spread(layer_inner(parts, hidden), "mp").reshape(rows.shape[0], hidden)
-    if ordering is not None:
-        inner = dot(ordering, inner).astype(BF)
-    blocks = dot(inner, w_down).astype(BF)
-    blocks = exchange(blocks.reshape(dp, -1, blocks.shape[1]), "dp")
-    return jnp.sum(blocks.astype(F32), axis=0)
+    return spread(layer_inner(parts, hidden), "mp").reshape(rows.shape[0], hidden)
+
+
+def summed(blocks):
+    return jnp.sum(exchange(blocks, "dp").astype(F32), axis=0)
 
 
 def per_device(
@@ -135,36 +166,59 @@
     first = lax.axis_index("section") == 0
     place = lax.axis_index("dp")
     owners = prompt_owner[0]
+    img_live = dp * TROWS * MAXT * 3 // 4
     own = (norm_gain, gate_w[0], up_w[0], down_w[0])
     other = tuple(swap(array) for array in own)
     layer0 = [jnp.where(first, a, b) for a, b in zip(own, other)]
     layer1 = [jnp.where(first, b, a) for a, b in zip(own, other)]
+    layer0, layer1 = lax.optimization_barrier((layer0, layer1))
     layer0[0], layer1[0] = layer0[0][0], layer1[0][0]
 
-    live = keep_live(rollout_rows[0], response_lengths[0], tile_counts[0])[0]
-    gathered = spread(live, "dp")
-    image = gathered[:, :IMG].reshape(dp * IMG, width)
-
+    local = rollout_rows[0, 0]
+    gathered = spread(marked(local[:IMG], tile_counts[0, 0] * TROWS), "dp")
+    gathered = gathered.reshape(dp * IMG, width)
+    replies = doubling_gather(marked(local[IMG:], response_lengths[0, 0]), "dp")
+    replies = replies.reshape(dp * LMAX, width)
+
+    index = jnp.arange(dp * IMG, dtype=jnp.int32)
+    place_image = placement(gathered, index, img_live)
+    image = pick(place_image, gathered)
     sent = projector_partial(image, proj_gain, proj_in)
     parts = spread(sent, "mp")
-    active = projector_active(parts, dp * IMG, width)
-    blocks = exchange(dot(active, proj_out).astype(BF).reshape(dp, IMG, width), "dp")
-    projected = jnp.sum(blocks.astype(F32), axis=0).astype(BF)
-    all_projected = spread(projected, "dp")
-
-    own_rows = jnp.concatenate([projected, live[IMG:]], axis=0)
-    rows = jnp.concatenate([all_projected, gathered[:, IMG:]], axis=1).reshape(dp * SLOT, width)
-    total = layer_blocks(rows, *layer0, None)
-    own_next = (own_rows.astype(F32) + total).astype(BF)
-    rows_next = spread(own_next, "dp")
-
-    source = jnp.sum(jnp.where(owners == place, jnp.arange(dp, dtype=jnp.int32), 0))
-    slot_early = lax.dynamic_index_in_dim(rows_next, source, 0, keepdims=False)
-    row_at = jnp.arange(dp * SLOT, dtype=jnp.int32)
-    target = (owners[:, None] * SLOT + jnp.arange(SLOT, dtype=jnp.int32)[None, :]).reshape(-1)
-    ordering = (row_at[:, None] == target[None, :]).astype(BF)
-    total = layer_blocks(rows_next.reshape(dp * SLOT, width), *layer1, ordering)
-    slot_late = (slot_early.astype(F32) + total).astype(BF)
+    active = projector_active(parts, img_live, width)
+    blocks = to_tiles(dot(active, proj_out).astype(BF))
+    projected = summed(blocks.reshape(dp, -1, LANES)).astype(BF)
+    projected = from_tiles(spread(projected, "dp"), width)
+
+    prompt_at = (index // LMAX) ^ place
+    place_reply = placement(replies, prompt_at * LMAX + index % LMAX, img_live)
+    rows = jnp.concatenate([projected, pick(place_reply, replies)], axis=0)
+
+    slot_row = jnp.arange(dp * SLOT, dtype=jnp.int32)
+    image_row = owners[:, None] * SLOT + jnp.arange(IMG, dtype=jnp.int32)[None, :]
+    all_prompts = jnp.arange(dp, dtype=jnp.int32)
+    met = (all_prompts[:, None] ^ place) == all_prompts[None, :]
+    met_owner = jnp.sum(jnp.where(met, owners[None, :], 0), axis=1)
+    reply_row = met_owner[:, None] * SLOT + IMG + jnp.arange(LMAX, dtype=jnp.int32)[None, :]
+    to_image = (slot_row[:, None] == image_row.reshape(-1)[None, :]).astype(BF)
+    to_reply = (slot_row[:, None] == reply_row.reshape(-1)[None, :]).astype(BF)
+    ordering = jnp.concatenate(
+        [dot(to_image, place_image).astype(BF), dot(to_reply, place_reply).astype(BF)], axis=1
+    )
+    owned = lax.dynamic_slice_in_dim(ordering, place * SLOT, SLOT, 0)
+
+    inner = layer_hidden(rows, *layer0[:3])
+    blocks = to_tiles(dot(inner, layer0[3]).astype(BF)).reshape(dp, -1, LANES)
+    share = blocks.shape[1]
+    kept_tiles = lax.dynamic_slice_in_dim(to_tiles(rows), place * share, share, 0)
+    next_tiles = (kept_tiles.astype(F32) + summed(blocks)).astype(BF)
+    rows = from_tiles(spread(next_tiles, "dp"), width)
+
+    slot_early = dot(owned, rows).astype(BF)
+    inner = layer_hidden(rows, *layer1[:3])
+    inner = dot(ordering, inner).astype(BF)
+    blocks = dot(inner, layer1[3]).astype(BF).reshape(dp, SLOT, width)
+    slot_late = (slot_early.astype(F32) + summed(blocks)).astype(BF)
 
     came = swap(jnp.where(first, slot_late, slot_early))
     kept = jnp.where(first, slot_early, slot_late)

time: 249 us -> 236 us (0.948)
  blocking collectives: 60.7 us -> 25.1 us
  starting transfers between devices: 80.3 us -> 97.1 us
  other arithmetic: 5.61 us -> 12.2 us
    all_to_all x3 -> x2, blocking collectives: 60.7 us -> 25.1 us  [exchange(): return lax.all_to_all(blocks, axis, 0, 0, tiled=True)]
    ppermute x0 -> x5, starting transfers between devices: none -> 24.4 us  [doubling_gather(): came = lax.ppermute(blocks, axis, [(i, i ^ step) for i in range(peers)])]
    ppermute x0 -> x5, waiting for transfers between devices: none -> 8.14 us  [doubling_gather(): came = lax.ppermute(blocks, axis, [(i, i ^ step) for i in range(peers)])]
    select_n x1 -> x5, other arithmetic: 0.01 us -> 7.71 us  [the longest x4 6.91 us: per_device(): layer1 = [jnp.where(first, b, a) for a, b in zip(own, other)]]
    all_to_all x8 -> x9, waiting for transfers between devices: 80.2 us -> 72.7 us  [exchange(): return lax.all_to_all(blocks, axis, 0, 0, tiled=True)]
    all_to_all x8 -> x9, starting transfers between devices: 52.6 us -> 45.9 us  [exchange(): return lax.all_to_all(blocks, axis, 0, 0, tiled=True)]
    dot_general x9 -> x14, matrix products: 9.74 us -> 9.34 us  [dot(): return jnp.dot(a, b, preferred_element_type=F32)]
  transfers between devices with their start and end apart: 13 -> 19, of which waited for: 10 -> 12; matrix products, arithmetic and copies ran while one was open for 2% -> 7% of each run, Pallas kernels for 0% -> 0%
where the time goes in v2:
time: 236 us; the launch traced here: 234 us
  starting transfers between devices  97.1 us (41%)
  waiting for transfers between devices  81.7 us (35%)
  blocking collectives  25.1 us (11%)
  other arithmetic  12.2 us (5%)
  matrix products  9.83 us (4%)
  local copies, waits for them, and re-layouts  6.08 us (3%)
    all_to_all x9, waiting for transfers between devices, exchange(): return lax.all_to_all(blocks, axis, 0, 0, tiled=True)  72.7 us
    all_to_all x9, starting transfers between devices, exchange(): return lax.all_to_all(blocks, axis, 0, 0, tiled=True)  45.9 us
    ppermute x5, starting transfers between devices, swap(): return lax.ppermute(block, 'section', [(0, 1), (1, 0)])  26.8 us
    all_to_all x2, blocking collectives, exchange(): return lax.all_to_all(blocks, axis, 0, 0, tiled=True)  25.1 us
    ppermute x5, starting transfers between devices, doubling_gather(): came = lax.ppermute(blocks, axis, [(i, i ^ step) for i in range(peers)])  24.4 us
    dot_general x14, matrix products, dot(): return jnp.dot(a, b, preferred_element_type=F32)  9.34 us
    ppermute x5, waiting for transfers between devices, doubling_gather(): came = lax.ppermute(blocks, axis, [(i, i ^ step) for i in range(peers)])  8.14 us
    select_n x4, other arithmetic, per_device(): layer1 = [jnp.where(first, b, a) for a, b in zip(own, other)]  6.91 us
  transfers between devices with their start and end apart: 19, of which 12 were waited for; matrix products, arithmetic and copies ran while one was open for 7% of the time, Pallas kernels for 0%

profile of v2, /device:TPU:9, one launch (start us, length us, event | category | flops | bytes accessed | tf_op | source)
XLA Modules:
  0.0 234.0 jit_solution(1614961049647833434)
XLA Ops:
  10.5 7.4 %collective-permute-start = (bf16[1,4,1024]{2,1,0:T(4,128)(2,1)S(1)}, bf16[1,4,1024]{2,1,0:T(4,128)(2,1)S(1)}, u32[]{:S(2)}, u32[]{:S(2)}) collective-permute-start(bf16[1,4,1024]{2,1,0:T(4,128)(2,1)S(1)} %get-tuple-element.27), channel_id=1, source_target_pairs={{0,8},{8,0},{16,24},{24,16},{32,40},{40,32},{48,56},{56,48},{64,72... | collective-permute-start | bytes 24584 | tf_op jit(solution)/shard_map/ppermute | solution.py:52
  20.1 4.5 %all-to-all-start = ((bf16[32,4,1024]{2,1,0:T(4,128)(2,1)}), bf16[32,4,1024]{2,1,0:T(4,128)(2,1)S(1)}, u32[]{:S(2)}, u32[]{:S(2)}) async-start(bf16[32,4,1024]{2,1,0:T(4,128)(2,1)} %broadcast_in_dim.59), calls=%async_computation | async-start | bytes 524288 | tf_op jit(solution)/shard_map/all_to_all | solution.py:22
  25.6 4.0 %collective-permute-start.1 = (bf16[2,4,1024]{2,1,0:T(4,128)(2,1)S(1)}, bf16[2,4,1024]{2,1,0:T(4,128)(2,1)S(1)}, u32[]{:S(2)}, u32[]{:S(2)}) collective-permute-start(bf16[2,4,1024]{2,1,0:T(4,128)(2,1)S(1)} %pad_maximum_fusion.6), channel_id=1, source_target_pairs={{0,16},{8,24},{16,0},{24,8},{32,48},{40,56},{48,32},{56,40},{64,80... | collective-permute-start | bytes 49160 | tf_op jit(solution)/shard_map/ppermute | solution.py:52
  32.0 5.5 %collective-permute-start.2 = (bf16[4,4,1024]{2,1,0:T(4,128)(2,1)S(1)}, bf16[4,4,1024]{2,1,0:T(4,128)(2,1)S(1)}, u32[]{:S(2)}, u32[]{:S(2)}) collective-permute-start(bf16[4,4,1024]{2,1,0:T(4,128)(2,1)S(1)} %pad_maximum_fusion.5), channel_id=1, source_target_pairs={{0,32},{8,40},{16,48},{24,56},{32,0},{40,8},{48,16},{56,24},{64,96... | collective-permute-start | bytes 98312 | tf_op jit(solution)/shard_map/ppermute | solution.py:52
  45.6 10.0 %all-to-all-start.1 = ((bf16[8,112,256]{2,1,0:T(8,128)(2,1)}), bf16[8,112,256]{2,1,0:T(8,128)(2,1)S(1)}, u32[]{:S(2)}, u32[]{:S(2)}) async-start(bf16[8,112,256]{2,1,0:T(8,128)(2,1)} %broadcast_in_dim.69), calls=%async_computation.1 | async-start | bytes 917504 | tf_op jit(solution)/shard_map/all_to_all | solution.py:22
  55.8 4.3 %collective-permute-start.4 = (bf16[16,4,1024]{2,1,0:T(4,128)(2,1)S(1)}, bf16[16,4,1024]{2,1,0:T(4,128)(2,1)S(1)}, u32[]{:S(2)}, u32[]{:S(2)}) collective-permute-start(bf16[16,4,1024]{2,1,0:T(4,128)(2,1)S(1)} %get-tuple-element.34), channel_id=1, source_target_pairs={{0,128},{8,136},{16,144},{24,152},{32,160},{40,168},{48,176},{56,1... | collective-permute-start | bytes 393224 | tf_op jit(solution)/shard_map/ppermute | solution.py:52
  63.5 4.4 %all-to-all-done.1 = bf16[8,112,256]{2,1,0:T(8,128)(2,1)S(1)} async-done(((bf16[8,112,256]{2,1,0:T(8,128)(2,1)}), bf16[8,112,256]{2,1,0:T(8,128)(2,1)S(1)}, u32[]{:S(2)}, u32[]{:S(2)}) %all-to-all-start.1) | async-done | bytes 458784 | tf_op jit(solution)/shard_map/all_to_all | solution.py:22
  69.5 8.9 %all-to-all-start.2 = ((bf16[32,24,128]{2,1,0:T(8,128)(2,1)}), bf16[32,24,128]{2,1,0:T(8,128)(2,1)S(1)}, u32[]{:S(2)}, u32[]{:S(2)}) async-start(bf16[32,24,128]{2,1,0:T(8,128)(2,1)} %bitcast.10), calls=%async_computation.2 | async-start | bytes 393216 | tf_op jit(solution)/shard_map/all_to_all | solution.py:22
  81.5 6.7 %all-to-all-done.2 = bf16[32,24,128]{2,1,0:T(8,128)(2,1)S(1)} async-done(((bf16[32,24,128]{2,1,0:T(8,128)(2,1)}), bf16[32,24,128]{2,1,0:T(8,128)(2,1)S(1)}, u32[]{:S(2)}, u32[]{:S(2)}) %all-to-all-start.2) | async-done | bytes 196640 | tf_op jit(solution)/shard_map/all_to_all | solution.py:22
  88.9 3.7 %all-to-all-start.3 = ((bf16[32,24,128]{2,1,0:T(8,128)(2,1)}), bf16[32,24,128]{2,1,0:T(8,128)(2,1)S(1)}, u32[]{:S(2)}, u32[]{:S(2)}) async-start(bf16[32,24,128]{2,1,0:T(8,128)(2,1)} %broadcast_in_dim.70), calls=%async_computation.3 | async-start | bytes 393216 | tf_op jit(solution)/shard_map/all_to_all | solution.py:22
  96.8 5.4 %all-to-all-done.3 = bf16[32,24,128]{2,1,0:T(8,128)(2,1)S(1)} async-done(((bf16[32,24,128]{2,1,0:T(8,128)(2,1)}), bf16[32,24,128]{2,1,0:T(8,128)(2,1)S(1)}, u32[]{:S(2)}, u32[]{:S(2)}) %all-to-all-start.3) | async-done | bytes 196640 | tf_op jit(solution)/shard_map/all_to_all | solution.py:22
  104.7 14.1 %all_to_all.55 = bf16[8,24,1152]{2,1,0:T(8,128)(2,1)S(1)} all-to-all(bf16[8,24,1152]{2,1,0:T(8,128)(2,1)S(1)} %bitcast.94), channel_id=1, replica_groups=mesh['section'=2,'dp'=32,'mp'=8] {'mp'}, dimensions={0} | all-to-all | bytes 884736 | tf_op jit(solution)/shard_map/all_to_all | solution.py:22
  119.1 11.0 %all_to_all.56 = bf16[8,24,512]{2,1,0:T(8,128)(2,1)S(1)} all-to-all(bf16[8,24,512]{2,1,0:T(8,128)(2,1)S(1)} %broadcast_in_dim.71), channel_id=1, replica_groups=mesh['section'=2,'dp'=32,'mp'=8] {'mp'}, dimensions={0} | all-to-all | bytes 393216 | tf_op jit(solution)/shard_map/all_to_all | solution.py:22
  131.3 3.8 %all-to-all-start.6 = ((bf16[32,48,128]{2,1,0:T(8,128)(2,1)}), bf16[32,48,128]{2,1,0:T(8,128)(2,1)S(1)}, u32[]{:S(2)}, u32[]{:S(2)}) async-start(bf16[32,48,128]{2,1,0:T(8,128)(2,1)} %bitcast.26), calls=%async_computation.6 | async-start | bytes 786432 | tf_op jit(solution)/shard_map/all_to_all | solution.py:22
  135.1 11.4 %all-to-all-done.6 = bf16[32,48,128]{2,1,0:T(8,128)(2,1)S(1)} async-done(((bf16[32,48,128]{2,1,0:T(8,128)(2,1)}), bf16[32,48,128]{2,1,0:T(8,128)(2,1)S(1)}, u32[]{:S(2)}, u32[]{:S(2)}) %all-to-all-start.6) | async-done | bytes 393248 | tf_op jit(solution)/shard_map/all_to_all | solution.py:22
  147.4 4.0 %all-to-all-start.7 = ((bf16[32,48,128]{2,1,0:T(8,128)(2,1)}), bf16[32,48,128]{2,1,0:T(8,128)(2,1)S(1)}, u32[]{:S(2)}, u32[]{:S(2)}) async-start(bf16[32,48,128]{2,1,0:T(8,128)(2,1)} %broadcast_in_dim.72), calls=%async_computation.7 | async-start | bytes 786432 | tf_op jit(solution)/shard_map/all_to_all | solution.py:22
  152.3 10.9 %all-to-all-done.7 = bf16[32,48,128]{2,1,0:T(8,128)(2,1)S(1)} async-done(((bf16[32,48,128]{2,1,0:T(8,128)(2,1)}), bf16[32,48,128]{2,1,0:T(8,128)(2,1)S(1)}, u32[]{:S(2)}, u32[]{:S(2)}) %all-to-all-start.7) | async-done | bytes 393248 | tf_op jit(solution)/shard_map/all_to_all | solution.py:22
  166.4 3.5 %all-to-all-start.8 = ((bf16[8,24,1152]{2,1,0:T(8,128)(2,1)}), bf16[8,24,1152]{2,1,0:T(8,128)(2,1)S(1)}, u32[]{:S(2)}, u32[]{:S(2)}) async-start(bf16[8,24,1152]{2,1,0:T(8,128)(2,1)} %bitcast.33), calls=%async_computation.8 | async-start | bytes 884736 | tf_op jit(solution)/shard_map/all_to_all | solution.py:22
  170.3 10.8 %all-to-all-done.8 = bf16[8,24,1152]{2,1,0:T(8,128)(2,1)S(1)} async-done(((bf16[8,24,1152]{2,1,0:T(8,128)(2,1)}), bf16[8,24,1152]{2,1,0:T(8,128)(2,1)S(1)}, u32[]{:S(2)}, u32[]{:S(2)}) %all-to-all-start.8) | async-done | bytes 442400 | tf_op jit(solution)/shard_map/all_to_all | solution.py:22
  182.0 3.4 %all-to-all-start.9 = ((bf16[8,24,512]{2,1,0:T(8,128)(2,1)}), bf16[8,24,512]{2,1,0:T(8,128)(2,1)S(1)}, u32[]{:S(2)}, u32[]{:S(2)}) async-start(bf16[8,24,512]{2,1,0:T(8,128)(2,1)} %broadcast_in_dim.73), calls=%async_computation.9 | async-start | bytes 393216 | tf_op jit(solution)/shard_map/all_to_all | solution.py:22
  185.8 10.5 %all-to-all-done.9 = bf16[8,24,512]{2,1,0:T(8,128)(2,1)S(1)} async-done(((bf16[8,24,512]{2,1,0:T(8,128)(2,1)}), bf16[8,24,512]{2,1,0:T(8,128)(2,1)S(1)}, u32[]{:S(2)}, u32[]{:S(2)}) %all-to-all-start.9) | async-done | bytes 196640 | tf_op jit(solution)/shard_map/all_to_all | solution.py:22
  197.7 4.2 %all-to-all-start.10 = ((bf16[32,8,1024]{2,1,0:T(8,128)(2,1)}), bf16[32,8,1024]{2,1,0:T(8,128)(2,1)S(1)}, u32[]{:S(2)}, u32[]{:S(2)}) async-start(bf16[32,8,1024]{2,1,0:T(8,128)(2,1)} %fusion), calls=%async_computation.10 | async-start | bytes 1048576 | tf_op jit(solution)/shard_map/all_to_all | solution.py:22
  201.9 12.6 %all-to-all-done.10 = bf16[32,8,1024]{2,1,0:T(8,128)(2,1)S(1)} async-done(((bf16[32,8,1024]{2,1,0:T(8,128)(2,1)}), bf16[32,8,1024]{2,1,0:T(8,128)(2,1)S(1)}, u32[]{:S(2)}, u32[]{:S(2)}) %all-to-all-start.10) | async-done | bytes 524320 | tf_op jit(solution)/shard_map/all_to_all | solution.py:22
  214.8 17.8 %collective-permute-start.9 = (bf16[8,1024]{1,0:T(8,128)(2,1)S(1)}, bf16[8,1024]{1,0:T(8,128)(2,1)S(1)}, u32[]{:S(2)}, u32[]{:S(2)}) collective-permute-start(bf16[8,1024]{1,0:T(8,128)(2,1)S(1)} %get-tuple-element.37), channel_id=1, source_target_pairs={{0,256},{256,0},{1,257},{257,1},{2,258},{258,2},{3,259},{259,3},{4... | collective-permute-start | bytes 49160 | tf_op jit(solution)/shard_map/ppermute | solution.py:31
  (136 shorter events, 49.2 us)
Async XLA Ops:
  0.0 68.4 %copy-start = (bf16[256,1024]{1,0:T(8,128)(2,1)S(1)}, bf16[256,1024]{1,0:T(8,128)(2,1)}, u32[]{:S(2)}) copy-start(bf16[256,1024]{1,0:T(8,128)(2,1)} %param.17) | copy-start | bytes 1572868
  0.0 25.3 %copy-start.1 = (bf16[1024,256]{1,0:T(8,128)(2,1)S(1)}, bf16[1024,256]{1,0:T(8,128)(2,1)}, u32[]{:S(2)}) copy-start(bf16[1024,256]{1,0:T(8,128)(2,1)} %param.16) | copy-start | bytes 1572868
  0.0 60.1 %collective-permute-start.5 = (bf16[1,1024]{1,0:T(2,128)(2,1)}, bf16[1,1024]{1,0:T(2,128)(2,1)S(1)}, u32[]{:S(2)}, u32[]{:S(2)}) collective-permute-start(bf16[1,1024]{1,0:T(2,128)(2,1)} %param.18), channel_id=1, source_target_pairs={{0,256},{256,0},{1,257},{257,1},{2,258},{258,2},{3,259},{259,3},{4... | collective-permute-start | bytes 6152 | tf_op jit(solution)/shard_map/ppermute | solution.py:31
  2.7 76.0 %collective-permute-start.6 = (bf16[1024,512]{1,0:T(8,128)(2,1)}, bf16[1024,512]{1,0:T(8,128)(2,1)}, u32[]{:S(2)}, u32[]{:S(2)}) collective-permute-start(bf16[1024,512]{1,0:T(8,128)(2,1)} %bitcast.99), channel_id=1, source_target_pairs={{0,256},{256,0},{1,257},{257,1},{2,258},{258,2},{3,259},{259,3},{4... | collective-permute-start | bytes 3145736 | tf_op jit(solution)/shard_map/ppermute | solution.py:31
  4.7 88.0 %collective-permute-start.7 = (bf16[1024,512]{1,0:T(8,128)(2,1)}, bf16[1024,512]{1,0:T(8,128)(2,1)}, u32[]{:S(2)}, u32[]{:S(2)}) collective-permute-start(bf16[1024,512]{1,0:T(8,128)(2,1)} %bitcast.100), channel_id=1, source_target_pairs={{0,256},{256,0},{1,257},{257,1},{2,258},{258,2},{3,259},{259,3},{4... | collective-permute-start | bytes 3145736 | tf_op jit(solution)/shard_map/ppermute | solution.py:31
  7.1 88.3 %collective-permute-start.8 = (bf16[512,1024]{1,0:T(8,128)(2,1)}, bf16[512,1024]{1,0:T(8,128)(2,1)}, u32[]{:S(2)}, u32[]{:S(2)}) collective-permute-start(bf16[512,1024]{1,0:T(8,128)(2,1)} %bitcast.101), channel_id=1, source_target_pairs={{0,256},{256,0},{1,257},{257,1},{2,258},{258,2},{3,259},{259,3},{4... | collective-permute-start | bytes 3145736 | tf_op jit(solution)/shard_map/ppermute | solution.py:31
  10.5 15.1 %collective-permute-start = (bf16[1,4,1024]{2,1,0:T(4,128)(2,1)S(1)}, bf16[1,4,1024]{2,1,0:T(4,128)(2,1)S(1)}, u32[]{:S(2)}, u32[]{:S(2)}) collective-permute-start(bf16[1,4,1024]{2,1,0:T(4,128)(2,1)S(1)} %get-tuple-element.27), channel_id=1, source_target_pairs={{0,8},{8,0},{16,24},{24,16},{32,40},{40,32},{48,56},{56,48},{64,72... | collective-permute-start | bytes 24584 | tf_op jit(solution)/shard_map/ppermute | solution.py:52
  20.1 23.6 %all-to-all-start = ((bf16[32,4,1024]{2,1,0:T(4,128)(2,1)}), bf16[32,4,1024]{2,1,0:T(4,128)(2,1)S(1)}, u32[]{:S(2)}, u32[]{:S(2)}) async-start(bf16[32,4,1024]{2,1,0:T(4,128)(2,1)} %broadcast_in_dim.59), calls=%async_computation | async-start | bytes 524288 | tf_op jit(solution)/shard_map/all_to_all | solution.py:22
  25.6 6.3 %collective-permute-start.1 = (bf16[2,4,1024]{2,1,0:T(4,128)(2,1)S(1)}, bf16[2,4,1024]{2,1,0:T(4,128)(2,1)S(1)}, u32[]{:S(2)}, u32[]{:S(2)}) collective-permute-start(bf16[2,4,1024]{2,1,0:T(4,128)(2,1)S(1)} %pad_maximum_fusion.6), channel_id=1, source_target_pairs={{0,16},{8,24},{16,0},{24,8},{32,48},{40,56},{48,32},{56,40},{64,80... | collective-permute-start | bytes 49160 | tf_op jit(solution)/shard_map/ppermute | solution.py:52
  32.0 8.6 %collective-permute-start.2 = (bf16[4,4,1024]{2,1,0:T(4,128)(2,1)S(1)}, bf16[4,4,1024]{2,1,0:T(4,128)(2,1)S(1)}, u32[]{:S(2)}, u32[]{:S(2)}) collective-permute-start(bf16[4,4,1024]{2,1,0:T(4,128)(2,1)S(1)} %pad_maximum_fusion.5), channel_id=1, source_target_pairs={{0,32},{8,40},{16,48},{24,56},{32,0},{40,8},{48,16},{56,24},{64,96... | collective-permute-start | bytes 98312 | tf_op jit(solution)/shard_map/ppermute | solution.py:52
  40.6 15.1 %collective-permute-start.3 = (bf16[8,4,1024]{2,1,0:T(4,128)(2,1)S(1)}, bf16[8,4,1024]{2,1,0:T(4,128)(2,1)S(1)}, u32[]{:S(2)}, u32[]{:S(2)}) collective-permute-start(bf16[8,4,1024]{2,1,0:T(4,128)(2,1)S(1)} %pad_maximum_fusion.4), channel_id=1, source_target_pairs={{0,64},{8,72},{16,80},{24,88},{32,96},{40,104},{48,112},{56,120},{... | collective-permute-start | bytes 196616 | tf_op jit(solution)/shard_map/ppermute | solution.py:52
  45.6 22.3 %all-to-all-start.1 = ((bf16[8,112,256]{2,1,0:T(8,128)(2,1)}), bf16[8,112,256]{2,1,0:T(8,128)(2,1)S(1)}, u32[]{:S(2)}, u32[]{:S(2)}) async-start(bf16[8,112,256]{2,1,0:T(8,128)(2,1)} %broadcast_in_dim.69), calls=%async_computation.1 | async-start | bytes 917504 | tf_op jit(solution)/shard_map/all_to_all | solution.py:22
  55.7 4.4 %copy-start.8 = (bf16[1,1024]{1,0:T(2,128)(2,1)S(1)}, bf16[1,1024]{1,0:T(2,128)(2,1)}, u32[]{:S(2)}) copy-start(bf16[1,1024]{1,0:T(2,128)(2,1)} %param.18) | copy-start | bytes 6148
  55.8 7.2 %collective-permute-start.4 = (bf16[16,4,1024]{2,1,0:T(4,128)(2,1)S(1)}, bf16[16,4,1024]{2,1,0:T(4,128)(2,1)S(1)}, u32[]{:S(2)}, u32[]{:S(2)}) collective-permute-start(bf16[16,4,1024]{2,1,0:T(4,128)(2,1)S(1)} %get-tuple-element.34), channel_id=1, source_target_pairs={{0,128},{8,136},{16,144},{24,152},{32,160},{40,168},{48,176},{56,1... | collective-permute-start | bytes 393224 | tf_op jit(solution)/shard_map/ppermute | solution.py:52
  68.4 10.3 %copy-start.2 = (bf16[1,1024,512]{2,1,0:T(8,128)(2,1)S(1)}, bf16[1,1024,512]{2,1,0:T(8,128)(2,1)}, u32[]{:S(2)}) copy-start(bf16[1,1024,512]{2,1,0:T(8,128)(2,1)} %param.19) | copy-start | bytes 3145732
  69.5 18.6 %all-to-all-start.2 = ((bf16[32,24,128]{2,1,0:T(8,128)(2,1)}), bf16[32,24,128]{2,1,0:T(8,128)(2,1)S(1)}, u32[]{:S(2)}, u32[]{:S(2)}) async-start(bf16[32,24,128]{2,1,0:T(8,128)(2,1)} %bitcast.10), calls=%async_computation.2 | async-start | bytes 393216 | tf_op jit(solution)/shard_map/all_to_all | solution.py:22
  78.7 13.9 %copy-start.3 = (bf16[1,1024,512]{2,1,0:T(8,128)(2,1)S(1)}, bf16[1,1024,512]{2,1,0:T(8,128)(2,1)}, u32[]{:S(2)}) copy-start(bf16[1,1024,512]{2,1,0:T(8,128)(2,1)} %param.20) | copy-start | bytes 3145732
  88.9 13.3 %all-to-all-start.3 = ((bf16[32,24,128]{2,1,0:T(8,128)(2,1)}), bf16[32,24,128]{2,1,0:T(8,128)(2,1)S(1)}, u32[]{:S(2)}, u32[]{:S(2)}) async-start(bf16[32,24,128]{2,1,0:T(8,128)(2,1)} %broadcast_in_dim.70), calls=%async_computation.3 | async-start | bytes 393216 | tf_op jit(solution)/shard_map/all_to_all | solution.py:22
  131.3 15.3 %all-to-all-start.6 = ((bf16[32,48,128]{2,1,0:T(8,128)(2,1)}), bf16[32,48,128]{2,1,0:T(8,128)(2,1)S(1)}, u32[]{:S(2)}, u32[]{:S(2)}) async-start(bf16[32,48,128]{2,1,0:T(8,128)(2,1)} %bitcast.26), calls=%async_computation.6 | async-start | bytes 786432 | tf_op jit(solution)/shard_map/all_to_all | solution.py:22
  147.4 15.7 %all-to-all-start.7 = ((bf16[32,48,128]{2,1,0:T(8,128)(2,1)}), bf16[32,48,128]{2,1,0:T(8,128)(2,1)S(1)}, u32[]{:S(2)}, u32[]{:S(2)}) async-start(bf16[32,48,128]{2,1,0:T(8,128)(2,1)} %broadcast_in_dim.72), calls=%async_computation.7 | async-start | bytes 786432 | tf_op jit(solution)/shard_map/all_to_all | solution.py:22
  166.4 14.7 %all-to-all-start.8 = ((bf16[8,24,1152]{2,1,0:T(8,128)(2,1)}), bf16[8,24,1152]{2,1,0:T(8,128)(2,1)S(1)}, u32[]{:S(2)}, u32[]{:S(2)}) async-start(bf16[8,24,1152]{2,1,0:T(8,128)(2,1)} %bitcast.33), calls=%async_computation.8 | async-start | bytes 884736 | tf_op jit(solution)/shard_map/all_to_all | solution.py:22
  182.0 14.2 %all-to-all-start.9 = ((bf16[8,24,512]{2,1,0:T(8,128)(2,1)}), bf16[8,24,512]{2,1,0:T(8,128)(2,1)S(1)}, u32[]{:S(2)}, u32[]{:S(2)}) async-start(bf16[8,24,512]{2,1,0:T(8,128)(2,1)} %broadcast_in_dim.73), calls=%async_computation.9 | async-start | bytes 393216 | tf_op jit(solution)/shard_map/all_to_all | solution.py:22
  197.7 16.8 %all-to-all-start.10 = ((bf16[32,8,1024]{2,1,0:T(8,128)(2,1)}), bf16[32,8,1024]{2,1,0:T(8,128)(2,1)S(1)}, u32[]{:S(2)}, u32[]{:S(2)}) async-start(bf16[32,8,1024]{2,1,0:T(8,128)(2,1)} %fusion), calls=%async_computation.10 | async-start | bytes 1048576 | tf_op jit(solution)/shard_map/all_to_all | solution.py:22
  214.8 18.6 %collective-permute-start.9 = (bf16[8,1024]{1,0:T(8,128)(2,1)S(1)}, bf16[8,1024]{1,0:T(8,128)(2,1)S(1)}, u32[]{:S(2)}, u32[]{:S(2)}) collective-permute-start(bf16[8,1024]{1,0:T(8,128)(2,1)S(1)} %get-tuple-element.37), channel_id=1, source_target_pairs={{0,256},{256,0},{1,257},{257,1},{2,258},{258,2},{3,259},{259,3},{4... | collective-permute-start | bytes 49160 | tf_op jit(solution)/shard_map/ppermute | solution.py:31
  (5 other events, 7.9 us)

commit v3 on v2

--- a/solution.py
+++ b/solution.py
@@ -42,16 +42,6 @@
 
 def dot(a, b):
     return jnp.dot(a, b, preferred_element_type=F32)
-
-
-def doubling_gather(block, axis):
-    peers = lax.axis_size(axis)
-    blocks = block[None]
-    while blocks.shape[0] < peers:
-        step = blocks.shape[0]
-        came = lax.ppermute(blocks, axis, [(i, i ^ step) for i in range(peers)])
-        blocks = jnp.concatenate([blocks, came], axis=0)
-    return blocks
 
 
 def marked(rows, count):
@@ -167,18 +157,25 @@
     place = lax.axis_index("dp")
     owners = prompt_owner[0]
     img_live = dp * TROWS * MAXT * 3 // 4
+    local = rollout_rows[0, 0]
+    local = jnp.concatenate(
+        [
+            marked(local[:IMG], tile_counts[0, 0] * TROWS),
+            marked(local[IMG:], response_lengths[0, 0]),
+        ]
+    )
+    copies = jnp.broadcast_to(local[None], (dp,) + local.shape)
     own = (norm_gain, gate_w[0], up_w[0], down_w[0])
+    own, copies = lax.optimization_barrier((own, copies))
     other = tuple(swap(array) for array in own)
     layer0 = [jnp.where(first, a, b) for a, b in zip(own, other)]
     layer1 = [jnp.where(first, b, a) for a, b in zip(own, other)]
     layer0, layer1 = lax.optimization_barrier((layer0, layer1))
     layer0[0], layer1[0] = layer0[0][0], layer1[0][0]
 
-    local = rollout_rows[0, 0]
-    gathered = spread(marked(local[:IMG], tile_counts[0, 0] * TROWS), "dp")
-    gathered = gathered.reshape(dp * IMG, width)
-    replies = doubling_gather(marked(local[IMG:], response_lengths[0, 0]), "dp")
-    replies = replies.reshape(dp * LMAX, width)
+    everyone = exchange(copies, "dp")
+    gathered = everyone[:, :IMG].reshape(dp * IMG, width)
+    replies = everyone[:, IMG:].reshape(dp * LMAX, width)
 
     index = jnp.arange(dp * IMG, dtype=jnp.int32)
     place_image = placement(gathered, index, img_live)
@@ -190,16 +187,12 @@
     projected = summed(blocks.reshape(dp, -1, LANES)).astype(BF)
     projected = from_tiles(spread(projected, "dp"), width)
 
-    prompt_at = (index // LMAX) ^ place
-    place_reply = placement(replies, prompt_at * LMAX + index % LMAX, img_live)
+    place_reply = placement(replies, index, img_live)
     rows = jnp.concatenate([projected, pick(place_reply, replies)], axis=0)
 
     slot_row = jnp.arange(dp * SLOT, dtype=jnp.int32)
     image_row = owners[:, None] * SLOT + jnp.arange(IMG, dtype=jnp.int32)[None, :]
-    all_prompts = jnp.arange(dp, dtype=jnp.int32)
-    met = (all_prompts[:, None] ^ place) == all_prompts[None, :]
-    met_owner = jnp.sum(jnp.where(met, owners[None, :], 0), axis=1)
-    reply_row = met_owner[:, None] * SLOT + IMG + jnp.arange(LMAX, dtype=jnp.int32)[None, :]
+    reply_row = owners[:, None] * SLOT + IMG + jnp.arange(LMAX, dtype=jnp.int32)[None, :]
     to_image = (slot_row[:, None] == image_row.reshape(-1)[None, :]).astype(BF)
     to_reply = (slot_row[:, None] == reply_row.reshape(-1)[None, :]).astype(BF)
     ordering = jnp.concatenate(

time: 236 us -> 219 us (0.928)
  starting transfers between devices: 97.1 us -> 77.3 us
    ppermute x5 -> x0, starting transfers between devices: 24.4 us -> none  [doubling_gather(): came = lax.ppermute(blocks, axis, [(i, i ^ step) for i in range(peers)])]
    all_to_all x9, waiting for transfers between devices: 72.7 us -> 81.8 us  [exchange(): return lax.all_to_all(blocks, axis, 0, 0, tiled=True)]
    all_to_all x9, starting transfers between devices: 45.9 us -> 54.1 us  [exchange(): return lax.all_to_all(blocks, axis, 0, 0, tiled=True)]
    ppermute x5 -> x0, waiting for transfers between devices: 8.14 us -> none  [doubling_gather(): came = lax.ppermute(blocks, axis, [(i, i ^ step) for i in range(peers)])]
    ppermute x5, starting transfers between devices: 26.8 us -> 23.1 us  [swap(): return lax.ppermute(block, 'section', [(0, 1), (1, 0)])]
  transfers between devices with their start and end apart: 19 -> 14, of which waited for: 12 -> 9; matrix products, arithmetic and copies ran while one was open for 7% -> 6% of each run, Pallas kernels for 0% -> 0%
where the time goes in v3:
time: 219 us; the launch traced here: 218 us
  waiting for transfers between devices  82.6 us (38%)
  starting transfers between devices  77.3 us (35%)
  blocking collectives  26.8 us (12%)
  other arithmetic  11.4 us (5%)
  matrix products  10.4 us (5%)
  local copies, waits for them, and re-layouts  7.33 us (3%)
    all_to_all x9, waiting for transfers between devices, exchange(): return lax.all_to_all(blocks, axis, 0, 0, tiled=True)  81.8 us
    all_to_all x9, starting transfers between devices, exchange(): return lax.all_to_all(blocks, axis, 0, 0, tiled=True)  54.1 us
    all_to_all x2, blocking collectives, exchange(): return lax.all_to_all(blocks, axis, 0, 0, tiled=True)  26.8 us
    ppermute x5, starting transfers between devices, swap(): return lax.ppermute(block, 'section', [(0, 1), (1, 0)])  23.1 us
    dot_general x14, matrix products, dot(): return jnp.dot(a, b, preferred_element_type=F32)  9.94 us
    select_n x4, other arithmetic, per_device(): layer1 = [jnp.where(first, b, a) for a, b in zip(own, other)]  7.11 us
  transfers between devices with their start and end apart: 14, of which 9 were waited for; matrix products, arithmetic and copies ran while one was open for 6% of the time, Pallas kernels for 0%

profile of v3, /device:TPU:9, one launch (start us, length us, event | category | flops | bytes accessed | tf_op | source)
XLA Modules:
  0.0 217.9 jit_solution(7277902730361612299)
XLA Ops:
  3.1 9.7 %all-to-all-start = ((bf16[32,8,1024]{2,1,0:T(8,128)(2,1)}), bf16[32,8,1024]{2,1,0:T(8,128)(2,1)S(1)}, u32[]{:S(2)}, u32[]{:S(2)}) async-start(bf16[32,8,1024]{2,1,0:T(8,128)(2,1)} %broadcast_in_dim.46), calls=%async_computation | async-start | bytes 1048576 | tf_op jit(solution)/shard_map/all_to_all | solution.py:22
  13.1 15.7 %all-to-all-done = bf16[32,8,1024]{2,1,0:T(8,128)(2,1)S(1)} async-done(((bf16[32,8,1024]{2,1,0:T(8,128)(2,1)}), bf16[32,8,1024]{2,1,0:T(8,128)(2,1)S(1)}, u32[]{:S(2)}, u32[]{:S(2)}) %all-to-all-start) | async-done | bytes 524320 | tf_op jit(solution)/shard_map/all_to_all | solution.py:22
  32.0 10.2 %all-to-all-start.1 = ((bf16[8,112,256]{2,1,0:T(8,128)(2,1)}), bf16[8,112,256]{2,1,0:T(8,128)(2,1)S(1)}, u32[]{:S(2)}, u32[]{:S(2)}) async-start(bf16[8,112,256]{2,1,0:T(8,128)(2,1)} %broadcast_in_dim.52), calls=%async_computation.1 | async-start | bytes 917504 | tf_op jit(solution)/shard_map/all_to_all | solution.py:22
  42.1 5.0 %collective-permute-start = (bf16[1,1024]{1,0:T(2,128)(2,1)S(1)}, bf16[1,1024]{1,0:T(2,128)(2,1)S(1)}, u32[]{:S(2)}, u32[]{:S(2)}) collective-permute-start(bf16[1,1024]{1,0:T(2,128)(2,1)S(1)} %copy-done.10), channel_id=1, source_target_pairs={{0,256},{256,0},{1,257},{257,1},{2,258},{258,2},{3,259},{259,3},{4... | collective-permute-start | bytes 6152 | tf_op jit(solution)/shard_map/ppermute | solution.py:31
  49.1 2.4 %collective-permute-start.2 = (bf16[1024,512]{1,0:T(8,128)(2,1)}, bf16[1024,512]{1,0:T(8,128)(2,1)S(1)}, u32[]{:S(2)}, u32[]{:S(2)}) collective-permute-start(bf16[1024,512]{1,0:T(8,128)(2,1)} %bitcast.2), channel_id=1, source_target_pairs={{0,256},{256,0},{1,257},{257,1},{2,258},{258,2},{3,259},{259,3},{4... | collective-permute-start | bytes 3145736 | tf_op jit(solution)/shard_map/ppermute | solution.py:31
  57.1 8.6 %all-to-all-start.2 = ((bf16[32,24,128]{2,1,0:T(8,128)(2,1)}), bf16[32,24,128]{2,1,0:T(8,128)(2,1)S(1)}, u32[]{:S(2)}, u32[]{:S(2)}) async-start(bf16[32,24,128]{2,1,0:T(8,128)(2,1)} %bitcast.13), calls=%async_computation.2 | async-start | bytes 393216 | tf_op jit(solution)/shard_map/all_to_all | solution.py:22
  65.9 2.7 %broadcast_select_fusion.3 = (bf16[1024,512]{1,0:T(8,128)(2,1)}, bf16[1024,512]{1,0:T(8,128)(2,1)}) fusion(bf16[1024,512]{1,0:T(8,128)(2,1)} %collective-permute-done.1, bf16[1024,512]{1,0:T(8,128)(2,1)S(1)} %bitcast.95, pred[]{:T(512)S(6)} %eq.35), kind=kLoop, calls=%fused_computation.25 | loop fusion | flops 1048576 | bytes 4194305 | tf_op jit(solution)/shard_map/jit(_where)/select_n | solution.py:172
  68.6 6.9 %all-to-all-done.2 = bf16[32,24,128]{2,1,0:T(8,128)(2,1)S(1)} async-done(((bf16[32,24,128]{2,1,0:T(8,128)(2,1)}), bf16[32,24,128]{2,1,0:T(8,128)(2,1)S(1)}, u32[]{:S(2)}, u32[]{:S(2)}) %all-to-all-start.2) | async-done | bytes 196640 | tf_op jit(solution)/shard_map/all_to_all | solution.py:22
  76.2 4.6 %all-to-all-start.3 = ((bf16[32,24,128]{2,1,0:T(8,128)(2,1)}), bf16[32,24,128]{2,1,0:T(8,128)(2,1)S(1)}, u32[]{:S(2)}, u32[]{:S(2)}) async-start(bf16[32,24,128]{2,1,0:T(8,128)(2,1)} %broadcast_in_dim.53), calls=%async_computation.3 | async-start | bytes 393216 | tf_op jit(solution)/shard_map/all_to_all | solution.py:22
  80.8 2.7 %broadcast_select_fusion.2 = (bf16[1024,512]{1,0:T(8,128)(2,1)}, bf16[1024,512]{1,0:T(8,128)(2,1)}) fusion(bf16[1024,512]{1,0:T(8,128)(2,1)S(1)} %collective-permute-done.2, bf16[1024,512]{1,0:T(8,128)(2,1)} %bitcast.2, pred[]{:T(512)S(6)} %eq.35), kind=kLoop, calls=%fused_computation.24 | loop fusion | flops 1048576 | bytes 4194305 | tf_op jit(solution)/shard_map/jit(_where)/select_n | solution.py:172
  85.3 5.2 %all-to-all-done.3 = bf16[32,24,128]{2,1,0:T(8,128)(2,1)S(1)} async-done(((bf16[32,24,128]{2,1,0:T(8,128)(2,1)}), bf16[32,24,128]{2,1,0:T(8,128)(2,1)S(1)}, u32[]{:S(2)}, u32[]{:S(2)}) %all-to-all-start.3) | async-done | bytes 196640 | tf_op jit(solution)/shard_map/all_to_all | solution.py:22
  93.0 15.1 %all_to_all.55 = bf16[8,24,1152]{2,1,0:T(8,128)(2,1)S(1)} all-to-all(bf16[8,24,1152]{2,1,0:T(8,128)(2,1)S(1)} %bitcast.89), channel_id=1, replica_groups=mesh['section'=2,'dp'=32,'mp'=8] {'mp'}, dimensions={0} | all-to-all | bytes 884736 | tf_op jit(solution)/shard_map/all_to_all | solution.py:22
  108.4 11.7 %all_to_all.56 = bf16[8,24,512]{2,1,0:T(8,128)(2,1)S(1)} all-to-all(bf16[8,24,512]{2,1,0:T(8,128)(2,1)S(1)} %broadcast_in_dim.54), channel_id=1, replica_groups=mesh['section'=2,'dp'=32,'mp'=8] {'mp'}, dimensions={0} | all-to-all | bytes 393216 | tf_op jit(solution)/shard_map/all_to_all | solution.py:22
  121.2 5.4 %all-to-all-start.6 = ((bf16[32,48,128]{2,1,0:T(8,128)(2,1)}), bf16[32,48,128]{2,1,0:T(8,128)(2,1)S(1)}, u32[]{:S(2)}, u32[]{:S(2)}) async-start(bf16[32,48,128]{2,1,0:T(8,128)(2,1)} %bitcast.26), calls=%async_computation.6 | async-start | bytes 786432 | tf_op jit(solution)/shard_map/all_to_all | solution.py:22
  126.7 11.4 %all-to-all-done.6 = bf16[32,48,128]{2,1,0:T(8,128)(2,1)S(1)} async-done(((bf16[32,48,128]{2,1,0:T(8,128)(2,1)}), bf16[32,48,128]{2,1,0:T(8,128)(2,1)S(1)}, u32[]{:S(2)}, u32[]{:S(2)}) %all-to-all-start.6) | async-done | bytes 393248 | tf_op jit(solution)/shard_map/all_to_all | solution.py:22
  139.0 4.3 %all-to-all-start.7 = ((bf16[32,48,128]{2,1,0:T(8,128)(2,1)}), bf16[32,48,128]{2,1,0:T(8,128)(2,1)S(1)}, u32[]{:S(2)}, u32[]{:S(2)}) async-start(bf16[32,48,128]{2,1,0:T(8,128)(2,1)} %broadcast_in_dim.55), calls=%async_computation.7 | async-start | bytes 786432 | tf_op jit(solution)/shard_map/all_to_all | solution.py:22
  143.3 11.4 %all-to-all-done.7 = bf16[32,48,128]{2,1,0:T(8,128)(2,1)S(1)} async-done(((bf16[32,48,128]{2,1,0:T(8,128)(2,1)}), bf16[32,48,128]{2,1,0:T(8,128)(2,1)S(1)}, u32[]{:S(2)}, u32[]{:S(2)}) %all-to-all-start.7) | async-done | bytes 393248 | tf_op jit(solution)/shard_map/all_to_all | solution.py:22
  158.0 3.6 %all-to-all-start.8 = ((bf16[8,24,1152]{2,1,0:T(8,128)(2,1)}), bf16[8,24,1152]{2,1,0:T(8,128)(2,1)S(1)}, u32[]{:S(2)}, u32[]{:S(2)}) async-start(bf16[8,24,1152]{2,1,0:T(8,128)(2,1)} %bitcast.33), calls=%async_computation.8 | async-start | bytes 884736 | tf_op jit(solution)/shard_map/all_to_all | solution.py:22
  162.0 10.9 %all-to-all-done.8 = bf16[8,24,1152]{2,1,0:T(8,128)(2,1)S(1)} async-done(((bf16[8,24,1152]{2,1,0:T(8,128)(2,1)}), bf16[8,24,1152]{2,1,0:T(8,128)(2,1)S(1)}, u32[]{:S(2)}, u32[]{:S(2)}) %all-to-all-start.8) | async-done | bytes 442400 | tf_op jit(solution)/shard_map/all_to_all | solution.py:22
  173.9 3.5 %all-to-all-start.9 = ((bf16[8,24,512]{2,1,0:T(8,128)(2,1)}), bf16[8,24,512]{2,1,0:T(8,128)(2,1)S(1)}, u32[]{:S(2)}, u32[]{:S(2)}) async-start(bf16[8,24,512]{2,1,0:T(8,128)(2,1)} %broadcast_in_dim.56), calls=%async_computation.9 | async-start | bytes 393216 | tf_op jit(solution)/shard_map/all_to_all | solution.py:22
  178.3 7.6 %all-to-all-done.9 = bf16[8,24,512]{2,1,0:T(8,128)(2,1)S(1)} async-done(((bf16[8,24,512]{2,1,0:T(8,128)(2,1)}), bf16[8,24,512]{2,1,0:T(8,128)(2,1)S(1)}, u32[]{:S(2)}, u32[]{:S(2)}) %all-to-all-start.9) | async-done | bytes 196640 | tf_op jit(solution)/shard_map/all_to_all | solution.py:22
  187.3 4.3 %all-to-all-start.10 = ((bf16[32,8,1024]{2,1,0:T(8,128)(2,1)}), bf16[32,8,1024]{2,1,0:T(8,128)(2,1)S(1)}, u32[]{:S(2)}, u32[]{:S(2)}) async-start(bf16[32,8,1024]{2,1,0:T(8,128)(2,1)} %fusion), calls=%async_computation.10 | async-start | bytes 1048576 | tf_op jit(solution)/shard_map/all_to_all | solution.py:22
  191.6 12.6 %all-to-all-done.10 = bf16[32,8,1024]{2,1,0:T(8,128)(2,1)S(1)} async-done(((bf16[32,8,1024]{2,1,0:T(8,128)(2,1)}), bf16[32,8,1024]{2,1,0:T(8,128)(2,1)S(1)}, u32[]{:S(2)}, u32[]{:S(2)}) %all-to-all-start.10) | async-done | bytes 524320 | tf_op jit(solution)/shard_map/all_to_all | solution.py:22
  204.5 11.9 %collective-permute-start.4 = (bf16[8,1024]{1,0:T(8,128)(2,1)S(1)}, bf16[8,1024]{1,0:T(8,128)(2,1)S(1)}, u32[]{:S(2)}, u32[]{:S(2)}) collective-permute-start(bf16[8,1024]{1,0:T(8,128)(2,1)S(1)} %get-tuple-element.45), channel_id=1, source_target_pairs={{0,256},{256,0},{1,257},{257,1},{2,258},{258,2},{3,259},{259,3},{4... | collective-permute-start | bytes 49160 | tf_op jit(solution)/shard_map/ppermute | solution.py:31
  (119 shorter events, 28.5 us)
Async XLA Ops:
  0.0 56.0 %copy-start = (bf16[256,1024]{1,0:T(8,128)(2,1)S(1)}, bf16[256,1024]{1,0:T(8,128)(2,1)}, u32[]{:S(2)}) copy-start(bf16[256,1024]{1,0:T(8,128)(2,1)} %param.17) | copy-start | bytes 1572868
  3.1 9.8 %copy-start.9 = (bf16[1024]{0:T(1024)(128)(2,1)S(1)}, bf16[1024]{0:T(1024)(128)(2,1)}, u32[]{:S(2)}) copy-start(bf16[1024]{0:T(1024)(128)(2,1)} %param.15) | copy-start | bytes 6148
  3.1 9.8 %copy-start.1 = (bf16[1024,256]{1,0:T(8,128)(2,1)S(1)}, bf16[1024,256]{1,0:T(8,128)(2,1)}, u32[]{:S(2)}) copy-start(bf16[1024,256]{1,0:T(8,128)(2,1)} %param.16) | copy-start | bytes 1572868
  3.1 25.8 %all-to-all-start = ((bf16[32,8,1024]{2,1,0:T(8,128)(2,1)}), bf16[32,8,1024]{2,1,0:T(8,128)(2,1)S(1)}, u32[]{:S(2)}, u32[]{:S(2)}) async-start(bf16[32,8,1024]{2,1,0:T(8,128)(2,1)} %broadcast_in_dim.46), calls=%async_computation | async-start | bytes 1048576 | tf_op jit(solution)/shard_map/all_to_all | solution.py:22
  30.8 16.3 %copy-start.2 = (bf16[1,1024,512]{2,1,0:T(8,128)(2,1)S(1)}, bf16[1,1024,512]{2,1,0:T(8,128)(2,1)}, u32[]{:S(2)}) copy-start(bf16[1,1024,512]{2,1,0:T(8,128)(2,1)} %param.19) | copy-start | bytes 3145732
  32.0 10.2 %copy-start.10 = (bf16[1,1024]{1,0:T(2,128)(2,1)S(1)}, bf16[1,1024]{1,0:T(2,128)(2,1)}, u32[]{:S(2)}) copy-start(bf16[1,1024]{1,0:T(2,128)(2,1)} %param.18) | copy-start | bytes 6148
  32.0 23.6 %all-to-all-start.1 = ((bf16[8,112,256]{2,1,0:T(8,128)(2,1)}), bf16[8,112,256]{2,1,0:T(8,128)(2,1)S(1)}, u32[]{:S(2)}, u32[]{:S(2)}) async-start(bf16[8,112,256]{2,1,0:T(8,128)(2,1)} %broadcast_in_dim.52), calls=%async_computation.1 | async-start | bytes 917504 | tf_op jit(solution)/shard_map/all_to_all | solution.py:22
  42.1 11.3 %collective-permute-start = (bf16[1,1024]{1,0:T(2,128)(2,1)S(1)}, bf16[1,1024]{1,0:T(2,128)(2,1)S(1)}, u32[]{:S(2)}, u32[]{:S(2)}) collective-permute-start(bf16[1,1024]{1,0:T(2,128)(2,1)S(1)} %copy-done.10), channel_id=1, source_target_pairs={{0,256},{256,0},{1,257},{257,1},{2,258},{258,2},{3,259},{259,3},{4... | collective-permute-start | bytes 6152 | tf_op jit(solution)/shard_map/ppermute | solution.py:31
  47.2 18.7 %collective-permute-start.1 = (bf16[1024,512]{1,0:T(8,128)(2,1)S(1)}, bf16[1024,512]{1,0:T(8,128)(2,1)}, u32[]{:S(2)}, u32[]{:S(2)}) collective-permute-start(bf16[1024,512]{1,0:T(8,128)(2,1)S(1)} %bitcast.94), channel_id=1, source_target_pairs={{0,256},{256,0},{1,257},{257,1},{2,258},{258,2},{3,259},{259,3},{4... | collective-permute-start | bytes 3145736 | tf_op jit(solution)/shard_map/ppermute | solution.py:31
  49.1 31.7 %collective-permute-start.2 = (bf16[1024,512]{1,0:T(8,128)(2,1)}, bf16[1024,512]{1,0:T(8,128)(2,1)S(1)}, u32[]{:S(2)}, u32[]{:S(2)}) collective-permute-start(bf16[1024,512]{1,0:T(8,128)(2,1)} %bitcast.2), channel_id=1, source_target_pairs={{0,256},{256,0},{1,257},{257,1},{2,258},{258,2},{3,259},{259,3},{4... | collective-permute-start | bytes 3145736 | tf_op jit(solution)/shard_map/ppermute | solution.py:31
  51.5 32.1 %collective-permute-start.3 = (bf16[512,1024]{1,0:T(8,128)(2,1)}, bf16[512,1024]{1,0:T(8,128)(2,1)}, u32[]{:S(2)}, u32[]{:S(2)}) collective-permute-start(bf16[512,1024]{1,0:T(8,128)(2,1)} %bitcast.3), channel_id=1, source_target_pairs={{0,256},{256,0},{1,257},{257,1},{2,258},{258,2},{3,259},{259,3},{4... | collective-permute-start | bytes 3145736 | tf_op jit(solution)/shard_map/ppermute | solution.py:31
  57.1 8.6 %copy-start.7 = (bf16[128,96]{0,1:T(8,128)(2,1)S(1)}, bf16[128,96]{0,1:T(8,128)(2,1)}, u32[]{:S(2)}) copy-start(bf16[128,96]{0,1:T(8,128)(2,1)} %fusion.4) | copy-start | bytes 73732
  57.1 18.4 %all-to-all-start.2 = ((bf16[32,24,128]{2,1,0:T(8,128)(2,1)}), bf16[32,24,128]{2,1,0:T(8,128)(2,1)S(1)}, u32[]{:S(2)}, u32[]{:S(2)}) async-start(bf16[32,24,128]{2,1,0:T(8,128)(2,1)} %bitcast.13), calls=%async_computation.2 | async-start | bytes 393216 | tf_op jit(solution)/shard_map/all_to_all | solution.py:22
  76.2 14.3 %all-to-all-start.3 = ((bf16[32,24,128]{2,1,0:T(8,128)(2,1)}), bf16[32,24,128]{2,1,0:T(8,128)(2,1)S(1)}, u32[]{:S(2)}, u32[]{:S(2)}) async-start(bf16[32,24,128]{2,1,0:T(8,128)(2,1)} %broadcast_in_dim.53), calls=%async_computation.3 | async-start | bytes 393216 | tf_op jit(solution)/shard_map/all_to_all | solution.py:22
  90.8 1.7 copy-start.4
  121.2 16.9 %all-to-all-start.6 = ((bf16[32,48,128]{2,1,0:T(8,128)(2,1)}), bf16[32,48,128]{2,1,0:T(8,128)(2,1)S(1)}, u32[]{:S(2)}, u32[]{:S(2)}) async-start(bf16[32,48,128]{2,1,0:T(8,128)(2,1)} %bitcast.26), calls=%async_computation.6 | async-start | bytes 786432 | tf_op jit(solution)/shard_map/all_to_all | solution.py:22
  139.0 15.7 %all-to-all-start.7 = ((bf16[32,48,128]{2,1,0:T(8,128)(2,1)}), bf16[32,48,128]{2,1,0:T(8,128)(2,1)S(1)}, u32[]{:S(2)}, u32[]{:S(2)}) async-start(bf16[32,48,128]{2,1,0:T(8,128)(2,1)} %broadcast_in_dim.55), calls=%async_computation.7 | async-start | bytes 786432 | tf_op jit(solution)/shard_map/all_to_all | solution.py:22
  154.8 2.1 copy-start.3
  158.0 3.6 %copy-start.11 = (s32[1,32]{1,0:T(1,128)S(1)}, s32[1,32]{1,0:T(1,128)}, u32[]{:S(2)}) copy-start(s32[1,32]{1,0:T(1,128)} %param.14) | copy-start | bytes 388
  158.0 14.9 %all-to-all-start.8 = ((bf16[8,24,1152]{2,1,0:T(8,128)(2,1)}), bf16[8,24,1152]{2,1,0:T(8,128)(2,1)S(1)}, u32[]{:S(2)}, u32[]{:S(2)}) async-start(bf16[8,24,1152]{2,1,0:T(8,128)(2,1)} %bitcast.33), calls=%async_computation.8 | async-start | bytes 884736 | tf_op jit(solution)/shard_map/all_to_all | solution.py:22
  173.9 3.5 %copy-start.8 = (bf16[128,96]{0,1:T(8,128)(2,1)S(1)}, bf16[128,96]{0,1:T(8,128)(2,1)}, u32[]{:S(2)}) copy-start(bf16[128,96]{0,1:T(8,128)(2,1)} %fusion.4) | copy-start | bytes 73732
  173.9 12.1 %all-to-all-start.9 = ((bf16[8,24,512]{2,1,0:T(8,128)(2,1)}), bf16[8,24,512]{2,1,0:T(8,128)(2,1)S(1)}, u32[]{:S(2)}, u32[]{:S(2)}) async-start(bf16[8,24,512]{2,1,0:T(8,128)(2,1)} %broadcast_in_dim.56), calls=%async_computation.9 | async-start | bytes 393216 | tf_op jit(solution)/shard_map/all_to_all | solution.py:22
  187.3 16.8 %all-to-all-start.10 = ((bf16[32,8,1024]{2,1,0:T(8,128)(2,1)}), bf16[32,8,1024]{2,1,0:T(8,128)(2,1)S(1)}, u32[]{:S(2)}, u32[]{:S(2)}) async-start(bf16[32,8,1024]{2,1,0:T(8,128)(2,1)} %fusion), calls=%async_computation.10 | async-start | bytes 1048576 | tf_op jit(solution)/shard_map/all_to_all | solution.py:22
  204.5 12.7 %collective-permute-start.4 = (bf16[8,1024]{1,0:T(8,128)(2,1)S(1)}, bf16[8,1024]{1,0:T(8,128)(2,1)S(1)}, u32[]{:S(2)}, u32[]{:S(2)}) collective-permute-start(bf16[8,1024]{1,0:T(8,128)(2,1)S(1)} %get-tuple-element.45), channel_id=1, source_target_pairs={{0,256},{256,0},{1,257},{257,1},{2,258},{258,2},{3,259},{259,3},{4... | collective-permute-start | bytes 49160 | tf_op jit(solution)/shard_map/ppermute | solution.py:31
  (2 other events, 1.3 us)

commit v4 on v3

--- a/solution.py
+++ b/solution.py
@@ -168,14 +168,14 @@
     own = (norm_gain, gate_w[0], up_w[0], down_w[0])
     own, copies = lax.optimization_barrier((own, copies))
     other = tuple(swap(array) for array in own)
+    everyone = exchange(copies, "dp")
+    gathered = everyone[:, :IMG].reshape(dp * IMG, width)
+    replies = everyone[:, IMG:].reshape(dp * LMAX, width)
+    gathered, other = lax.optimization_barrier((gathered, other))
     layer0 = [jnp.where(first, a, b) for a, b in zip(own, other)]
     layer1 = [jnp.where(first, b, a) for a, b in zip(own, other)]
     layer0, layer1 = lax.optimization_barrier((layer0, layer1))
     layer0[0], layer1[0] = layer0[0][0], layer1[0][0]
-
-    everyone = exchange(copies, "dp")
-    gathered = everyone[:, :IMG].reshape(dp * IMG, width)
-    replies = everyone[:, IMG:].reshape(dp * LMAX, width)
 
     index = jnp.arange(dp * IMG, dtype=jnp.int32)
     place_image = placement(gathered, index, img_live)
@@ -200,17 +200,23 @@
     )
     owned = lax.dynamic_slice_in_dim(ordering, place * SLOT, SLOT, 0)
 
-    inner = layer_hidden(rows, *layer0[:3])
-    blocks = to_tiles(dot(inner, layer0[3]).astype(BF)).reshape(dp, -1, LANES)
-    share = blocks.shape[1]
+    gain0, gain1 = layer0[0].astype(F32), layer1[0].astype(F32)
+    rows, ordering, owned, layer0, layer1, gain0, gain1 = lax.optimization_barrier(
+        (rows, ordering, owned, layer0[1:], layer1[1:], gain0, gain1)
+    )
+    inner = layer_hidden(rows, gain0, *layer0[:2])
+    blocks = to_tiles(dot(inner, layer0[2]).astype(BF)).reshape(dp, -1, LANES)
+    total, rows = lax.optimization_barrier((exchange(blocks, "dp"), rows))
+    share = total.shape[1]
     kept_tiles = lax.dynamic_slice_in_dim(to_tiles(rows), place * share, share, 0)
-    next_tiles = (kept_tiles.astype(F32) + summed(blocks)).astype(BF)
+    next_tiles = (kept_tiles.astype(F32) + jnp.sum(total.astype(F32), axis=0)).astype(BF)
     rows = from_tiles(spread(next_tiles, "dp"), width)
 
     slot_early = dot(owned, rows).astype(BF)
-    inner = layer_hidden(rows, *layer1[:3])
+    slot_early, rows = lax.optimization_barrier((slot_early, rows))
+    inner = layer_hidden(rows, gain1, *layer1[:2])
     inner = dot(ordering, inner).astype(BF)
-    blocks = dot(inner, layer1[3]).astype(BF).reshape(dp, SLOT, width)
+    blocks = dot(inner, layer1[2]).astype(BF).reshape(dp, SLOT, width)
     slot_late = (slot_early.astype(F32) + summed(blocks)).astype(BF)
 
     came = swap(jnp.where(first, slot_late, slot_early))

time: 219 us -> 212 us (0.968)
  blocking collectives: 26.8 us -> 82.6 us
  waiting for transfers between devices: 82.6 us -> 40.8 us
  starting transfers between devices: 77.3 us -> 60.7 us
  local copies, waits for them, and re-layouts: 7.33 us -> 4.52 us
  matrix products: 10.4 us -> 7.71 us
    all_to_all x2 -> x6, blocking collectives: 26.8 us -> 82.6 us  [exchange(): return lax.all_to_all(blocks, axis, 0, 0, tiled=True)]
    all_to_all x9 -> x5, waiting for transfers between devices: 81.8 us -> 40 us  [exchange(): return lax.all_to_all(blocks, axis, 0, 0, tiled=True)]
    all_to_all x9 -> x5, starting transfers between devices: 54.1 us -> 38 us  [exchange(): return lax.all_to_all(blocks, axis, 0, 0, tiled=True)]
    dot_general x14, matrix products: 9.94 us -> 7.22 us  [dot(): return jnp.dot(a, b, preferred_element_type=F32)]
  transfers between devices with their start and end apart: 14 -> 10, of which waited for: 9 -> 6; matrix products, arithmetic and copies ran while one was open for 6% -> 5% of each run, Pallas kernels for 0% -> 0%
where the time goes in v4:
time: 212 us; the launch traced here: 211 us
  blocking collectives  82.6 us (39%)
  starting transfers between devices  60.7 us (29%)
  waiting for transfers between devices  40.8 us (19%)
  other arithmetic  12.6 us (6%)
  matrix products  7.71 us (4%)
  local copies, waits for them, and re-layouts  4.52 us (2%)
    all_to_all x6, blocking collectives, exchange(): return lax.all_to_all(blocks, axis, 0, 0, tiled=True)  82.6 us
    all_to_all x5, waiting for transfers between devices, exchange(): return lax.all_to_all(blocks, axis, 0, 0, tiled=True)  40 us
    all_to_all x5, starting transfers between devices, exchange(): return lax.all_to_all(blocks, axis, 0, 0, tiled=True)  38 us
    ppermute x5, starting transfers between devices, swap(): return lax.ppermute(block, 'section', [(0, 1), (1, 0)])  22.7 us
    dot_general x14, matrix products, dot(): return jnp.dot(a, b, preferred_element_type=F32)  7.22 us
    select_n x4, other arithmetic, per_device(): layer1 = [jnp.where(first, b, a) for a, b in zip(own, other)]  7.14 us
  transfers between devices with their start and end apart: 10, of which 6 were waited for; matrix products, arithmetic and copies ran while one was open for 5% of the time, Pallas kernels for 0%

profile of v4, /device:TPU:9, one launch (start us, length us, event | category | flops | bytes accessed | tf_op | source)
XLA Modules:
  0.0 211.0 jit_solution(1245113654207554217)
XLA Ops:
  3.2 9.7 %all-to-all-start = ((bf16[32,8,1024]{2,1,0:T(8,128)(2,1)}), bf16[32,8,1024]{2,1,0:T(8,128)(2,1)S(1)}, u32[]{:S(2)}, u32[]{:S(2)}) async-start(bf16[32,8,1024]{2,1,0:T(8,128)(2,1)} %broadcast_in_dim.46), calls=%async_computation | async-start | bytes 1048576 | tf_op jit(solution)/shard_map/all_to_all | solution.py:22
  13.0 3.1 %collective-permute-start = (bf16[1,1024]{1,0:T(2,128)(2,1)S(1)}, bf16[1,1024]{1,0:T(2,128)(2,1)S(1)}, u32[]{:S(2)}, u32[]{:S(2)}) collective-permute-start(bf16[1,1024]{1,0:T(2,128)(2,1)S(1)} %copy-done.12), channel_id=1, source_target_pairs={{0,256},{256,0},{1,257},{257,1},{2,258},{258,2},{3,259},{259,3},{4... | collective-permute-start | bytes 6152 | tf_op jit(solution)/shard_map/ppermute | solution.py:31
  16.1 1.9 collective-permute-start.1
  18.1 2.4 %collective-permute-start.2 = (bf16[1024,512]{1,0:T(8,128)(2,1)}, bf16[1024,512]{1,0:T(8,128)(2,1)}, u32[]{:S(2)}, u32[]{:S(2)}) collective-permute-start(bf16[1024,512]{1,0:T(8,128)(2,1)} %bitcast.97), channel_id=1, source_target_pairs={{0,256},{256,0},{1,257},{257,1},{2,258},{258,2},{3,259},{259,3},{4... | collective-permute-start | bytes 3145736 | tf_op jit(solution)/shard_map/ppermute | solution.py:31
  20.5 1.9 collective-permute-start.3
  23.1 5.9 %all-to-all-done = bf16[32,8,1024]{2,1,0:T(8,128)(2,1)S(1)} async-done(((bf16[32,8,1024]{2,1,0:T(8,128)(2,1)}), bf16[32,8,1024]{2,1,0:T(8,128)(2,1)S(1)}, u32[]{:S(2)}, u32[]{:S(2)}) %all-to-all-start) | async-done | bytes 524320 | tf_op jit(solution)/shard_map/all_to_all | solution.py:22
  31.8 10.0 %all-to-all-start.1 = ((bf16[8,112,256]{2,1,0:T(8,128)(2,1)}), bf16[8,112,256]{2,1,0:T(8,128)(2,1)S(1)}, u32[]{:S(2)}, u32[]{:S(2)}) async-start(bf16[8,112,256]{2,1,0:T(8,128)(2,1)} %broadcast_in_dim.50), calls=%async_computation.1 | async-start | bytes 917504 | tf_op jit(solution)/shard_map/all_to_all | solution.py:22
  42.0 2.8 %broadcast_select_fusion.3 = (bf16[1024,512]{1,0:T(8,128)(2,1)}, bf16[1024,512]{1,0:T(8,128)(2,1)}) fusion(bf16[1024,512]{1,0:T(8,128)(2,1)} %collective-permute-done.1, bf16[1024,512]{1,0:T(8,128)(2,1)S(1)} %bitcast.96, pred[]{:T(512)S(6)} %eq.35), kind=kLoop, calls=%fused_computation.25 | loop fusion | flops 1048576 | bytes 4194305 | tf_op jit(solution)/shard_map/jit(_where)/select_n | solution.py:176
  44.8 2.7 %broadcast_select_fusion.2 = (bf16[1024,512]{1,0:T(8,128)(2,1)}, bf16[1024,512]{1,0:T(8,128)(2,1)}) fusion(bf16[1024,512]{1,0:T(8,128)(2,1)} %collective-permute-done.2, bf16[1024,512]{1,0:T(8,128)(2,1)S(1)} %bitcast.98, pred[]{:T(512)S(6)} %eq.35), kind=kLoop, calls=%fused_computation.24 | loop fusion | flops 1048576 | bytes 4194305 | tf_op jit(solution)/shard_map/jit(_where)/select_n | solution.py:176
  47.4 6.8 %all-to-all-done.1 = bf16[8,112,256]{2,1,0:T(8,128)(2,1)S(1)} async-done(((bf16[8,112,256]{2,1,0:T(8,128)(2,1)}), bf16[8,112,256]{2,1,0:T(8,128)(2,1)S(1)}, u32[]{:S(2)}, u32[]{:S(2)}) %all-to-all-start.1) | async-done | bytes 458784 | tf_op jit(solution)/shard_map/all_to_all | solution.py:22
  55.9 9.4 %all-to-all-start.2 = ((bf16[32,24,128]{2,1,0:T(8,128)(2,1)}), bf16[32,24,128]{2,1,0:T(8,128)(2,1)S(1)}, u32[]{:S(2)}, u32[]{:S(2)}) async-start(bf16[32,24,128]{2,1,0:T(8,128)(2,1)} %bitcast.12), calls=%async_computation.2 | async-start | bytes 393216 | tf_op jit(solution)/shard_map/all_to_all | solution.py:22
  68.1 6.9 %all-to-all-done.2 = bf16[32,24,128]{2,1,0:T(8,128)(2,1)S(1)} async-done(((bf16[32,24,128]{2,1,0:T(8,128)(2,1)}), bf16[32,24,128]{2,1,0:T(8,128)(2,1)S(1)}, u32[]{:S(2)}, u32[]{:S(2)}) %all-to-all-start.2) | async-done | bytes 196640 | tf_op jit(solution)/shard_map/all_to_all | solution.py:22
  75.8 4.6 %all-to-all-start.3 = ((bf16[32,24,128]{2,1,0:T(8,128)(2,1)}), bf16[32,24,128]{2,1,0:T(8,128)(2,1)S(1)}, u32[]{:S(2)}, u32[]{:S(2)}) async-start(bf16[32,24,128]{2,1,0:T(8,128)(2,1)} %broadcast_in_dim.51), calls=%async_computation.3 | async-start | bytes 393216 | tf_op jit(solution)/shard_map/all_to_all | solution.py:22
  81.3 8.8 %all-to-all-done.3 = bf16[32,24,128]{2,1,0:T(8,128)(2,1)S(1)} async-done(((bf16[32,24,128]{2,1,0:T(8,128)(2,1)}), bf16[32,24,128]{2,1,0:T(8,128)(2,1)S(1)}, u32[]{:S(2)}, u32[]{:S(2)}) %all-to-all-start.3) | async-done | bytes 196640 | tf_op jit(solution)/shard_map/all_to_all | solution.py:22
  91.0 1.7 convolution_convert_fusion.6
  93.1 14.3 %all_to_all.55 = bf16[8,24,1152]{2,1,0:T(8,128)(2,1)S(1)} all-to-all(bf16[8,24,1152]{2,1,0:T(8,128)(2,1)S(1)} %bitcast.92), channel_id=1, replica_groups=mesh['section'=2,'dp'=32,'mp'=8] {'mp'}, dimensions={0} | all-to-all | bytes 884736 | tf_op jit(solution)/shard_map/all_to_all | solution.py:22
  107.7 11.9 %all_to_all.56 = bf16[8,24,512]{2,1,0:T(8,128)(2,1)S(1)} all-to-all(bf16[8,24,512]{2,1,0:T(8,128)(2,1)S(1)} %broadcast_in_dim.54), channel_id=1, replica_groups=mesh['section'=2,'dp'=32,'mp'=8] {'mp'}, dimensions={0} | all-to-all | bytes 393216 | tf_op jit(solution)/shard_map/all_to_all | solution.py:22
  120.7 4.3 %all-to-all-start.6 = ((bf16[32,48,128]{2,1,0:T(8,128)(2,1)}), bf16[32,48,128]{2,1,0:T(8,128)(2,1)S(1)}, u32[]{:S(2)}, u32[]{:S(2)}) async-start(bf16[32,48,128]{2,1,0:T(8,128)(2,1)} %bitcast.24), calls=%async_computation.6 | async-start | bytes 786432 | tf_op jit(solution)/shard_map/all_to_all | solution.py:22
  125.0 11.6 %all-to-all-done.6 = bf16[32,48,128]{2,1,0:T(8,128)(2,1)S(1)} async-done(((bf16[32,48,128]{2,1,0:T(8,128)(2,1)}), bf16[32,48,128]{2,1,0:T(8,128)(2,1)S(1)}, u32[]{:S(2)}, u32[]{:S(2)}) %all-to-all-start.6) | async-done | bytes 393248 | tf_op jit(solution)/shard_map/all_to_all | solution.py:22
  136.8 15.4 %all_to_all.57 = bf16[32,48,128]{2,1,0:T(8,128)(2,1)S(1)} all-to-all(bf16[32,48,128]{2,1,0:T(8,128)(2,1)S(1)} %broadcast_in_dim.55), channel_id=1, replica_groups=mesh['section'=2,'dp'=32,'mp'=8] {'dp'}, dimensions={0} | all-to-all | bytes 786432 | tf_op jit(solution)/shard_map/all_to_all | solution.py:22
  154.3 13.7 %all_to_all.58 = bf16[8,24,1152]{2,1,0:T(8,128)(2,1)S(1)} all-to-all(bf16[8,24,1152]{2,1,0:T(8,128)(2,1)S(1)} %bitcast.93), channel_id=1, replica_groups=mesh['section'=2,'dp'=32,'mp'=8] {'mp'}, dimensions={0} | all-to-all | bytes 884736 | tf_op jit(solution)/shard_map/all_to_all | solution.py:22
  168.2 11.0 %all_to_all.59 = bf16[8,24,512]{2,1,0:T(8,128)(2,1)S(1)} all-to-all(bf16[8,24,512]{2,1,0:T(8,128)(2,1)S(1)} %broadcast_in_dim.56), channel_id=1, replica_groups=mesh['section'=2,'dp'=32,'mp'=8] {'mp'}, dimensions={0} | all-to-all | bytes 393216 | tf_op jit(solution)/shard_map/all_to_all | solution.py:22
  179.9 16.3 %all_to_all.60 = bf16[32,8,1024]{2,1,0:T(8,128)(2,1)S(1)} all-to-all(bf16[32,8,1024]{2,1,0:T(8,128)(2,1)S(1)} %fusion), channel_id=1, replica_groups=mesh['section'=2,'dp'=32,'mp'=8] {'dp'}, dimensions={0} | all-to-all | bytes 1048576 | tf_op jit(solution)/shard_map/all_to_all | solution.py:22
  196.3 13.3 %collective-permute-start.4 = (bf16[8,1024]{1,0:T(8,128)(2,1)S(1)}, bf16[8,1024]{1,0:T(8,128)(2,1)S(1)}, u32[]{:S(2)}, u32[]{:S(2)}) collective-permute-start(bf16[8,1024]{1,0:T(8,128)(2,1)S(1)} %get-tuple-element.85), channel_id=1, source_target_pairs={{0,256},{256,0},{1,257},{257,1},{2,258},{258,2},{3,259},{259,3},{4... | collective-permute-start | bytes 49160 | tf_op jit(solution)/shard_map/ppermute | solution.py:31
  (121 shorter events, 18.5 us)
Async XLA Ops:
  0.0 54.7 %copy-start = (bf16[256,1024]{1,0:T(8,128)(2,1)S(1)}, bf16[256,1024]{1,0:T(8,128)(2,1)}, u32[]{:S(2)}) copy-start(bf16[256,1024]{1,0:T(8,128)(2,1)} %param.17) | copy-start | bytes 1572868
  0.0 16.1 %copy-start.2 = (bf16[1,1024,512]{2,1,0:T(8,128)(2,1)S(1)}, bf16[1,1024,512]{2,1,0:T(8,128)(2,1)}, u32[]{:S(2)}) copy-start(bf16[1,1024,512]{2,1,0:T(8,128)(2,1)} %param.19) | copy-start | bytes 3145732
  3.2 9.8 %copy-start.12 = (bf16[1,1024]{1,0:T(2,128)(2,1)S(1)}, bf16[1,1024]{1,0:T(2,128)(2,1)}, u32[]{:S(2)}) copy-start(bf16[1,1024]{1,0:T(2,128)(2,1)} %param.18) | copy-start | bytes 6148
  3.2 19.2 %copy-start.13 = (s32[1,32]{1,0:T(1,128)S(1)}, s32[1,32]{1,0:T(1,128)}, u32[]{:S(2)}) copy-start(s32[1,32]{1,0:T(1,128)} %param.14) | copy-start | bytes 388
  3.2 19.2 %copy-start.8 = (bf16[1024]{0:T(1024)(128)(2,1)S(1)}, bf16[1024]{0:T(1024)(128)(2,1)}, u32[]{:S(2)}) copy-start(bf16[1024]{0:T(1024)(128)(2,1)} %param.15) | copy-start | bytes 6148
  3.2 19.4 %copy-start.1 = (bf16[1024,256]{1,0:T(8,128)(2,1)S(1)}, bf16[1024,256]{1,0:T(8,128)(2,1)}, u32[]{:S(2)}) copy-start(bf16[1024,256]{1,0:T(8,128)(2,1)} %param.16) | copy-start | bytes 1572868
  3.2 25.8 %all-to-all-start = ((bf16[32,8,1024]{2,1,0:T(8,128)(2,1)}), bf16[32,8,1024]{2,1,0:T(8,128)(2,1)S(1)}, u32[]{:S(2)}, u32[]{:S(2)}) async-start(bf16[32,8,1024]{2,1,0:T(8,128)(2,1)} %broadcast_in_dim.46), calls=%async_computation | async-start | bytes 1048576 | tf_op jit(solution)/shard_map/all_to_all | solution.py:22
  13.0 16.9 %collective-permute-start = (bf16[1,1024]{1,0:T(2,128)(2,1)S(1)}, bf16[1,1024]{1,0:T(2,128)(2,1)S(1)}, u32[]{:S(2)}, u32[]{:S(2)}) collective-permute-start(bf16[1,1024]{1,0:T(2,128)(2,1)S(1)} %copy-done.12), channel_id=1, source_target_pairs={{0,256},{256,0},{1,257},{257,1},{2,258},{258,2},{3,259},{259,3},{4... | collective-permute-start | bytes 6152 | tf_op jit(solution)/shard_map/ppermute | solution.py:31
  16.1 13.8 %collective-permute-start.1 = (bf16[1024,512]{1,0:T(8,128)(2,1)S(1)}, bf16[1024,512]{1,0:T(8,128)(2,1)}, u32[]{:S(2)}, u32[]{:S(2)}) collective-permute-start(bf16[1024,512]{1,0:T(8,128)(2,1)S(1)} %bitcast.95), channel_id=1, source_target_pairs={{0,256},{256,0},{1,257},{257,1},{2,258},{258,2},{3,259},{259,3},{4... | collective-permute-start | bytes 3145736 | tf_op jit(solution)/shard_map/ppermute | solution.py:31
  18.1 11.9 %collective-permute-start.2 = (bf16[1024,512]{1,0:T(8,128)(2,1)}, bf16[1024,512]{1,0:T(8,128)(2,1)}, u32[]{:S(2)}, u32[]{:S(2)}) collective-permute-start(bf16[1024,512]{1,0:T(8,128)(2,1)} %bitcast.97), channel_id=1, source_target_pairs={{0,256},{256,0},{1,257},{257,1},{2,258},{258,2},{3,259},{259,3},{4... | collective-permute-start | bytes 3145736 | tf_op jit(solution)/shard_map/ppermute | solution.py:31
  20.5 9.5 %collective-permute-start.3 = (bf16[512,1024]{1,0:T(8,128)(2,1)}, bf16[512,1024]{1,0:T(8,128)(2,1)}, u32[]{:S(2)}, u32[]{:S(2)}) collective-permute-start(bf16[512,1024]{1,0:T(8,128)(2,1)} %bitcast.99), channel_id=1, source_target_pairs={{0,256},{256,0},{1,257},{257,1},{2,258},{258,2},{3,259},{259,3},{4... | collective-permute-start | bytes 3145736 | tf_op jit(solution)/shard_map/ppermute | solution.py:31
  31.8 22.5 %all-to-all-start.1 = ((bf16[8,112,256]{2,1,0:T(8,128)(2,1)}), bf16[8,112,256]{2,1,0:T(8,128)(2,1)S(1)}, u32[]{:S(2)}, u32[]{:S(2)}) async-start(bf16[8,112,256]{2,1,0:T(8,128)(2,1)} %broadcast_in_dim.50), calls=%async_computation.1 | async-start | bytes 917504 | tf_op jit(solution)/shard_map/all_to_all | solution.py:22
  42.0 2.8 %copy-start.3 = (bf16[1,1024,512]{2,1,0:T(8,128)(2,1)S(1)}, bf16[1,1024,512]{2,1,0:T(8,128)(2,1)}, u32[]{:S(2)}) copy-start(bf16[1,1024,512]{2,1,0:T(8,128)(2,1)} %param.20) | copy-start | bytes 3145732
  55.9 19.2 %all-to-all-start.2 = ((bf16[32,24,128]{2,1,0:T(8,128)(2,1)}), bf16[32,24,128]{2,1,0:T(8,128)(2,1)S(1)}, u32[]{:S(2)}, u32[]{:S(2)}) async-start(bf16[32,24,128]{2,1,0:T(8,128)(2,1)} %bitcast.12), calls=%async_computation.2 | async-start | bytes 393216 | tf_op jit(solution)/shard_map/all_to_all | solution.py:22
  75.8 14.3 %all-to-all-start.3 = ((bf16[32,24,128]{2,1,0:T(8,128)(2,1)}), bf16[32,24,128]{2,1,0:T(8,128)(2,1)S(1)}, u32[]{:S(2)}, u32[]{:S(2)}) async-start(bf16[32,24,128]{2,1,0:T(8,128)(2,1)} %broadcast_in_dim.51), calls=%async_computation.3 | async-start | bytes 393216 | tf_op jit(solution)/shard_map/all_to_all | solution.py:22
  90.3 0.7 copy-start.10
  91.0 1.7 copy-start.6
  91.0 1.7 copy-start.11
  120.7 15.9 %all-to-all-start.6 = ((bf16[32,48,128]{2,1,0:T(8,128)(2,1)}), bf16[32,48,128]{2,1,0:T(8,128)(2,1)S(1)}, u32[]{:S(2)}, u32[]{:S(2)}) async-start(bf16[32,48,128]{2,1,0:T(8,128)(2,1)} %bitcast.24), calls=%async_computation.6 | async-start | bytes 786432 | tf_op jit(solution)/shard_map/all_to_all | solution.py:22
  136.7 15.9 %copy-start.5 = (bf16[1024,512]{1,0:T(8,128)(2,1)S(1)}, bf16[1024,512]{1,0:T(8,128)(2,1)}, u32[]{:S(2)}) copy-start(bf16[1024,512]{1,0:T(8,128)(2,1)} %get-tuple-element.69) | copy-start | bytes 3145732
  136.8 15.4 %copy-start.7 = (bf16[8,192]{0,1:T(8,128)(2,1)S(1)}, bf16[8,192]{0,1:T(8,128)(2,1)}, u32[]{:S(2)}) copy-start(bf16[8,192]{0,1:T(8,128)(2,1)} %fusion.33) | copy-start | bytes 9220
  152.2 0.7 copy-start.9
  152.4 1.2 copy-start.4
  196.3 14.1 %collective-permute-start.4 = (bf16[8,1024]{1,0:T(8,128)(2,1)S(1)}, bf16[8,1024]{1,0:T(8,128)(2,1)S(1)}, u32[]{:S(2)}, u32[]{:S(2)}) collective-permute-start(bf16[8,1024]{1,0:T(8,128)(2,1)S(1)} %get-tuple-element.85), channel_id=1, source_target_pairs={{0,256},{256,0},{1,257},{257,1},{2,258},{258,2},{3,259},{259,3},{4... | collective-permute-start | bytes 49160 | tf_op jit(solution)/shard_map/ppermute | solution.py:31

commit v5 on v4

--- a/solution.py
+++ b/solution.py
@@ -19,7 +19,11 @@
 
 
 def exchange(blocks, axis):
-    return lax.all_to_all(blocks, axis, 0, 0, tiled=True)
+    peers = lax.axis_size(axis)
+    order = None
+    if axis == "mp":
+        order = [list(range(0, peers, 2)) + list(range(1, peers, 2))]
+    return lax.all_to_all(blocks, axis, 0, 0, tiled=True, axis_index_groups=order)
 
 
 def spread(block, axis):
@@ -172,10 +176,9 @@
     gathered = everyone[:, :IMG].reshape(dp * IMG, width)
     replies = everyone[:, IMG:].reshape(dp * LMAX, width)
     gathered, other = lax.optimization_barrier((gathered, other))
-    layer0 = [jnp.where(first, a, b) for a, b in zip(own, other)]
-    layer1 = [jnp.where(first, b, a) for a, b in zip(own, other)]
+    layer0 = [jnp.where(first, a, b) for a, b in zip(own[1:], other[1:])]
+    layer1 = [jnp.where(first, b, a) for a, b in zip(own[1:], other[1:])]
     layer0, layer1 = lax.optimization_barrier((layer0, layer1))
-    layer0[0], layer1[0] = layer0[0][0], layer1[0][0]
 
     index = jnp.arange(dp * IMG, dtype=jnp.int32)
     place_image = placement(gathered, index, img_live)
@@ -200,20 +203,21 @@
     )
     owned = lax.dynamic_slice_in_dim(ordering, place * SLOT, SLOT, 0)
 
-    gain0, gain1 = layer0[0].astype(F32), layer1[0].astype(F32)
-    rows, ordering, owned, layer0, layer1, gain0, gain1 = lax.optimization_barrier(
-        (rows, ordering, owned, layer0[1:], layer1[1:], gain0, gain1)
-    )
+    rows, ordering, owned, layer0, layer1, gains = lax.optimization_barrier(
+        (rows, ordering, owned, layer0, layer1, (own[0], other[0]))
+    )
+    gain0 = jnp.where(first, *gains)[0].astype(F32)
     inner = layer_hidden(rows, gain0, *layer0[:2])
     blocks = to_tiles(dot(inner, layer0[2]).astype(BF)).reshape(dp, -1, LANES)
-    total, rows = lax.optimization_barrier((exchange(blocks, "dp"), rows))
+    total, rows, at = lax.optimization_barrier((exchange(blocks, "dp"), rows, place))
     share = total.shape[1]
-    kept_tiles = lax.dynamic_slice_in_dim(to_tiles(rows), place * share, share, 0)
+    kept_tiles = lax.dynamic_slice_in_dim(to_tiles(rows), at * share, share, 0)
     next_tiles = (kept_tiles.astype(F32) + jnp.sum(total.astype(F32), axis=0)).astype(BF)
     rows = from_tiles(spread(next_tiles, "dp"), width)
 
     slot_early = dot(owned, rows).astype(BF)
-    slot_early, rows = lax.optimization_barrier((slot_early, rows))
+    slot_early, rows, gains = lax.optimization_barrier((slot_early, rows, gains))
+    gain1 = jnp.where(first, *gains[::-1])[0].astype(F32)
     inner = layer_hidden(rows, gain1, *layer1[:2])
     inner = dot(ordering, inner).astype(BF)
     blocks = dot(inner, layer1[2]).astype(BF).reshape(dp, SLOT, width)

time: 212 us -> 207 us (0.976)
  blocking collectives: 82.6 us -> 95.9 us
  waiting for transfers between devices: 40.8 us -> 29.6 us
  starting transfers between devices: 60.7 us -> 54.3 us
    all_to_all x6 -> x7, blocking collectives: 82.6 us -> 95.9 us  [exchange(): lax.all_to_all(blocks, axis, 0, 0, tiled=True, axis_index_groups=order)]
    all_to_all x5 -> x4, waiting for transfers between devices: 40 us -> 28.7 us  [exchange(): lax.all_to_all(blocks, axis, 0, 0, tiled=True, axis_index_groups=order)]
    all_to_all x5 -> x4, starting transfers between devices: 38 us -> 29.3 us  [exchange(): lax.all_to_all(blocks, axis, 0, 0, tiled=True, axis_index_groups=order)]
    ppermute x5, starting transfers between devices: 22.7 us -> 25 us  [swap(): return lax.ppermute(block, 'section', [(0, 1), (1, 0)])]
    select_n x4 -> x3, other arithmetic: 7.14 us -> 6.87 us  [per_device(): layer1 = [jnp.where(first, b, a) for a, b in zip(own[1:], other[1:])]]
  transfers between devices with their start and end apart: 10 -> 9, of which waited for: 6 -> 5; matrix products, arithmetic and copies ran while one was open for 5% -> 5% of each run, Pallas kernels for 0% -> 0%
where the time goes in v5:
time: 207 us; the launch traced here: 205 us
  blocking collectives  95.9 us (46%)
  starting transfers between devices  54.3 us (26%)
  waiting for transfers between devices  29.6 us (14%)
  other arithmetic  11.8 us (6%)
  local copies, waits for them, and re-layouts  6.31 us (3%)
  matrix products  5.63 us (3%)
    all_to_all x7, blocking collectives, exchange(): lax.all_to_all(blocks, axis, 0, 0, tiled=True, axis_index_groups=order)  95.9 us
    all_to_all x4, starting transfers between devices, exchange(): lax.all_to_all(blocks, axis, 0, 0, tiled=True, axis_index_groups=order)  29.3 us
    all_to_all x4, waiting for transfers between devices, exchange(): lax.all_to_all(blocks, axis, 0, 0, tiled=True, axis_index_groups=order)  28.7 us
    ppermute x5, starting transfers between devices, swap(): return lax.ppermute(block, 'section', [(0, 1), (1, 0)])  25 us
    select_n x3, other arithmetic, per_device(): layer1 = [jnp.where(first, b, a) for a, b in zip(own[1:], other[1:])]  6.87 us
    dot_general x14, matrix products, dot(): return jnp.dot(a, b, preferred_element_type=F32)  5.14 us
  transfers between devices with their start and end apart: 9, of which 5 were waited for; matrix products, arithmetic and copies ran while one was open for 5% of the time, Pallas kernels for 0%

profile of v5, /device:TPU:9, one launch (start us, length us, event | category | flops | bytes accessed | tf_op | source)
XLA Modules:
  0.0 205.5 jit_solution(3979177488312217246)
XLA Ops:
  3.2 9.7 %all-to-all-start = ((bf16[32,8,1024]{2,1,0:T(8,128)(2,1)}), bf16[32,8,1024]{2,1,0:T(8,128)(2,1)S(1)}, u32[]{:S(2)}, u32[]{:S(2)}) async-start(bf16[32,8,1024]{2,1,0:T(8,128)(2,1)} %broadcast_in_dim.46), calls=%async_computation | async-start | bytes 1048576 | tf_op jit(solution)/shard_map/all_to_all | solution.py:26
  12.9 3.1 %collective-permute-start = (bf16[1,1024]{1,0:T(2,128)(2,1)S(1)}, bf16[1,1024]{1,0:T(2,128)(2,1)S(1)}, u32[]{:S(2)}, u32[]{:S(2)}) collective-permute-start(bf16[1,1024]{1,0:T(2,128)(2,1)S(1)} %copy-done.10), channel_id=1, source_target_pairs={{0,256},{256,0},{1,257},{257,1},{2,258},{258,2},{3,259},{259,3},{4... | collective-permute-start | bytes 6152 | tf_op jit(solution)/shard_map/ppermute | solution.py:35
  16.1 1.9 collective-permute-start.1
  18.0 2.4 %collective-permute-start.2 = (bf16[1024,512]{1,0:T(8,128)(2,1)}, bf16[1024,512]{1,0:T(8,128)(2,1)}, u32[]{:S(2)}, u32[]{:S(2)}) collective-permute-start(bf16[1024,512]{1,0:T(8,128)(2,1)} %bitcast.98), channel_id=1, source_target_pairs={{0,256},{256,0},{1,257},{257,1},{2,258},{258,2},{3,259},{259,3},{4... | collective-permute-start | bytes 3145736 | tf_op jit(solution)/shard_map/ppermute | solution.py:35
  20.5 1.9 collective-permute-start.3
  23.7 5.3 %all-to-all-done = bf16[32,8,1024]{2,1,0:T(8,128)(2,1)S(1)} async-done(((bf16[32,8,1024]{2,1,0:T(8,128)(2,1)}), bf16[32,8,1024]{2,1,0:T(8,128)(2,1)S(1)}, u32[]{:S(2)}, u32[]{:S(2)}) %all-to-all-start) | async-done | bytes 524320 | tf_op jit(solution)/shard_map/all_to_all | solution.py:26
  31.3 10.0 %all-to-all-start.1 = ((bf16[8,112,256]{2,1,0:T(8,128)(2,1)}), bf16[8,112,256]{2,1,0:T(8,128)(2,1)S(1)}, u32[]{:S(2)}, u32[]{:S(2)}) async-start(bf16[8,112,256]{2,1,0:T(8,128)(2,1)} %broadcast_in_dim.50), calls=%async_computation.1 | async-start | bytes 917504 | tf_op jit(solution)/shard_map/all_to_all | solution.py:26
  42.0 2.7 %broadcast_select_fusion.3 = (bf16[1024,512]{1,0:T(8,128)(2,1)}, bf16[1024,512]{1,0:T(8,128)(2,1)}) fusion(bf16[1024,512]{1,0:T(8,128)(2,1)} %collective-permute-done.1, bf16[1024,512]{1,0:T(8,128)(2,1)S(1)} %bitcast.97, pred[]{:T(512)S(6)} %eq.35), kind=kLoop, calls=%fused_computation.25 | loop fusion | flops 1048576 | bytes 4194305 | tf_op jit(solution)/shard_map/jit(_where)/select_n | solution.py:180
  44.7 8.9 %all-to-all-done.1 = bf16[8,112,256]{2,1,0:T(8,128)(2,1)S(1)} async-done(((bf16[8,112,256]{2,1,0:T(8,128)(2,1)}), bf16[8,112,256]{2,1,0:T(8,128)(2,1)S(1)}, u32[]{:S(2)}, u32[]{:S(2)}) %all-to-all-start.1) | async-done | bytes 458784 | tf_op jit(solution)/shard_map/all_to_all | solution.py:26
  54.0 1.2 convolution_convert_fusion.8
  55.2 5.8 %all-to-all-start.2 = ((bf16[32,24,128]{2,1,0:T(8,128)(2,1)}), bf16[32,24,128]{2,1,0:T(8,128)(2,1)S(1)}, u32[]{:S(2)}, u32[]{:S(2)}) async-start(bf16[32,24,128]{2,1,0:T(8,128)(2,1)} %bitcast.12), calls=%async_computation.2 | async-start | bytes 393216 | tf_op jit(solution)/shard_map/all_to_all | solution.py:26
  61.0 2.8 %broadcast_select_fusion.2 = (bf16[1024,512]{1,0:T(8,128)(2,1)}, bf16[1024,512]{1,0:T(8,128)(2,1)}) fusion(bf16[1024,512]{1,0:T(8,128)(2,1)} %collective-permute-done.2, bf16[1024,512]{1,0:T(8,128)(2,1)S(1)} %bitcast.99, pred[]{:T(512)S(6)} %eq.35), kind=kLoop, calls=%fused_computation.24 | loop fusion | flops 1048576 | bytes 4194305 | tf_op jit(solution)/shard_map/jit(_where)/select_n | solution.py:180
  63.8 1.4 broadcast_select_fusion
  65.2 5.7 %all-to-all-done.2 = bf16[32,24,128]{2,1,0:T(8,128)(2,1)S(1)} async-done(((bf16[32,24,128]{2,1,0:T(8,128)(2,1)}), bf16[32,24,128]{2,1,0:T(8,128)(2,1)S(1)}, u32[]{:S(2)}, u32[]{:S(2)}) %all-to-all-start.2) | async-done | bytes 196640 | tf_op jit(solution)/shard_map/all_to_all | solution.py:26
  71.7 3.7 %all-to-all-start.3 = ((bf16[32,24,128]{2,1,0:T(8,128)(2,1)}), bf16[32,24,128]{2,1,0:T(8,128)(2,1)S(1)}, u32[]{:S(2)}, u32[]{:S(2)}) async-start(bf16[32,24,128]{2,1,0:T(8,128)(2,1)} %broadcast_in_dim.51), calls=%async_computation.3 | async-start | bytes 393216 | tf_op jit(solution)/shard_map/all_to_all | solution.py:26
  76.2 8.9 %all-to-all-done.3 = bf16[32,24,128]{2,1,0:T(8,128)(2,1)S(1)} async-done(((bf16[32,24,128]{2,1,0:T(8,128)(2,1)}), bf16[32,24,128]{2,1,0:T(8,128)(2,1)S(1)}, u32[]{:S(2)}, u32[]{:S(2)}) %all-to-all-start.3) | async-done | bytes 196640 | tf_op jit(solution)/shard_map/all_to_all | solution.py:26
  88.6 14.8 %all_to_all.55 = bf16[8,24,1152]{2,1,0:T(8,128)(2,1)S(1)} all-to-all(bf16[8,24,1152]{2,1,0:T(8,128)(2,1)S(1)} %bitcast.92), channel_id=1, replica_groups={{0,2,4,6,1,3,5,7},{8,10,12,14,9,11,13,15},{16,18,20,22,17,19,21,23},{24..., dimensions={0} | all-to-all | bytes 884736 | tf_op jit(solution)/shard_map/all_to_all | solution.py:26
  103.7 10.1 %all_to_all.56 = bf16[8,24,512]{2,1,0:T(8,128)(2,1)S(1)} all-to-all(bf16[8,24,512]{2,1,0:T(8,128)(2,1)S(1)} %broadcast_in_dim.54), channel_id=1, replica_groups={{0,2,4,6,1,3,5,7},{8,10,12,14,9,11,13,15},{16,18,20,22,17,19,21,23},{24..., dimensions={0} | all-to-all | bytes 393216 | tf_op jit(solution)/shard_map/all_to_all | solution.py:26
  114.2 15.9 %all_to_all.57 = bf16[32,48,128]{2,1,0:T(8,128)(2,1)S(1)} all-to-all(bf16[32,48,128]{2,1,0:T(8,128)(2,1)S(1)} %bitcast.95), channel_id=1, replica_groups=mesh['section'=2,'dp'=32,'mp'=8] {'dp'}, dimensions={0} | all-to-all | bytes 786432 | tf_op jit(solution)/shard_map/all_to_all | solution.py:26
  130.2 15.3 %all_to_all.58 = bf16[32,48,128]{2,1,0:T(8,128)(2,1)S(1)} all-to-all(bf16[32,48,128]{2,1,0:T(8,128)(2,1)S(1)} %broadcast_in_dim.55), channel_id=1, replica_groups=mesh['section'=2,'dp'=32,'mp'=8] {'dp'}, dimensions={0} | all-to-all | bytes 786432 | tf_op jit(solution)/shard_map/all_to_all | solution.py:26
  147.5 12.8 %all_to_all.59 = bf16[8,24,1152]{2,1,0:T(8,128)(2,1)S(1)} all-to-all(bf16[8,24,1152]{2,1,0:T(8,128)(2,1)S(1)} %bitcast.93), channel_id=1, replica_groups={{0,2,4,6,1,3,5,7},{8,10,12,14,9,11,13,15},{16,18,20,22,17,19,21,23},{24..., dimensions={0} | all-to-all | bytes 884736 | tf_op jit(solution)/shard_map/all_to_all | solution.py:26
  160.6 10.8 %all_to_all.60 = bf16[8,24,512]{2,1,0:T(8,128)(2,1)S(1)} all-to-all(bf16[8,24,512]{2,1,0:T(8,128)(2,1)S(1)} %broadcast_in_dim.56), channel_id=1, replica_groups={{0,2,4,6,1,3,5,7},{8,10,12,14,9,11,13,15},{16,18,20,22,17,19,21,23},{24..., dimensions={0} | all-to-all | bytes 393216 | tf_op jit(solution)/shard_map/all_to_all | solution.py:26
  172.1 16.3 %all_to_all.61 = bf16[32,8,1024]{2,1,0:T(8,128)(2,1)S(1)} all-to-all(bf16[32,8,1024]{2,1,0:T(8,128)(2,1)S(1)} %fusion), channel_id=1, replica_groups=mesh['section'=2,'dp'=32,'mp'=8] {'dp'}, dimensions={0} | all-to-all | bytes 1048576 | tf_op jit(solution)/shard_map/all_to_all | solution.py:26
  188.5 15.6 %collective-permute-start.4 = (bf16[8,1024]{1,0:T(8,128)(2,1)S(1)}, bf16[8,1024]{1,0:T(8,128)(2,1)S(1)}, u32[]{:S(2)}, u32[]{:S(2)}) collective-permute-start(bf16[8,1024]{1,0:T(8,128)(2,1)S(1)} %get-tuple-element.87), channel_id=1, source_target_pairs={{0,256},{256,0},{1,257},{257,1},{2,258},{258,2},{3,259},{259,3},{4... | collective-permute-start | bytes 49160 | tf_op jit(solution)/shard_map/ppermute | solution.py:35
  (123 shorter events, 16.5 us)
Async XLA Ops:
  0.0 54.0 %copy-start = (bf16[256,1024]{1,0:T(8,128)(2,1)S(1)}, bf16[256,1024]{1,0:T(8,128)(2,1)}, u32[]{:S(2)}) copy-start(bf16[256,1024]{1,0:T(8,128)(2,1)} %param.17) | copy-start | bytes 1572868
  0.0 16.1 %copy-start.2 = (bf16[1,1024,512]{2,1,0:T(8,128)(2,1)S(1)}, bf16[1,1024,512]{2,1,0:T(8,128)(2,1)}, u32[]{:S(2)}) copy-start(bf16[1,1024,512]{2,1,0:T(8,128)(2,1)} %param.19) | copy-start | bytes 3145732
  3.2 9.8 %copy-start.10 = (bf16[1,1024]{1,0:T(2,128)(2,1)S(1)}, bf16[1,1024]{1,0:T(2,128)(2,1)}, u32[]{:S(2)}) copy-start(bf16[1,1024]{1,0:T(2,128)(2,1)} %param.18) | copy-start | bytes 6148
  3.2 19.2 %copy-start.14 = (bf16[1024]{0:T(1024)(128)(2,1)S(1)}, bf16[1024]{0:T(1024)(128)(2,1)}, u32[]{:S(2)}) copy-start(bf16[1024]{0:T(1024)(128)(2,1)} %param.15) | copy-start | bytes 6148
  3.2 19.2 %copy-start.1 = (bf16[1024,256]{1,0:T(8,128)(2,1)S(1)}, bf16[1024,256]{1,0:T(8,128)(2,1)}, u32[]{:S(2)}) copy-start(bf16[1024,256]{1,0:T(8,128)(2,1)} %param.16) | copy-start | bytes 1572868
  3.2 25.8 %all-to-all-start = ((bf16[32,8,1024]{2,1,0:T(8,128)(2,1)}), bf16[32,8,1024]{2,1,0:T(8,128)(2,1)S(1)}, u32[]{:S(2)}, u32[]{:S(2)}) async-start(bf16[32,8,1024]{2,1,0:T(8,128)(2,1)} %broadcast_in_dim.46), calls=%async_computation | async-start | bytes 1048576 | tf_op jit(solution)/shard_map/all_to_all | solution.py:26
  12.9 16.5 %collective-permute-start = (bf16[1,1024]{1,0:T(2,128)(2,1)S(1)}, bf16[1,1024]{1,0:T(2,128)(2,1)S(1)}, u32[]{:S(2)}, u32[]{:S(2)}) collective-permute-start(bf16[1,1024]{1,0:T(2,128)(2,1)S(1)} %copy-done.10), channel_id=1, source_target_pairs={{0,256},{256,0},{1,257},{257,1},{2,258},{258,2},{3,259},{259,3},{4... | collective-permute-start | bytes 6152 | tf_op jit(solution)/shard_map/ppermute | solution.py:35
  16.1 13.3 %collective-permute-start.1 = (bf16[1024,512]{1,0:T(8,128)(2,1)S(1)}, bf16[1024,512]{1,0:T(8,128)(2,1)}, u32[]{:S(2)}, u32[]{:S(2)}) collective-permute-start(bf16[1024,512]{1,0:T(8,128)(2,1)S(1)} %bitcast.96), channel_id=1, source_target_pairs={{0,256},{256,0},{1,257},{257,1},{2,258},{258,2},{3,259},{259,3},{4... | collective-permute-start | bytes 3145736 | tf_op jit(solution)/shard_map/ppermute | solution.py:35
  18.0 11.4 %collective-permute-start.2 = (bf16[1024,512]{1,0:T(8,128)(2,1)}, bf16[1024,512]{1,0:T(8,128)(2,1)}, u32[]{:S(2)}, u32[]{:S(2)}) collective-permute-start(bf16[1024,512]{1,0:T(8,128)(2,1)} %bitcast.98), channel_id=1, source_target_pairs={{0,256},{256,0},{1,257},{257,1},{2,258},{258,2},{3,259},{259,3},{4... | collective-permute-start | bytes 3145736 | tf_op jit(solution)/shard_map/ppermute | solution.py:35
  20.5 9.0 %collective-permute-start.3 = (bf16[512,1024]{1,0:T(8,128)(2,1)}, bf16[512,1024]{1,0:T(8,128)(2,1)}, u32[]{:S(2)}, u32[]{:S(2)}) collective-permute-start(bf16[512,1024]{1,0:T(8,128)(2,1)} %bitcast.100), channel_id=1, source_target_pairs={{0,256},{256,0},{1,257},{257,1},{2,258},{258,2},{3,259},{259,3},{4... | collective-permute-start | bytes 3145736 | tf_op jit(solution)/shard_map/ppermute | solution.py:35
  29.4 55.9 %copy-start.12 = (bf16[1,1024]{1,0:T(2,128)(2,1)}, bf16[1,1024]{1,0:T(2,128)(2,1)S(1)}, u32[]{:S(2)}) copy-start(bf16[1,1024]{1,0:T(2,128)(2,1)S(1)} %collective-permute-done) | copy-start | bytes 6148
  31.3 22.3 %all-to-all-start.1 = ((bf16[8,112,256]{2,1,0:T(8,128)(2,1)}), bf16[8,112,256]{2,1,0:T(8,128)(2,1)S(1)}, u32[]{:S(2)}, u32[]{:S(2)}) async-start(bf16[8,112,256]{2,1,0:T(8,128)(2,1)} %broadcast_in_dim.50), calls=%async_computation.1 | async-start | bytes 917504 | tf_op jit(solution)/shard_map/all_to_all | solution.py:26
  54.0 7.0 %copy-start.3 = (bf16[1,1024,512]{2,1,0:T(8,128)(2,1)S(1)}, bf16[1,1024,512]{2,1,0:T(8,128)(2,1)}, u32[]{:S(2)}) copy-start(bf16[1,1024,512]{2,1,0:T(8,128)(2,1)} %param.20) | copy-start | bytes 3145732
  55.2 15.7 %all-to-all-start.2 = ((bf16[32,24,128]{2,1,0:T(8,128)(2,1)}), bf16[32,24,128]{2,1,0:T(8,128)(2,1)S(1)}, u32[]{:S(2)}, u32[]{:S(2)}) async-start(bf16[32,24,128]{2,1,0:T(8,128)(2,1)} %bitcast.12), calls=%async_computation.2 | async-start | bytes 393216 | tf_op jit(solution)/shard_map/all_to_all | solution.py:26
  61.0 2.8 %copy-start.4 = (bf16[1,512,1024]{2,1,0:T(8,128)(2,1)S(1)}, bf16[1,512,1024]{2,1,0:T(8,128)(2,1)}, u32[]{:S(2)}) copy-start(bf16[1,512,1024]{2,1,0:T(8,128)(2,1)} %param.21) | copy-start | bytes 3145732
  71.7 13.4 %all-to-all-start.3 = ((bf16[32,24,128]{2,1,0:T(8,128)(2,1)}), bf16[32,24,128]{2,1,0:T(8,128)(2,1)S(1)}, u32[]{:S(2)}, u32[]{:S(2)}) async-start(bf16[32,24,128]{2,1,0:T(8,128)(2,1)} %broadcast_in_dim.51), calls=%async_computation.3 | async-start | bytes 393216 | tf_op jit(solution)/shard_map/all_to_all | solution.py:26
  85.1 1.2 copy-start.8
  85.1 1.6 copy-start.7
  130.1 16.1 %copy-start.6 = (bf16[1024,512]{1,0:T(8,128)(2,1)S(1)}, bf16[1024,512]{1,0:T(8,128)(2,1)}, u32[]{:S(2)}) copy-start(bf16[1024,512]{1,0:T(8,128)(2,1)} %get-tuple-element.71) | copy-start | bytes 3145732
  130.2 15.3 %copy-start.9 = (bf16[8,192]{0,1:T(8,128)(2,1)S(1)}, bf16[8,192]{0,1:T(8,128)(2,1)}, u32[]{:S(2)}) copy-start(bf16[8,192]{0,1:T(8,128)(2,1)} %fusion.33) | copy-start | bytes 9220
  145.5 0.7 copy-start.11
  145.5 0.7 copy-start.13
  145.7 1.2 copy-start.5
  188.5 16.4 %collective-permute-start.4 = (bf16[8,1024]{1,0:T(8,128)(2,1)S(1)}, bf16[8,1024]{1,0:T(8,128)(2,1)S(1)}, u32[]{:S(2)}, u32[]{:S(2)}) collective-permute-start(bf16[8,1024]{1,0:T(8,128)(2,1)S(1)} %get-tuple-element.87), channel_id=1, source_target_pairs={{0,256},{256,0},{1,257},{257,1},{2,258},{258,2},{3,259},{259,3},{4... | collective-permute-start | bytes 49160 | tf_op jit(solution)/shard_map/ppermute | solution.py:35
  (1 other events, 0.7 us)

commit v6 on v5

--- a/solution.py
+++ b/solution.py
@@ -22,7 +22,7 @@
     peers = lax.axis_size(axis)
     order = None
     if axis == "mp":
-        order = [list(range(0, peers, 2)) + list(range(1, peers, 2))]
+        order = [[0, 1, 4, 5, 2, 3, 6, 7]]
     return lax.all_to_all(blocks, axis, 0, 0, tiled=True, axis_index_groups=order)
 
 
@@ -113,9 +113,11 @@
 
 def layer_partial(rows, gain, w_gate, w_up):
     values = rows.astype(F32)
-    squares = jnp.sum(values * values, axis=1)
+    squares = jnp.sum(values * values, axis=1, keepdims=True)
     normed = (values * gain.astype(F32)).astype(BF)
-    stats = jnp.pad(jnp.stack(terms(squares, 2), axis=1), ((0, 0), (0, LANES - 2)))
+    coarse = lax.reduce_precision(squares, 8, 7)
+    lane = lax.broadcasted_iota(jnp.int32, (rows.shape[0], LANES), 1)
+    stats = jnp.where(lane == 0, coarse, jnp.where(lane == 1, squares - coarse, 0)).astype(BF)
     return jnp.concatenate(
         [dot(normed, w_gate).astype(BF), dot(normed, w_up).astype(BF), stats], axis=1
     )
@@ -184,7 +186,9 @@
     place_image = placement(gathered, index, img_live)
     image = pick(place_image, gathered)
     sent = projector_partial(image, proj_gain, proj_in)
+    sent, everyone = lax.optimization_barrier((sent, everyone))
     parts = spread(sent, "mp")
+    replies = everyone[:, IMG:].reshape(dp * LMAX, width)
     active = projector_active(parts, img_live, width)
     blocks = to_tiles(dot(active, proj_out).astype(BF))
     projected = summed(blocks.reshape(dp, -1, LANES)).astype(BF)

time: 207 us -> 206 us (level)
  waiting for transfers between devices: 29.6 us -> 26.6 us
  starting transfers between devices: 54.3 us -> 56.8 us
    all_to_all x4, waiting for transfers between devices: 28.7 us -> 25.8 us  [exchange(): lax.all_to_all(blocks, axis, 0, 0, tiled=True, axis_index_groups=order)]
where the time goes in v6:
time: 206 us; the launch traced here: 205 us
  blocking collectives  95.9 us (47%)
  starting transfers between devices  56.8 us (28%)
  waiting for transfers between devices  26.6 us (13%)
  other arithmetic  12.7 us (6%)
  matrix products  6.27 us (3%)
  local copies, waits for them, and re-layouts  4.45 us (2%)
    all_to_all x7, blocking collectives, exchange(): lax.all_to_all(blocks, axis, 0, 0, tiled=True, axis_index_groups=order)  95.9 us
    all_to_all x4, starting transfers between devices, exchange(): lax.all_to_all(blocks, axis, 0, 0, tiled=True, axis_index_groups=order)  31.1 us
    all_to_all x4, waiting for transfers between devices, exchange(): lax.all_to_all(blocks, axis, 0, 0, tiled=True, axis_index_groups=order)  25.8 us
    ppermute x5, starting transfers between devices, swap(): return lax.ppermute(block, 'section', [(0, 1), (1, 0)])  25.7 us
    select_n x3, other arithmetic, per_device(): layer1 = [jnp.where(first, b, a) for a, b in zip(own[1:], other[1:])]  7.15 us
    dot_general x14, matrix products, dot(): return jnp.dot(a, b, preferred_element_type=F32)  5.11 us
  transfers between devices with their start and end apart: 9, of which 5 were waited for; matrix products, arithmetic and copies ran while one was open for 5% of the time, Pallas kernels for 0%

profile of v6, /device:TPU:9, one launch (start us, length us, event | category | flops | bytes accessed | tf_op | source)
XLA Modules:
  0.0 204.8 jit_solution(7795435442554444753)
XLA Ops:
  3.2 9.7 %all-to-all-start = ((bf16[32,8,1024]{2,1,0:T(8,128)(2,1)}), bf16[32,8,1024]{2,1,0:T(8,128)(2,1)S(1)}, u32[]{:S(2)}, u32[]{:S(2)}) async-start(bf16[32,8,1024]{2,1,0:T(8,128)(2,1)} %broadcast_in_dim.77), calls=%async_computation | async-start | bytes 1048576 | tf_op jit(solution)/shard_map/all_to_all | solution.py:26
  13.0 3.1 %collective-permute-start = (bf16[1,1024]{1,0:T(2,128)(2,1)S(1)}, bf16[1,1024]{1,0:T(2,128)(2,1)S(1)}, u32[]{:S(2)}, u32[]{:S(2)}) collective-permute-start(bf16[1,1024]{1,0:T(2,128)(2,1)S(1)} %copy-done.10), channel_id=1, source_target_pairs={{0,256},{256,0},{1,257},{257,1},{2,258},{258,2},{3,259},{259,3},{4... | collective-permute-start | bytes 6152 | tf_op jit(solution)/shard_map/ppermute | solution.py:35
  16.1 1.9 collective-permute-start.1
  18.0 2.4 %collective-permute-start.2 = (bf16[1024,512]{1,0:T(8,128)(2,1)}, bf16[1024,512]{1,0:T(8,128)(2,1)}, u32[]{:S(2)}, u32[]{:S(2)}) collective-permute-start(bf16[1024,512]{1,0:T(8,128)(2,1)} %bitcast.96), channel_id=1, source_target_pairs={{0,256},{256,0},{1,257},{257,1},{2,258},{258,2},{3,259},{259,3},{4... | collective-permute-start | bytes 3145736 | tf_op jit(solution)/shard_map/ppermute | solution.py:35
  20.5 1.9 collective-permute-start.3
  23.1 5.9 %all-to-all-done = bf16[32,8,1024]{2,1,0:T(8,128)(2,1)S(1)} async-done(((bf16[32,8,1024]{2,1,0:T(8,128)(2,1)}), bf16[32,8,1024]{2,1,0:T(8,128)(2,1)S(1)}, u32[]{:S(2)}, u32[]{:S(2)}) %all-to-all-start) | async-done | bytes 524320 | tf_op jit(solution)/shard_map/all_to_all | solution.py:26
  31.3 10.0 %all-to-all-start.1 = ((bf16[8,112,256]{2,1,0:T(8,128)(2,1)}), bf16[8,112,256]{2,1,0:T(8,128)(2,1)S(1)}, u32[]{:S(2)}, u32[]{:S(2)}) async-start(bf16[8,112,256]{2,1,0:T(8,128)(2,1)} %broadcast_in_dim.135), calls=%async_computation.1 | async-start | bytes 917504 | tf_op jit(solution)/shard_map/all_to_all | solution.py:26
  41.9 2.8 %broadcast_select_fusion.3 = (bf16[1024,512]{1,0:T(8,128)(2,1)}, bf16[1024,512]{1,0:T(8,128)(2,1)}) fusion(bf16[1024,512]{1,0:T(8,128)(2,1)} %collective-permute-done.1, bf16[1024,512]{1,0:T(8,128)(2,1)S(1)} %bitcast.95, pred[]{:T(512)S(6)} %eq.49), kind=kLoop, calls=%fused_computation.25 | loop fusion | flops 1048576 | bytes 4194305 | tf_op jit(solution)/shard_map/jit(_where)/select_n | solution.py:182
  44.7 2.7 %broadcast_select_fusion.2 = (bf16[1024,512]{1,0:T(8,128)(2,1)}, bf16[1024,512]{1,0:T(8,128)(2,1)}) fusion(bf16[1024,512]{1,0:T(8,128)(2,1)} %collective-permute-done.2, bf16[1024,512]{1,0:T(8,128)(2,1)S(1)} %bitcast.97, pred[]{:T(512)S(6)} %eq.49), kind=kLoop, calls=%fused_computation.24 | loop fusion | flops 1048576 | bytes 4194305 | tf_op jit(solution)/shard_map/jit(_where)/select_n | solution.py:182
  47.3 4.1 %all-to-all-done.1 = bf16[8,112,256]{2,1,0:T(8,128)(2,1)S(1)} async-done(((bf16[8,112,256]{2,1,0:T(8,128)(2,1)}), bf16[8,112,256]{2,1,0:T(8,128)(2,1)S(1)}, u32[]{:S(2)}, u32[]{:S(2)}) %all-to-all-start.1) | async-done | bytes 458784 | tf_op jit(solution)/shard_map/all_to_all | solution.py:26
  51.9 1.1 convolution_convert_fusion.8
  53.0 7.4 %all-to-all-start.2 = ((bf16[32,24,128]{2,1,0:T(8,128)(2,1)}), bf16[32,24,128]{2,1,0:T(8,128)(2,1)S(1)}, u32[]{:S(2)}, u32[]{:S(2)}) async-start(bf16[32,24,128]{2,1,0:T(8,128)(2,1)} %bitcast.12), calls=%async_computation.2 | async-start | bytes 393216 | tf_op jit(solution)/shard_map/all_to_all | solution.py:26
  60.5 1.7 broadcast_select_fusion
  62.2 7.8 %all-to-all-done.2 = bf16[32,24,128]{2,1,0:T(8,128)(2,1)S(1)} async-done(((bf16[32,24,128]{2,1,0:T(8,128)(2,1)}), bf16[32,24,128]{2,1,0:T(8,128)(2,1)S(1)}, u32[]{:S(2)}, u32[]{:S(2)}) %all-to-all-start.2) | async-done | bytes 196640 | tf_op jit(solution)/shard_map/all_to_all | solution.py:26
  70.8 4.0 %all-to-all-start.3 = ((bf16[32,24,128]{2,1,0:T(8,128)(2,1)}), bf16[32,24,128]{2,1,0:T(8,128)(2,1)S(1)}, u32[]{:S(2)}, u32[]{:S(2)}) async-start(bf16[32,24,128]{2,1,0:T(8,128)(2,1)} %broadcast_in_dim.136), calls=%async_computation.3 | async-start | bytes 393216 | tf_op jit(solution)/shard_map/all_to_all | solution.py:26
  76.3 8.0 %all-to-all-done.3 = bf16[32,24,128]{2,1,0:T(8,128)(2,1)S(1)} async-done(((bf16[32,24,128]{2,1,0:T(8,128)(2,1)}), bf16[32,24,128]{2,1,0:T(8,128)(2,1)S(1)}, u32[]{:S(2)}, u32[]{:S(2)}) %all-to-all-start.3) | async-done | bytes 196640 | tf_op jit(solution)/shard_map/all_to_all | solution.py:26
  87.3 15.2 %all_to_all.55 = bf16[8,24,1152]{2,1,0:T(8,128)(2,1)S(1)} all-to-all(bf16[8,24,1152]{2,1,0:T(8,128)(2,1)S(1)} %bitcast.90), channel_id=1, replica_groups={{0,1,4,5,2,3,6,7},{8,9,12,13,10,11,14,15},{16,17,20,21,18,19,22,23},{24..., dimensions={0} | all-to-all | bytes 884736 | tf_op jit(solution)/shard_map/all_to_all | solution.py:26
  102.8 10.1 %all_to_all.56 = bf16[8,24,512]{2,1,0:T(8,128)(2,1)S(1)} all-to-all(bf16[8,24,512]{2,1,0:T(8,128)(2,1)S(1)} %broadcast_in_dim.142), channel_id=1, replica_groups={{0,1,4,5,2,3,6,7},{8,9,12,13,10,11,14,15},{16,17,20,21,18,19,22,23},{24..., dimensions={0} | all-to-all | bytes 393216 | tf_op jit(solution)/shard_map/all_to_all | solution.py:26
  113.3 15.5 %all_to_all.57 = bf16[32,48,128]{2,1,0:T(8,128)(2,1)S(1)} all-to-all(bf16[32,48,128]{2,1,0:T(8,128)(2,1)S(1)} %bitcast.93), channel_id=1, replica_groups=mesh['section'=2,'dp'=32,'mp'=8] {'dp'}, dimensions={0} | all-to-all | bytes 786432 | tf_op jit(solution)/shard_map/all_to_all | solution.py:26
  129.0 15.3 %all_to_all.58 = bf16[32,48,128]{2,1,0:T(8,128)(2,1)S(1)} all-to-all(bf16[32,48,128]{2,1,0:T(8,128)(2,1)S(1)} %broadcast_in_dim.143), channel_id=1, replica_groups=mesh['section'=2,'dp'=32,'mp'=8] {'dp'}, dimensions={0} | all-to-all | bytes 786432 | tf_op jit(solution)/shard_map/all_to_all | solution.py:26
  146.4 12.7 %all_to_all.59 = bf16[8,24,1152]{2,1,0:T(8,128)(2,1)S(1)} all-to-all(bf16[8,24,1152]{2,1,0:T(8,128)(2,1)S(1)} %bitcast.91), channel_id=1, replica_groups={{0,1,4,5,2,3,6,7},{8,9,12,13,10,11,14,15},{16,17,20,21,18,19,22,23},{24..., dimensions={0} | all-to-all | bytes 884736 | tf_op jit(solution)/shard_map/all_to_all | solution.py:26
  159.4 10.6 %all_to_all.60 = bf16[8,24,512]{2,1,0:T(8,128)(2,1)S(1)} all-to-all(bf16[8,24,512]{2,1,0:T(8,128)(2,1)S(1)} %broadcast_in_dim.146), channel_id=1, replica_groups={{0,1,4,5,2,3,6,7},{8,9,12,13,10,11,14,15},{16,17,20,21,18,19,22,23},{24..., dimensions={0} | all-to-all | bytes 393216 | tf_op jit(solution)/shard_map/all_to_all | solution.py:26
  170.6 16.3 %all_to_all.61 = bf16[32,8,1024]{2,1,0:T(8,128)(2,1)S(1)} all-to-all(bf16[32,8,1024]{2,1,0:T(8,128)(2,1)S(1)} %fusion), channel_id=1, replica_groups=mesh['section'=2,'dp'=32,'mp'=8] {'dp'}, dimensions={0} | all-to-all | bytes 1048576 | tf_op jit(solution)/shard_map/all_to_all | solution.py:26
  187.1 16.3 %collective-permute-start.4 = (bf16[8,1024]{1,0:T(8,128)(2,1)S(1)}, bf16[8,1024]{1,0:T(8,128)(2,1)S(1)}, u32[]{:S(2)}, u32[]{:S(2)}) collective-permute-start(bf16[8,1024]{1,0:T(8,128)(2,1)S(1)} %get-tuple-element.89), channel_id=1, source_target_pairs={{0,256},{256,0},{1,257},{257,1},{2,258},{258,2},{3,259},{259,3},{4... | collective-permute-start | bytes 49160 | tf_op jit(solution)/shard_map/ppermute | solution.py:35
  (117 shorter events, 16.0 us)
Async XLA Ops:
  0.0 51.8 %copy-start = (bf16[256,1024]{1,0:T(8,128)(2,1)S(1)}, bf16[256,1024]{1,0:T(8,128)(2,1)}, u32[]{:S(2)}) copy-start(bf16[256,1024]{1,0:T(8,128)(2,1)} %param.17) | copy-start | bytes 1572868
  0.0 16.1 %copy-start.2 = (bf16[1,1024,512]{2,1,0:T(8,128)(2,1)S(1)}, bf16[1,1024,512]{2,1,0:T(8,128)(2,1)}, u32[]{:S(2)}) copy-start(bf16[1,1024,512]{2,1,0:T(8,128)(2,1)} %param.19) | copy-start | bytes 3145732
  3.2 9.8 %copy-start.10 = (bf16[1,1024]{1,0:T(2,128)(2,1)S(1)}, bf16[1,1024]{1,0:T(2,128)(2,1)}, u32[]{:S(2)}) copy-start(bf16[1,1024]{1,0:T(2,128)(2,1)} %param.18) | copy-start | bytes 6148
  3.2 19.2 %copy-start.11 = (bf16[1024]{0:T(1024)(128)(2,1)S(1)}, bf16[1024]{0:T(1024)(128)(2,1)}, u32[]{:S(2)}) copy-start(bf16[1024]{0:T(1024)(128)(2,1)} %param.15) | copy-start | bytes 6148
  3.2 19.3 %copy-start.1 = (bf16[1024,256]{1,0:T(8,128)(2,1)S(1)}, bf16[1024,256]{1,0:T(8,128)(2,1)}, u32[]{:S(2)}) copy-start(bf16[1024,256]{1,0:T(8,128)(2,1)} %param.16) | copy-start | bytes 1572868
  3.2 25.8 %all-to-all-start = ((bf16[32,8,1024]{2,1,0:T(8,128)(2,1)}), bf16[32,8,1024]{2,1,0:T(8,128)(2,1)S(1)}, u32[]{:S(2)}, u32[]{:S(2)}) async-start(bf16[32,8,1024]{2,1,0:T(8,128)(2,1)} %broadcast_in_dim.77), calls=%async_computation | async-start | bytes 1048576 | tf_op jit(solution)/shard_map/all_to_all | solution.py:26
  12.9 9.5 %copy-start.12 = (s32[1,32]{1,0:T(1,128)S(1)}, s32[1,32]{1,0:T(1,128)}, u32[]{:S(2)}) copy-start(s32[1,32]{1,0:T(1,128)} %param.14) | copy-start | bytes 388
  13.0 16.1 %collective-permute-start = (bf16[1,1024]{1,0:T(2,128)(2,1)S(1)}, bf16[1,1024]{1,0:T(2,128)(2,1)S(1)}, u32[]{:S(2)}, u32[]{:S(2)}) collective-permute-start(bf16[1,1024]{1,0:T(2,128)(2,1)S(1)} %copy-done.10), channel_id=1, source_target_pairs={{0,256},{256,0},{1,257},{257,1},{2,258},{258,2},{3,259},{259,3},{4... | collective-permute-start | bytes 6152 | tf_op jit(solution)/shard_map/ppermute | solution.py:35
  16.1 13.0 %collective-permute-start.1 = (bf16[1024,512]{1,0:T(8,128)(2,1)S(1)}, bf16[1024,512]{1,0:T(8,128)(2,1)}, u32[]{:S(2)}, u32[]{:S(2)}) collective-permute-start(bf16[1024,512]{1,0:T(8,128)(2,1)S(1)} %bitcast.94), channel_id=1, source_target_pairs={{0,256},{256,0},{1,257},{257,1},{2,258},{258,2},{3,259},{259,3},{4... | collective-permute-start | bytes 3145736 | tf_op jit(solution)/shard_map/ppermute | solution.py:35
  18.0 11.1 %collective-permute-start.2 = (bf16[1024,512]{1,0:T(8,128)(2,1)}, bf16[1024,512]{1,0:T(8,128)(2,1)}, u32[]{:S(2)}, u32[]{:S(2)}) collective-permute-start(bf16[1024,512]{1,0:T(8,128)(2,1)} %bitcast.96), channel_id=1, source_target_pairs={{0,256},{256,0},{1,257},{257,1},{2,258},{258,2},{3,259},{259,3},{4... | collective-permute-start | bytes 3145736 | tf_op jit(solution)/shard_map/ppermute | solution.py:35
  20.5 8.7 %collective-permute-start.3 = (bf16[512,1024]{1,0:T(8,128)(2,1)}, bf16[512,1024]{1,0:T(8,128)(2,1)}, u32[]{:S(2)}, u32[]{:S(2)}) collective-permute-start(bf16[512,1024]{1,0:T(8,128)(2,1)} %bitcast.98), channel_id=1, source_target_pairs={{0,256},{256,0},{1,257},{257,1},{2,258},{258,2},{3,259},{259,3},{4... | collective-permute-start | bytes 3145736 | tf_op jit(solution)/shard_map/ppermute | solution.py:35
  30.3 11.5 %copy-start.3 = (bf16[1,1024,512]{2,1,0:T(8,128)(2,1)S(1)}, bf16[1,1024,512]{2,1,0:T(8,128)(2,1)}, u32[]{:S(2)}) copy-start(bf16[1,1024,512]{2,1,0:T(8,128)(2,1)} %param.19) | copy-start | bytes 3145732
  31.3 20.1 %all-to-all-start.1 = ((bf16[8,112,256]{2,1,0:T(8,128)(2,1)}), bf16[8,112,256]{2,1,0:T(8,128)(2,1)S(1)}, u32[]{:S(2)}, u32[]{:S(2)}) async-start(bf16[8,112,256]{2,1,0:T(8,128)(2,1)} %broadcast_in_dim.135), calls=%async_computation.1 | async-start | bytes 917504 | tf_op jit(solution)/shard_map/all_to_all | solution.py:26
  41.8 2.8 %copy-start.4 = (bf16[1,1024,512]{2,1,0:T(8,128)(2,1)S(1)}, bf16[1,1024,512]{2,1,0:T(8,128)(2,1)}, u32[]{:S(2)}) copy-start(bf16[1,1024,512]{2,1,0:T(8,128)(2,1)} %param.20) | copy-start | bytes 3145732
  53.0 17.0 %all-to-all-start.2 = ((bf16[32,24,128]{2,1,0:T(8,128)(2,1)}), bf16[32,24,128]{2,1,0:T(8,128)(2,1)S(1)}, u32[]{:S(2)}, u32[]{:S(2)}) async-start(bf16[32,24,128]{2,1,0:T(8,128)(2,1)} %bitcast.12), calls=%async_computation.2 | async-start | bytes 393216 | tf_op jit(solution)/shard_map/all_to_all | solution.py:26
  70.8 13.6 %all-to-all-start.3 = ((bf16[32,24,128]{2,1,0:T(8,128)(2,1)}), bf16[32,24,128]{2,1,0:T(8,128)(2,1)S(1)}, u32[]{:S(2)}, u32[]{:S(2)}) async-start(bf16[32,24,128]{2,1,0:T(8,128)(2,1)} %broadcast_in_dim.136), calls=%async_computation.3 | async-start | bytes 393216 | tf_op jit(solution)/shard_map/all_to_all | solution.py:26
  84.4 1.3 copy-start.8
  85.4 1.3 copy-start.7
  128.9 15.8 %copy-start.6 = (bf16[1024,512]{1,0:T(8,128)(2,1)S(1)}, bf16[1024,512]{1,0:T(8,128)(2,1)}, u32[]{:S(2)}) copy-start(bf16[1024,512]{1,0:T(8,128)(2,1)} %get-tuple-element.75) | copy-start | bytes 3145732
  144.6 1.2 copy-start.5
  159.4 10.6 %copy-start.9 = (bf16[256,192]{0,1:T(8,128)(2,1)S(1)}, bf16[256,192]{0,1:T(8,128)(2,1)}, u32[]{:S(2)}) copy-start(bf16[256,192]{0,1:T(8,128)(2,1)} %pad_maximum_fusion.3) | copy-start | bytes 294916
  187.1 17.1 %collective-permute-start.4 = (bf16[8,1024]{1,0:T(8,128)(2,1)S(1)}, bf16[8,1024]{1,0:T(8,128)(2,1)S(1)}, u32[]{:S(2)}, u32[]{:S(2)}) collective-permute-start(bf16[8,1024]{1,0:T(8,128)(2,1)S(1)} %get-tuple-element.89), channel_id=1, source_target_pairs={{0,256},{256,0},{1,257},{257,1},{2,258},{258,2},{3,259},{259,3},{4... | collective-permute-start | bytes 49160 | tf_op jit(solution)/shard_map/ppermute | solution.py:35

commit v7 on v6

--- a/solution.py
+++ b/solution.py
@@ -89,10 +89,13 @@
     column = dot(gain[None, :], w_in)
     centered = dot(scaled, w_in) - (sums / width)[:, None] * column
     rows, hidden = centered.shape
-    small = jnp.stack(terms(sums, 3) + terms(squares, 3))
-    small = jnp.pad(small, ((0, 0), (0, hidden - rows)))
+    half = hidden // 2
+    spare = ((0, 0), (0, half - rows))
+    small = jnp.concatenate(
+        [jnp.pad(jnp.stack(terms(values, 3)), spare) for values in (sums, squares)], axis=1
+    )
     extra = jnp.concatenate([small, jnp.concatenate(terms(column, 3))], axis=0)
-    extra = jnp.pad(extra, ((0, 16 - extra.shape[0]), (0, 0)))
+    extra = jnp.pad(extra, ((0, 8 - extra.shape[0]), (0, 0)))
     return jnp.concatenate([centered.astype(BF), extra], axis=0)
 
 
@@ -100,8 +103,9 @@
     values = parts.astype(F32)
     extra = values[:, rows:]
     sums = jnp.sum(extra[:, 0:3, :rows], axis=1)
-    squares = jnp.sum(extra[:, 3:6, :rows], axis=(0, 1))
-    columns = jnp.sum(extra[:, 6:9], axis=1)
+    half = extra.shape[2] // 2
+    squares = jnp.sum(extra[:, 0:3, half : half + rows], axis=(0, 1))
+    columns = jnp.sum(extra[:, 3:6], axis=1)
     center = jnp.sum(sums, axis=0) / VIS
     variance = squares / VIS - center * center
     offsets = sums / width - center[None, :]

time: 206 us -> 205 us (level)
  no operation moved by 1% of the time
where the time goes in v7:
time: 205 us; the launch traced here: 204 us
  blocking collectives  96.2 us (47%)
  starting transfers between devices  57.2 us (28%)
  waiting for transfers between devices  25.5 us (12%)
  other arithmetic  12.7 us (6%)
  matrix products  6.3 us (3%)
  local copies, waits for them, and re-layouts  4.41 us (2%)
  between operations  2.05 us (1%)
    all_to_all x7, blocking collectives, exchange(): lax.all_to_all(blocks, axis, 0, 0, tiled=True, axis_index_groups=order)  96.2 us
    all_to_all x4, starting transfers between devices, exchange(): lax.all_to_all(blocks, axis, 0, 0, tiled=True, axis_index_groups=order)  31.4 us
    ppermute x5, starting transfers between devices, swap(): return lax.ppermute(block, 'section', [(0, 1), (1, 0)])  25.7 us
    all_to_all x4, waiting for transfers between devices, exchange(): lax.all_to_all(blocks, axis, 0, 0, tiled=True, axis_index_groups=order)  24.7 us
    select_n x3, other arithmetic, per_device(): layer1 = [jnp.where(first, b, a) for a, b in zip(own[1:], other[1:])]  7.15 us
    dot_general x14, matrix products, dot(): return jnp.dot(a, b, preferred_element_type=F32)  5.14 us
  transfers between devices with their start and end apart: 9, of which 5 were waited for; matrix products, arithmetic and copies ran while one was open for 5% of the time, Pallas kernels for 0%

profile of v7, /device:TPU:9, one launch (start us, length us, event | category | flops | bytes accessed | tf_op | source)
XLA Modules:
  0.0 204.3 jit_solution(5554427509196901897)
XLA Ops:
  3.2 9.7 %all-to-all-start = ((bf16[32,8,1024]{2,1,0:T(8,128)(2,1)}), bf16[32,8,1024]{2,1,0:T(8,128)(2,1)S(1)}, u32[]{:S(2)}, u32[]{:S(2)}) async-start(bf16[32,8,1024]{2,1,0:T(8,128)(2,1)} %broadcast_in_dim.77), calls=%async_computation | async-start | bytes 1048576 | tf_op jit(solution)/shard_map/all_to_all | solution.py:26
  13.0 3.1 %collective-permute-start = (bf16[1,1024]{1,0:T(2,128)(2,1)S(1)}, bf16[1,1024]{1,0:T(2,128)(2,1)S(1)}, u32[]{:S(2)}, u32[]{:S(2)}) collective-permute-start(bf16[1,1024]{1,0:T(2,128)(2,1)S(1)} %copy-done.10), channel_id=1, source_target_pairs={{0,256},{256,0},{1,257},{257,1},{2,258},{258,2},{3,259},{259,3},{4... | collective-permute-start | bytes 6152 | tf_op jit(solution)/shard_map/ppermute | solution.py:35
  16.1 1.9 collective-permute-start.1
  18.0 2.4 %collective-permute-start.2 = (bf16[1024,512]{1,0:T(8,128)(2,1)}, bf16[1024,512]{1,0:T(8,128)(2,1)}, u32[]{:S(2)}, u32[]{:S(2)}) collective-permute-start(bf16[1024,512]{1,0:T(8,128)(2,1)} %bitcast.96), channel_id=1, source_target_pairs={{0,256},{256,0},{1,257},{257,1},{2,258},{258,2},{3,259},{259,3},{4... | collective-permute-start | bytes 3145736 | tf_op jit(solution)/shard_map/ppermute | solution.py:35
  20.5 1.9 collective-permute-start.3
  23.1 5.9 %all-to-all-done = bf16[32,8,1024]{2,1,0:T(8,128)(2,1)S(1)} async-done(((bf16[32,8,1024]{2,1,0:T(8,128)(2,1)}), bf16[32,8,1024]{2,1,0:T(8,128)(2,1)S(1)}, u32[]{:S(2)}, u32[]{:S(2)}) %all-to-all-start) | async-done | bytes 524320 | tf_op jit(solution)/shard_map/all_to_all | solution.py:26
  31.3 10.0 %all-to-all-start.1 = ((bf16[8,104,256]{2,1,0:T(8,128)(2,1)}), bf16[8,104,256]{2,1,0:T(8,128)(2,1)S(1)}, u32[]{:S(2)}, u32[]{:S(2)}) async-start(bf16[8,104,256]{2,1,0:T(8,128)(2,1)} %broadcast_in_dim.135), calls=%async_computation.1 | async-start | bytes 851968 | tf_op jit(solution)/shard_map/all_to_all | solution.py:26
  41.9 2.8 %broadcast_select_fusion.3 = (bf16[1024,512]{1,0:T(8,128)(2,1)}, bf16[1024,512]{1,0:T(8,128)(2,1)}) fusion(bf16[1024,512]{1,0:T(8,128)(2,1)} %collective-permute-done.1, bf16[1024,512]{1,0:T(8,128)(2,1)S(1)} %bitcast.95, pred[]{:T(512)S(6)} %eq.49), kind=kLoop, calls=%fused_computation.25 | loop fusion | flops 1048576 | bytes 4194305 | tf_op jit(solution)/shard_map/jit(_where)/select_n | solution.py:186
  44.7 2.7 %broadcast_select_fusion.2 = (bf16[1024,512]{1,0:T(8,128)(2,1)}, bf16[1024,512]{1,0:T(8,128)(2,1)}) fusion(bf16[1024,512]{1,0:T(8,128)(2,1)} %collective-permute-done.2, bf16[1024,512]{1,0:T(8,128)(2,1)S(1)} %bitcast.97, pred[]{:T(512)S(6)} %eq.49), kind=kLoop, calls=%fused_computation.24 | loop fusion | flops 1048576 | bytes 4194305 | tf_op jit(solution)/shard_map/jit(_where)/select_n | solution.py:186
  47.3 2.9 %all-to-all-done.1 = bf16[8,104,256]{2,1,0:T(8,128)(2,1)S(1)} async-done(((bf16[8,104,256]{2,1,0:T(8,128)(2,1)}), bf16[8,104,256]{2,1,0:T(8,128)(2,1)S(1)}, u32[]{:S(2)}, u32[]{:S(2)}) %all-to-all-start.1) | async-done | bytes 426016 | tf_op jit(solution)/shard_map/all_to_all | solution.py:26
  50.6 1.2 convolution_convert_fusion.8
  51.8 7.7 %all-to-all-start.2 = ((bf16[32,24,128]{2,1,0:T(8,128)(2,1)}), bf16[32,24,128]{2,1,0:T(8,128)(2,1)S(1)}, u32[]{:S(2)}, u32[]{:S(2)}) async-start(bf16[32,24,128]{2,1,0:T(8,128)(2,1)} %bitcast.12), calls=%async_computation.2 | async-start | bytes 393216 | tf_op jit(solution)/shard_map/all_to_all | solution.py:26
  59.7 1.7 broadcast_select_fusion
  61.4 7.9 %all-to-all-done.2 = bf16[32,24,128]{2,1,0:T(8,128)(2,1)S(1)} async-done(((bf16[32,24,128]{2,1,0:T(8,128)(2,1)}), bf16[32,24,128]{2,1,0:T(8,128)(2,1)S(1)}, u32[]{:S(2)}, u32[]{:S(2)}) %all-to-all-start.2) | async-done | bytes 196640 | tf_op jit(solution)/shard_map/all_to_all | solution.py:26
  70.0 3.9 %all-to-all-start.3 = ((bf16[32,24,128]{2,1,0:T(8,128)(2,1)}), bf16[32,24,128]{2,1,0:T(8,128)(2,1)S(1)}, u32[]{:S(2)}, u32[]{:S(2)}) async-start(bf16[32,24,128]{2,1,0:T(8,128)(2,1)} %broadcast_in_dim.136), calls=%async_computation.3 | async-start | bytes 393216 | tf_op jit(solution)/shard_map/all_to_all | solution.py:26
  75.5 8.0 %all-to-all-done.3 = bf16[32,24,128]{2,1,0:T(8,128)(2,1)S(1)} async-done(((bf16[32,24,128]{2,1,0:T(8,128)(2,1)}), bf16[32,24,128]{2,1,0:T(8,128)(2,1)S(1)}, u32[]{:S(2)}, u32[]{:S(2)}) %all-to-all-start.3) | async-done | bytes 196640 | tf_op jit(solution)/shard_map/all_to_all | solution.py:26
  86.5 15.4 %all_to_all.55 = bf16[8,24,1152]{2,1,0:T(8,128)(2,1)S(1)} all-to-all(bf16[8,24,1152]{2,1,0:T(8,128)(2,1)S(1)} %bitcast.90), channel_id=1, replica_groups={{0,1,4,5,2,3,6,7},{8,9,12,13,10,11,14,15},{16,17,20,21,18,19,22,23},{24..., dimensions={0} | all-to-all | bytes 884736 | tf_op jit(solution)/shard_map/all_to_all | solution.py:26
  102.2 10.1 %all_to_all.56 = bf16[8,24,512]{2,1,0:T(8,128)(2,1)S(1)} all-to-all(bf16[8,24,512]{2,1,0:T(8,128)(2,1)S(1)} %broadcast_in_dim.142), channel_id=1, replica_groups={{0,1,4,5,2,3,6,7},{8,9,12,13,10,11,14,15},{16,17,20,21,18,19,22,23},{24..., dimensions={0} | all-to-all | bytes 393216 | tf_op jit(solution)/shard_map/all_to_all | solution.py:26
  112.7 15.5 %all_to_all.57 = bf16[32,48,128]{2,1,0:T(8,128)(2,1)S(1)} all-to-all(bf16[32,48,128]{2,1,0:T(8,128)(2,1)S(1)} %bitcast.93), channel_id=1, replica_groups=mesh['section'=2,'dp'=32,'mp'=8] {'dp'}, dimensions={0} | all-to-all | bytes 786432 | tf_op jit(solution)/shard_map/all_to_all | solution.py:26
  128.3 15.4 %all_to_all.58 = bf16[32,48,128]{2,1,0:T(8,128)(2,1)S(1)} all-to-all(bf16[32,48,128]{2,1,0:T(8,128)(2,1)S(1)} %broadcast_in_dim.143), channel_id=1, replica_groups=mesh['section'=2,'dp'=32,'mp'=8] {'dp'}, dimensions={0} | all-to-all | bytes 786432 | tf_op jit(solution)/shard_map/all_to_all | solution.py:26
  145.7 12.6 %all_to_all.59 = bf16[8,24,1152]{2,1,0:T(8,128)(2,1)S(1)} all-to-all(bf16[8,24,1152]{2,1,0:T(8,128)(2,1)S(1)} %bitcast.91), channel_id=1, replica_groups={{0,1,4,5,2,3,6,7},{8,9,12,13,10,11,14,15},{16,17,20,21,18,19,22,23},{24..., dimensions={0} | all-to-all | bytes 884736 | tf_op jit(solution)/shard_map/all_to_all | solution.py:26
  158.6 10.8 %all_to_all.60 = bf16[8,24,512]{2,1,0:T(8,128)(2,1)S(1)} all-to-all(bf16[8,24,512]{2,1,0:T(8,128)(2,1)S(1)} %broadcast_in_dim.146), channel_id=1, replica_groups={{0,1,4,5,2,3,6,7},{8,9,12,13,10,11,14,15},{16,17,20,21,18,19,22,23},{24..., dimensions={0} | all-to-all | bytes 393216 | tf_op jit(solution)/shard_map/all_to_all | solution.py:26
  170.1 16.3 %all_to_all.61 = bf16[32,8,1024]{2,1,0:T(8,128)(2,1)S(1)} all-to-all(bf16[32,8,1024]{2,1,0:T(8,128)(2,1)S(1)} %fusion), channel_id=1, replica_groups=mesh['section'=2,'dp'=32,'mp'=8] {'dp'}, dimensions={0} | all-to-all | bytes 1048576 | tf_op jit(solution)/shard_map/all_to_all | solution.py:26
  186.5 16.4 %collective-permute-start.4 = (bf16[8,1024]{1,0:T(8,128)(2,1)S(1)}, bf16[8,1024]{1,0:T(8,128)(2,1)S(1)}, u32[]{:S(2)}, u32[]{:S(2)}) collective-permute-start(bf16[8,1024]{1,0:T(8,128)(2,1)S(1)} %get-tuple-element.89), channel_id=1, source_target_pairs={{0,256},{256,0},{1,257},{257,1},{2,258},{258,2},{3,259},{259,3},{4... | collective-permute-start | bytes 49160 | tf_op jit(solution)/shard_map/ppermute | solution.py:35
  (118 shorter events, 15.9 us)
Async XLA Ops:
  0.0 50.6 %copy-start = (bf16[256,1024]{1,0:T(8,128)(2,1)S(1)}, bf16[256,1024]{1,0:T(8,128)(2,1)}, u32[]{:S(2)}) copy-start(bf16[256,1024]{1,0:T(8,128)(2,1)} %param.17) | copy-start | bytes 1572868
  0.0 16.1 %copy-start.2 = (bf16[1,1024,512]{2,1,0:T(8,128)(2,1)S(1)}, bf16[1,1024,512]{2,1,0:T(8,128)(2,1)}, u32[]{:S(2)}) copy-start(bf16[1,1024,512]{2,1,0:T(8,128)(2,1)} %param.19) | copy-start | bytes 3145732
  3.2 9.8 %copy-start.10 = (bf16[1,1024]{1,0:T(2,128)(2,1)S(1)}, bf16[1,1024]{1,0:T(2,128)(2,1)}, u32[]{:S(2)}) copy-start(bf16[1,1024]{1,0:T(2,128)(2,1)} %param.18) | copy-start | bytes 6148
  3.2 19.2 %copy-start.11 = (bf16[1024]{0:T(1024)(128)(2,1)S(1)}, bf16[1024]{0:T(1024)(128)(2,1)}, u32[]{:S(2)}) copy-start(bf16[1024]{0:T(1024)(128)(2,1)} %param.15) | copy-start | bytes 6148
  3.2 19.3 %copy-start.1 = (bf16[1024,256]{1,0:T(8,128)(2,1)S(1)}, bf16[1024,256]{1,0:T(8,128)(2,1)}, u32[]{:S(2)}) copy-start(bf16[1024,256]{1,0:T(8,128)(2,1)} %param.16) | copy-start | bytes 1572868
  3.2 25.8 %all-to-all-start = ((bf16[32,8,1024]{2,1,0:T(8,128)(2,1)}), bf16[32,8,1024]{2,1,0:T(8,128)(2,1)S(1)}, u32[]{:S(2)}, u32[]{:S(2)}) async-start(bf16[32,8,1024]{2,1,0:T(8,128)(2,1)} %broadcast_in_dim.77), calls=%async_computation | async-start | bytes 1048576 | tf_op jit(solution)/shard_map/all_to_all | solution.py:26
  12.9 9.5 %copy-start.12 = (s32[1,32]{1,0:T(1,128)S(1)}, s32[1,32]{1,0:T(1,128)}, u32[]{:S(2)}) copy-start(s32[1,32]{1,0:T(1,128)} %param.14) | copy-start | bytes 388
  13.0 16.1 %collective-permute-start = (bf16[1,1024]{1,0:T(2,128)(2,1)S(1)}, bf16[1,1024]{1,0:T(2,128)(2,1)S(1)}, u32[]{:S(2)}, u32[]{:S(2)}) collective-permute-start(bf16[1,1024]{1,0:T(2,128)(2,1)S(1)} %copy-done.10), channel_id=1, source_target_pairs={{0,256},{256,0},{1,257},{257,1},{2,258},{258,2},{3,259},{259,3},{4... | collective-permute-start | bytes 6152 | tf_op jit(solution)/shard_map/ppermute | solution.py:35
  16.1 13.0 %collective-permute-start.1 = (bf16[1024,512]{1,0:T(8,128)(2,1)S(1)}, bf16[1024,512]{1,0:T(8,128)(2,1)}, u32[]{:S(2)}, u32[]{:S(2)}) collective-permute-start(bf16[1024,512]{1,0:T(8,128)(2,1)S(1)} %bitcast.94), channel_id=1, source_target_pairs={{0,256},{256,0},{1,257},{257,1},{2,258},{258,2},{3,259},{259,3},{4... | collective-permute-start | bytes 3145736 | tf_op jit(solution)/shard_map/ppermute | solution.py:35
  18.0 11.1 %collective-permute-start.2 = (bf16[1024,512]{1,0:T(8,128)(2,1)}, bf16[1024,512]{1,0:T(8,128)(2,1)}, u32[]{:S(2)}, u32[]{:S(2)}) collective-permute-start(bf16[1024,512]{1,0:T(8,128)(2,1)} %bitcast.96), channel_id=1, source_target_pairs={{0,256},{256,0},{1,257},{257,1},{2,258},{258,2},{3,259},{259,3},{4... | collective-permute-start | bytes 3145736 | tf_op jit(solution)/shard_map/ppermute | solution.py:35
  20.5 8.7 %collective-permute-start.3 = (bf16[512,1024]{1,0:T(8,128)(2,1)}, bf16[512,1024]{1,0:T(8,128)(2,1)}, u32[]{:S(2)}, u32[]{:S(2)}) collective-permute-start(bf16[512,1024]{1,0:T(8,128)(2,1)} %bitcast.98), channel_id=1, source_target_pairs={{0,256},{256,0},{1,257},{257,1},{2,258},{258,2},{3,259},{259,3},{4... | collective-permute-start | bytes 3145736 | tf_op jit(solution)/shard_map/ppermute | solution.py:35
  30.3 11.5 %copy-start.3 = (bf16[1,1024,512]{2,1,0:T(8,128)(2,1)S(1)}, bf16[1,1024,512]{2,1,0:T(8,128)(2,1)}, u32[]{:S(2)}) copy-start(bf16[1,1024,512]{2,1,0:T(8,128)(2,1)} %param.19) | copy-start | bytes 3145732
  31.3 18.9 %all-to-all-start.1 = ((bf16[8,104,256]{2,1,0:T(8,128)(2,1)}), bf16[8,104,256]{2,1,0:T(8,128)(2,1)S(1)}, u32[]{:S(2)}, u32[]{:S(2)}) async-start(bf16[8,104,256]{2,1,0:T(8,128)(2,1)} %broadcast_in_dim.135), calls=%async_computation.1 | async-start | bytes 851968 | tf_op jit(solution)/shard_map/all_to_all | solution.py:26
  41.8 2.8 %copy-start.4 = (bf16[1,1024,512]{2,1,0:T(8,128)(2,1)S(1)}, bf16[1,1024,512]{2,1,0:T(8,128)(2,1)}, u32[]{:S(2)}) copy-start(bf16[1,1024,512]{2,1,0:T(8,128)(2,1)} %param.20) | copy-start | bytes 3145732
  51.8 17.5 %all-to-all-start.2 = ((bf16[32,24,128]{2,1,0:T(8,128)(2,1)}), bf16[32,24,128]{2,1,0:T(8,128)(2,1)S(1)}, u32[]{:S(2)}, u32[]{:S(2)}) async-start(bf16[32,24,128]{2,1,0:T(8,128)(2,1)} %bitcast.12), calls=%async_computation.2 | async-start | bytes 393216 | tf_op jit(solution)/shard_map/all_to_all | solution.py:26
  70.0 13.5 %all-to-all-start.3 = ((bf16[32,24,128]{2,1,0:T(8,128)(2,1)}), bf16[32,24,128]{2,1,0:T(8,128)(2,1)S(1)}, u32[]{:S(2)}, u32[]{:S(2)}) async-start(bf16[32,24,128]{2,1,0:T(8,128)(2,1)} %broadcast_in_dim.136), calls=%async_computation.3 | async-start | bytes 393216 | tf_op jit(solution)/shard_map/all_to_all | solution.py:26
  83.5 1.3 copy-start.8
  84.6 1.3 copy-start.7
  128.3 15.8 %copy-start.6 = (bf16[1024,512]{1,0:T(8,128)(2,1)S(1)}, bf16[1024,512]{1,0:T(8,128)(2,1)}, u32[]{:S(2)}) copy-start(bf16[1024,512]{1,0:T(8,128)(2,1)} %get-tuple-element.75) | copy-start | bytes 3145732
  143.9 1.2 copy-start.5
  158.6 10.8 %copy-start.9 = (bf16[256,192]{0,1:T(8,128)(2,1)S(1)}, bf16[256,192]{0,1:T(8,128)(2,1)}, u32[]{:S(2)}) copy-start(bf16[256,192]{0,1:T(8,128)(2,1)} %pad_maximum_fusion.3) | copy-start | bytes 294916
  186.5 17.2 %collective-permute-start.4 = (bf16[8,1024]{1,0:T(8,128)(2,1)S(1)}, bf16[8,1024]{1,0:T(8,128)(2,1)S(1)}, u32[]{:S(2)}, u32[]{:S(2)}) collective-permute-start(bf16[8,1024]{1,0:T(8,128)(2,1)S(1)} %get-tuple-element.89), channel_id=1, source_target_pairs={{0,256},{256,0},{1,257},{257,1},{2,258},{258,2},{3,259},{259,3},{4... | collective-permute-start | bytes 49160 | tf_op jit(solution)/shard_map/ppermute | solution.py:35
